TPU v7x, 256 devices: a whole 4x4x8 slice. The times are simulated.
256 devices in a mesh: elem: 16 (over z, core), four: 16 (over y, x).
Axes of the slice: x: 4, y: 4, z: 8, core: 2. Of those that a mesh axis runs over, the one named last changes fastest.
Arguments:
- vel_hat: float32 [3, 512, 32768], P(None, 'four', 'elem')
- metric: float32 [4, 512], P(None, 'elem'), may hold values from -0.4 to 0.4
- area: float32 [512], P('elem'), may hold values from 0.5 to 2
- visc: float32 [32768], P('elem'), may hold values from 0.05 to 0.5
- rotor_element: int32 [512], P('elem'), may hold values from 0 to 31
- stator_element: int32 [512], P('elem'), may hold values from 0 to 31
- mortar_offset: int32 [512], P('elem'), may hold values from 0 to 7
- stator_source: int32 [512], P('elem'), may hold values from 0 to 511, as said below
Outputs:
- tendency: float32 [3, 512, 32768], P(None, 'four', 'elem')
Inputs may be any that keep to these rules, and one draw needn't show every extreme that they name: stator_source[g] is d * 32 + s for a slot s of elem index d.
All inputs are finite; a program needn't handle non-finite values.
Results may differ from a plain program's by a relative error of at most 0.0001.
Values sent between devices are 32-bit elements; how exact they have to be, the bound alone decides.
No kernel may reach another device: no remote copies, remote signals or barrier semaphores. Data moves between devices by JAX's collectives and lax.ppermute only.
A program may use at most 128 MiB of HBM per device.

v0:
```python
import math

import jax
import jax.numpy as jnp
import numpy as np
from jax import lax
from jax.experimental import pallas as pl
from jax.experimental.pallas import tpu as pltpu
from jax.sharding import PartitionSpec as P

NQ = 8
MODES = 512
PLANES = 768
HALF = PLANES // 2
PAIRS = MODES // 2
GROUPS = 16
ROWS = 96
LANES = 128

LAMBDA_COEF = 10.0
TAU_COEF = 2.0
KZ_DIV = 32.0

F32 = jnp.float32
BF16 = jnp.bfloat16
VMEM = pltpu.MemorySpace.VMEM
SMEM = pltpu.MemorySpace.SMEM


def element_tables():
    order = NQ - 1
    points = -np.cos(np.pi * np.arange(NQ) / order)
    barycentric = np.array([(-1.0) ** index_a for index_a in range(NQ)])
    barycentric[0] *= 0.5
    barycentric[-1] *= 0.5
    derivative = np.zeros((NQ, NQ))
    for index_a in range(NQ):
        for index_b in range(NQ):
            if index_a != index_b:
                derivative[index_a, index_b] = (
                    barycentric[index_b]
                    / barycentric[index_a]
                    / (points[index_a] - points[index_b])
                )
        derivative[index_a, index_a] = -np.sum(derivative[index_a])
    angles = np.pi * np.arange(NQ) / order
    weights = np.ones(NQ)
    for harmonic in range(1, order // 2 + 1):
        weights = weights - 2.0 * np.cos(2 * harmonic * angles) / (4 * harmonic * harmonic - 1)
    weights = weights * 2.0 / order
    weights[0] *= 0.5
    weights[-1] *= 0.5
    identity = np.eye(NQ)
    along_xi = np.kron(np.eye(2), np.kron(identity, derivative))
    along_eta = np.kron(np.eye(2), np.kron(derivative, identity))
    node_weight = np.kron(weights, weights)
    interp = np.ones((NQ, NQ, NQ))
    for offset in range(NQ):
        targets = points * (1.0 - offset / 16.0) + offset / 16.0
        for index_a in range(NQ):
            for index_b in range(NQ):
                for index_c in range(NQ):
                    if index_c != index_b:
                        interp[offset, index_a, index_b] *= (targets[index_a] - points[index_c]) / (
                            points[index_b] - points[index_c]
                        )
    return along_xi, along_eta, node_weight, interp


def two_parts(table):
    table = np.asarray(table, np.float32)
    high = table.astype(BF16)
    low = (table - high.astype(np.float32)).astype(BF16)
    return high, low


def as_left(table):
    high, low = two_parts(table)
    return jnp.asarray(np.concatenate([high, low, high], 1))


def as_right(table):
    high, low = two_parts(table)
    return jnp.asarray(np.concatenate([high, low, high], 0))


def span_tables():
    plane = np.arange(HALF)[:, None]
    number = np.arange(PAIRS)[None, :]
    angle = 2.0 * np.pi * ((plane * number) % PLANES) / PLANES
    cosine, sine = np.cos(angle), np.sin(angle)
    scale = np.full((PAIRS, 1), 2.0 / PLANES)
    scale[0] = 1.0 / PLANES
    return cosine, sine, cosine.T * scale, sine.T * (2.0 / PLANES)


def split(value):
    high = value.astype(BF16)
    low = (value - high.astype(F32)).astype(BF16)
    return high, low


def dot(left, right):
    return jnp.dot(left, right, preferred_element_type=F32)


def left_split(value):
    high, low = split(value)
    return jnp.concatenate([high, high, low], -1)


def right_split(value):
    high, low = split(value)
    return jnp.concatenate([high, high, low], 0)


def lane_scalars(first, second):
    lane = lax.broadcasted_iota(jnp.int32, (1, LANES), 1)
    return jnp.where(lane < LANES // 2, first, second)


def pack_kernel(field_ref, out_ref, in_ref, done_ref, in_sems, out_sems):
    def load(block):
        return pltpu.make_async_copy(
            field_ref.at[:, pl.ds(block * LANES, LANES)], in_ref.at[block], in_sems.at[block]
        )

    def store(block):
        return pltpu.make_async_copy(done_ref.at[block], out_ref.at[block], out_sems.at[block])

    for block in range(GROUPS):
        load(block).start()
    for block in range(GROUPS):
        load(block).wait()
        for component in range(3):
            for parity in range(2):
                done_ref[block, pl.ds(component * 32 + parity * 16, 16), :] = in_ref[
                    block, pl.ds(component * 32 + parity, 16, stride=2), :
                ]
        store(block).start()
    for block in range(GROUPS):
        store(block).wait()


def pack(field):
    anywhere = pl.BlockSpec(memory_space=pl.ANY)
    return pl.pallas_call(
        pack_kernel,
        in_specs=[anywhere],
        out_specs=anywhere,
        out_shape=jax.ShapeDtypeStruct((GROUPS, ROWS, LANES), F32),
        scratch_shapes=[
            pltpu.VMEM((GROUPS, ROWS, LANES), F32),
            pltpu.VMEM((GROUPS, ROWS, LANES), F32),
            pltpu.SemaphoreType.DMA((GROUPS,)),
            pltpu.SemaphoreType.DMA((GROUPS,)),
        ],
        cost_estimate=pl.CostEstimate(flops=0, bytes_accessed=1600000, transcendentals=0),
        name="pack",
    )(field)


def trace_kernel(rotor_ref, packed_ref, out_ref, top_ref):
    zeros = jnp.zeros((LANES - ROWS, LANES), F32)
    for block in range(GROUPS):
        turned = jnp.concatenate([packed_ref[block], zeros], 0).T
        top_ref[pl.ds(block * 16, 8), :] = turned[56:64]
        top_ref[pl.ds(block * 16 + 8, 8), :] = turned[120:128]
    for slot in range(32):
        start = pl.multiple_of(rotor_ref[slot] * 8, 8)
        out_ref[pl.ds(slot * 8, 8), :] = top_ref[pl.ds(start, 8), :]


def traces(rotor_element, packed):
    return pl.pallas_call(
        trace_kernel,
        in_specs=[pl.BlockSpec(memory_space=SMEM), pl.BlockSpec(memory_space=VMEM)],
        out_specs=pl.BlockSpec(memory_space=VMEM),
        out_shape=jax.ShapeDtypeStruct((256, LANES), F32),
        scratch_shapes=[pltpu.VMEM((256, LANES), F32)],
        cost_estimate=pl.CostEstimate(flops=0, bytes_accessed=8000000, transcendentals=0),
        name="traces",
    )(rotor_element, packed)


def helm_kernel(
    metric_ref, area_ref, stator_ref, packed_ref, visc_ref, weight_ref, forward_ref, back_ref, out_ref
):
    step = packed_ref.shape[0]
    first = pl.program_id(0) * step
    four = lax.axis_index("four")
    row = lax.broadcasted_iota(jnp.int32, (ROWS, LANES), 0)
    inner = row % 32
    number = jnp.where(
        (inner == 16) & (four == 0), MODES // 2, four * 16 + inner % 16
    )
    wave = number.astype(F32) / KZ_DIV
    wave_sq = wave * wave
    lane = lax.broadcasted_iota(jnp.int32, (1, LANES), 1)
    bottom = lane % 64 < NQ
    field = packed_ref[...].reshape(step * ROWS, LANES)
    grads = dot(left_split(field), forward_ref[...])
    masses, fluxes = [], []
    for block in range(step):
        pair = (first + block) * 2
        rx, ry, sx, sy = [
            lane_scalars(metric_ref[i, pair], metric_ref[i, pair + 1]) for i in range(4)
        ]
        count_a, count_b = jnp.int32(0), jnp.int32(0)
        for edge in range(32):
            here = stator_ref[edge]
            count_a = count_a + jnp.where(here == pair, 1, 0)
            count_b = count_b + jnp.where(here == pair + 1, 1, 0)
        count = lane_scalars(count_a, count_b).astype(F32)
        own = jnp.where(bottom, TAU_COEF * count, 0.0)
        area = lane_scalars(area_ref[pair], area_ref[pair + 1])
        weight = area * weight_ref[...]
        viscous = weight * visc_ref[pl.ds(first + block, 1), :]
        rows = slice(block * ROWS, (block + 1) * ROWS)
        grad_xi, grad_eta = grads[rows, :LANES], grads[rows, LANES:]
        cross = viscous * (rx * sx + ry * sy)
        flux_xi = (viscous * (rx * rx + ry * ry)) * grad_xi + cross * grad_eta
        flux_eta = cross * grad_xi + (viscous * (sx * sx + sy * sy)) * grad_eta
        fluxes.append(jnp.concatenate([flux_xi, flux_eta], 1))
        masses.append((weight * LAMBDA_COEF + own + viscous * wave_sq) * field[rows])
    stiff = dot(left_split(jnp.concatenate(fluxes, 0)), back_ref[...])
    for block in range(step):
        out_ref[block] = masses[block] + stiff[block * ROWS : (block + 1) * ROWS]


def helmholtz(metric, area, stator_element, packed, visc, weight, forward, back):
    step = 4
    return pl.pallas_call(
        helm_kernel,
        grid=(GROUPS // step,),
        in_specs=[
            pl.BlockSpec(memory_space=SMEM),
            pl.BlockSpec(memory_space=SMEM),
            pl.BlockSpec(memory_space=SMEM),
            pl.BlockSpec((step, ROWS, LANES), lambda i: (i, 0, 0)),
            pl.BlockSpec((GROUPS, LANES), lambda i: (0, 0)),
            pl.BlockSpec((1, LANES), lambda i: (0, 0)),
            pl.BlockSpec((3 * LANES, 2 * LANES), lambda i: (0, 0)),
            pl.BlockSpec((6 * LANES, LANES), lambda i: (0, 0)),
        ],
        out_specs=pl.BlockSpec((step, ROWS, LANES), lambda i: (i, 0, 0)),
        out_shape=jax.ShapeDtypeStruct((GROUPS, ROWS, LANES), F32),
        cost_estimate=pl.CostEstimate(flops=2000000000, bytes_accessed=8000000, transcendentals=0),
        name="helm",
    )(metric, area, stator_element, packed, visc, weight, forward, back)


def plane_kernel(
    metric_ref, got_ref, cos_ref, sin_ref, cos_back_ref, sin_back_ref, forward_ref, out_ref
):
    pair = lax.axis_index("four") * 2
    rx, ry, sx, sy = [
        lane_scalars(metric_ref[i, pair], metric_ref[i, pair + 1]) for i in range(4)
    ]
    number = lax.broadcasted_iota(jnp.int32, (PAIRS, LANES), 0)
    wave = number.astype(F32) / KZ_DIV
    sign = jnp.where(number % 2 == 0, 1.0, -1.0).astype(F32)
    plane = lax.broadcasted_iota(jnp.int32, (HALF, LANES), 0)
    third = jnp.where(plane % 3 == 0, 1.0, -0.5).astype(F32)
    is_first = plane == 0
    evens, odds = [], []
    for component in range(3):
        evens.append(got_ref[:, pl.ds(component * 32, 16), :].reshape(PAIRS, LANES))
        odds.append(got_ref[:, pl.ds(component * 32 + 16, 16), :].reshape(PAIRS, LANES))
    evens_z = [wave * odd for odd in odds]
    odds_z = [-wave * even for even in evens]
    last_cos = [odd[0:1] for odd in odds]
    even_all = jnp.concatenate(evens + evens_z, 1)
    odd_all = jnp.concatenate(odds + odds_z, 1)
    cos_part = dot(cos_ref[...], right_split(even_all))
    sin_part = dot(sin_ref[...], right_split(odd_all))
    plus, minus = [], []
    for index in range(6):
        lanes = slice(index * LANES, (index + 1) * LANES)
        cos_here, sin_here = cos_part[:, lanes], sin_part[:, lanes]
        middle = jnp.sum(sign * (evens + evens_z)[index], 0, keepdims=True)
        if index < 3:
            cos_here = cos_here + third * last_cos[index]
            middle = middle + last_cos[index]
        plus.append(cos_here + sin_here)
        minus.append(jnp.where(is_first, middle, cos_here - sin_here))

    def advect(values):
        along_xi = values[0] * rx + values[1] * ry
        along_eta = values[0] * sx + values[1] * sy
        results = []
        for component in range(3):
            grads = dot(left_split(values[component]), forward_ref[...])
            results.append(
                along_xi * grads[:, :LANES]
                + along_eta * grads[:, LANES:]
                + values[2] * values[3 + component]
            )
        return results

    ahead, mirrored = advect(plus), advect(minus)
    middles = [value[0:1] for value in mirrored]
    mirrored = [jnp.where(is_first, 0.0, value) for value in mirrored]
    even_sum = [a + b for a, b in zip(ahead, mirrored)]
    odd_sum = [a - b for a, b in zip(ahead, mirrored)]
    even_out = dot(cos_back_ref[...], right_split(jnp.concatenate(even_sum, 1)))
    odd_out = dot(sin_back_ref[...], right_split(jnp.concatenate(odd_sum, 1)))
    scale = jnp.where(number == 0, 1.0 / PLANES, 2.0 / PLANES).astype(F32)
    for component in range(3):
        lanes = slice(component * LANES, (component + 1) * LANES)
        even_here = even_out[:, lanes] + (scale * sign) * middles[component]
        last = (2.0 / PLANES) * (
            jnp.sum(third * even_sum[component], 0, keepdims=True) + middles[component]
        )
        odd_here = jnp.where(number == 0, last, odd_out[:, lanes])
        out_ref[:, pl.ds(component * 32, 16), :] = even_here.reshape(GROUPS, 16, LANES)
        out_ref[:, pl.ds(component * 32 + 16, 16), :] = odd_here.reshape(GROUPS, 16, LANES)


def planes(metric, got, cosine, sine, cos_back, sin_back, forward):
    whole = pl.BlockSpec(memory_space=VMEM)
    return pl.pallas_call(
        plane_kernel,
        in_specs=[pl.BlockSpec(memory_space=SMEM)] + [whole] * 6,
        out_specs=whole,
        out_shape=jax.ShapeDtypeStruct((GROUPS, ROWS, LANES), F32),
        compiler_params=pltpu.CompilerParams(vmem_limit_bytes=48 * 1024 * 1024),
        cost_estimate=pl.CostEstimate(flops=3000000000, bytes_accessed=4000000, transcendentals=0),
        name="planes",
    )(metric, got, cosine, sine, cos_back, sin_back, forward)


def penalty_kernel(
    source_ref, stator_ref, offset_ref, interp_ref, pieces_ref, helm_ref, out_ref,
    received_ref, base_ref, place_ref,
):
    for edge in range(32):
        rows = pl.ds(edge * 8, 8)
        start = pl.multiple_of(source_ref[edge] * 8, 8)
        received_ref[rows, :] = pieces_ref[pl.ds(start, 8), :]
        base_ref[rows, :] = interp_ref[pl.ds(pl.multiple_of(offset_ref[edge] * 8, 8), 8), :]
        place_ref[rows, :] = jnp.full((8, LANES), stator_ref[edge], jnp.int32)
    lane = lax.broadcasted_iota(jnp.int32, (256, LANES), 1)
    home = place_ref[...] - jnp.where(lane < 64, 0, 1)
    base = base_ref[...]
    left = left_split(received_ref[...].T[:ROWS])
    for block in range(GROUPS):
        matrix = jnp.where(home == 2 * block, base, 0.0)
        high, low = split(matrix)
        right = jnp.concatenate([high, low, high], 0)
        out_ref[block] = helm_ref[block] - dot(left, right)


def penalty(stator_source, stator_element, mortar_offset, interp, pieces, helm):
    whole = pl.BlockSpec(memory_space=VMEM)
    scalars = pl.BlockSpec(memory_space=SMEM)
    return pl.pallas_call(
        penalty_kernel,
        in_specs=[scalars] * 3 + [whole] * 3,
        out_specs=whole,
        out_shape=jax.ShapeDtypeStruct((GROUPS, ROWS, LANES), F32),
        scratch_shapes=[
            pltpu.VMEM((256, LANES), F32),
            pltpu.VMEM((256, LANES), F32),
            pltpu.VMEM((256, LANES), jnp.int32),
        ],
        cost_estimate=pl.CostEstimate(flops=1000000000, bytes_accessed=8000000, transcendentals=0),
        name="penalty",
    )(stator_source, stator_element, mortar_offset, interp, pieces, helm)


def sum_kernel(nonlinear_ref, rest_ref, out_ref, done_ref, out_sems):
    def store(block):
        return pltpu.make_async_copy(
            done_ref.at[block], out_ref.at[:, pl.ds(block * LANES, LANES)], out_sems.at[block]
        )

    for block in range(GROUPS):
        value = -nonlinear_ref[block] - rest_ref[block]
        for component in range(3):
            for parity in range(2):
                start = component * 32 + parity * 16
                done_ref[block, pl.ds(component * 32 + parity, 16, stride=2), :] = value[
                    start : start + 16
                ]
        store(block).start()
    for block in range(GROUPS):
        store(block).wait()


def final_sum(nonlinear, rest):
    whole = pl.BlockSpec(memory_space=VMEM)
    return pl.pallas_call(
        sum_kernel,
        in_specs=[whole, whole],
        out_specs=pl.BlockSpec(memory_space=pl.ANY),
        out_shape=jax.ShapeDtypeStruct((ROWS, GROUPS * LANES), F32),
        scratch_shapes=[
            pltpu.VMEM((GROUPS, ROWS, LANES), F32),
            pltpu.SemaphoreType.DMA((GROUPS,)),
        ],
        cost_estimate=pl.CostEstimate(flops=0, bytes_accessed=2400000, transcendentals=0),
        name="final_sum",
    )(nonlinear, rest)


def local(vel_hat, metric, area, visc, rotor_element, stator_element, mortar_offset, stator_source):
    along_xi, along_eta, node_weight, interp = element_tables()
    cosine, sine, cos_back, sin_back = span_tables()
    forward = as_right(np.concatenate([along_xi.T, along_eta.T], 1))
    back = as_right(np.concatenate([along_xi, along_eta], 0))
    weight = jnp.asarray(np.tile(node_weight, 2)[None, :], F32)
    spread = np.zeros((NQ, NQ, LANES))
    spread[:, :, 0:NQ] = TAU_COEF * interp.transpose(0, 2, 1)
    spread[:, :, 64 : 64 + NQ] = TAU_COEF * interp.transpose(0, 2, 1)
    spread = jnp.asarray(spread.reshape(NQ * NQ, LANES), F32)

    packed = pack(vel_hat.reshape(ROWS, GROUPS * LANES))
    got = lax.all_to_all(packed, "four", 0, 0, tiled=True)
    trace = traces(rotor_element, packed)
    pieces = lax.all_gather(trace, "elem", axis=0, tiled=True)
    helm = helmholtz(
        metric, area, stator_element, packed, visc.reshape(GROUPS, LANES), weight, forward, back
    )
    advect_hat = planes(
        metric, got, as_left(cosine), as_left(sine), as_left(cos_back), as_left(sin_back), forward
    )
    nonlinear = lax.all_to_all(advect_hat, "four", 0, 0, tiled=True)
    rest = penalty(stator_source, stator_element, mortar_offset, spread, pieces, helm)
    return final_sum(nonlinear, rest).reshape(vel_hat.shape)


def solution(mesh):
    in_specs = (
        P(None, "four", "elem"),
        P(None, "elem"),
        P("elem"),
        P("elem"),
        P("elem"),
        P("elem"),
        P("elem"),
        P("elem"),
    )
    out_specs = P(None, "four", "elem")
    return jax.shard_map(local, mesh=mesh, in_specs=in_specs, out_specs=out_specs, check_vma=False)
```

profile of v0, /device:TPU:1, one launch (start us, length us, event | category | flops | bytes accessed | tf_op | source)
XLA Modules:
  0.0 68.6 jit_solution(10997453134359437600)
XLA Ops:
  6.5 0.0 all-gather.2.cloned.1.call-start
  6.5 0.0 copy-start
  6.5 0.0 copy-start.1
  6.5 0.0 copy-start.2
  6.5 0.0 copy-start.3
  6.6 0.0 copy-start.4
  6.6 0.0 copy-start.5
  6.6 2.2 %pack.1.packed_ref = f32[16,96,128]{2,1,0:T(8,128)} custom-call(f32[96,2048]{1,0:T(8,128)} %bitcast.3), custom_call_target="tpu_custom_call" | custom-call | bytes 1600000 | tf_op jit(solution)/shard_map/pack/pallas_call | solution.py:147
  8.8 2.2 %traces.1 = f32[256,128]{1,0:T(8,128)} custom-call(s32[32]{0:T(128)} %rotor_ref.1, f32[16,96,128]{2,1,0:T(8,128)} %pack.1.packed_ref), custom_call_target="tpu_custom_call" | custom-call | bytes 8000000 | tf_op jit(solution)/shard_map/traces/pallas_call | solution.py:175
  10.9 0.0 all-gather.2.cloned.1.call-update
  11.0 21.1 %all_to_all.10.got_ref = f32[16,96,128]{2,1,0:T(8,128)S(1)} all-to-all(f32[16,96,128]{2,1,0:T(8,128)} %pack.1.packed_ref), channel_id=1, replica_groups=mesh['elem'=16,'four'=16] {'four'}, dimensions={0} | all-to-all | bytes 1572864 | tf_op jit(solution)/shard_map/all_to_all | solution.py:419
  32.1 0.0 copy-done
  32.1 0.0 copy-done.1
  32.1 0.0 copy-done.2
  32.1 0.0 copy-done.3
  32.1 0.0 copy-done.4
  32.1 0.0 copy-done.5
  32.1 4.1 %planes.1 = f32[16,96,128]{2,1,0:T(8,128)} custom-call(f32[4,32]{1,0:T(4,128)S(1)} %copy-done, f32[16,96,128]{2,1,0:T(8,128)S(1)} %all_to_all.10.got_ref, bf16[384,768]{1,0:T(8,128)(2,1)S(1)} %copy-done.4, bf16[384,768]{1,0:T(8,128)(2,1)S(1)} %copy-done.3, bf16[256,1152]{1,0:T(8,128)(2,1)S(1)} %copy-done.2, bf16[256,1152]{1,0:T(8,128)(2,1)S(1)} %copy-done.1, ...), custom_call_target="tpu_custom_call" | custom-call | flops 3000000000 | bytes 4000000 | tf_op jit(solution)/shard_map/planes/pallas_call | solution.py:322
  36.2 3.6 %all-to-all-start.1 = ((f32[16,96,128]{2,1,0:T(8,128)}), f32[16,96,128]{2,1,0:T(8,128)S(1)}, u32[]{:S(2)}, u32[]{:S(2)}) async-start(f32[16,96,128]{2,1,0:T(8,128)} %planes.1), calls=%async_computation.1 | async-start | bytes 1572864 | tf_op jit(solution)/shard_map/all_to_all | solution.py:428
  39.8 5.1 %helm.1.helm_ref = f32[16,96,128]{2,1,0:T(8,128)} custom-call(f32[4,32]{1,0:T(4,128)} %metric_ref.3, f32[32]{0:T(128)} %area_ref.1, s32[32]{0:T(128)} %stator_ref.3, f32[16,96,128]{2,1,0:T(8,128)} %pack.1.packed_ref, f32[16,128]{1,0:T(8,128)} %bitcast.4, f32[1,128]{1,0:T(1,128)} %constant.18.clone.weight_ref, bf16[384,256]{1,0:T(8,128)(2,1)} %constant.16.clone.forward_ref, ...), custom_call_target="tpu_custom_call" | custom-call | flops 2000000000 | bytes 8000000 | tf_op jit(solution)/shard_map/helm/pallas_call | solution.py:233
  44.9 9.9 %all-gather.2.cloned.1.call-done.pieces_ref = f32[4096,128]{1,0:T(8,128)} async-done(((f32[256,128]{1,0:T(8,128)}), f32[4096,128]{1,0:T(8,128)}) %all-gather.2.cloned.1.call-update) | async-done | bytes 2097168 | tf_op jit(solution)/shard_map/all_gather | solution.py:421
  54.9 3.6 %penalty.1.rest_ref = f32[16,96,128]{2,1,0:T(8,128)} custom-call(s32[32]{0:T(128)} %source_ref.1, s32[32]{0:T(128)} %stator_ref.3, s32[32]{0:T(128)} %offset_ref.1, f32[64,128]{1,0:T(8,128)} %constant.19.clone.interp_ref, f32[4096,128]{1,0:T(8,128)} %all-gather.2.cloned.1.call-done.pieces_ref, f32[16,96,128]{2,1,0:T(8,128)} %helm.1.helm_ref), custom_call_target="tpu_custom_call" | custom-call | flops 1000000000 | bytes 8000000 | tf_op jit(solution)/shard_map/penalty/pallas_call | solution.py:357
  58.5 0.0 all-to-all-done.1.nonlinear_ref
  58.5 0.0 copy-start.6
  58.5 0.9 %copy-done.6 = f32[16,96,128]{2,1,0:T(8,128)} copy-done((f32[16,96,128]{2,1,0:T(8,128)}, f32[16,96,128]{2,1,0:T(8,128)S(1)}, u32[]{:S(2)}) %copy-start.6) | copy-done | bytes 786456
  59.3 2.4 %final_sum.1 = f32[96,2048]{1,0:T(8,128)} custom-call(f32[16,96,128]{2,1,0:T(8,128)} %copy-done.6, f32[16,96,128]{2,1,0:T(8,128)} %penalty.1.rest_ref), custom_call_target="tpu_custom_call" | custom-call | bytes 2400000 | tf_op jit(solution)/shard_map/final_sum/pallas_call | solution.py:393
Async XLA Ops:
  6.5 48.4 %all-gather.2.cloned.1.call-start = ((), (), s32[]{:S(2)}) async-start(), calls=%async_computation.2 | async-start | bytes 2228224 | tf_op jit(solution)/shard_map/all_gather | solution.py:421
  6.5 25.5 %copy-start = (f32[4,32]{1,0:T(4,128)S(1)}, f32[4,32]{1,0:T(4,128)}, u32[]{:S(2)}) copy-start(f32[4,32]{1,0:T(4,128)} %metric_ref.3) | copy-start | bytes 1540
  6.5 25.5 %copy-start.1 = (bf16[256,1152]{1,0:T(8,128)(2,1)S(1)}, bf16[256,1152]{1,0:T(8,128)(2,1)}, u32[]{:S(2)}) copy-start(bf16[256,1152]{1,0:T(8,128)(2,1)} %constant.23.clone.sin_back_ref) | copy-start | bytes 1769476
  6.5 25.5 %copy-start.2 = (bf16[256,1152]{1,0:T(8,128)(2,1)S(1)}, bf16[256,1152]{1,0:T(8,128)(2,1)}, u32[]{:S(2)}) copy-start(bf16[256,1152]{1,0:T(8,128)(2,1)} %constant.22.clone.cos_back_ref) | copy-start | bytes 1769476
  6.5 25.5 %copy-start.3 = (bf16[384,768]{1,0:T(8,128)(2,1)S(1)}, bf16[384,768]{1,0:T(8,128)(2,1)}, u32[]{:S(2)}) copy-start(bf16[384,768]{1,0:T(8,128)(2,1)} %constant.21.clone.sin_ref) | copy-start | bytes 1769476
  6.6 25.5 %copy-start.4 = (bf16[384,768]{1,0:T(8,128)(2,1)S(1)}, bf16[384,768]{1,0:T(8,128)(2,1)}, u32[]{:S(2)}) copy-start(bf16[384,768]{1,0:T(8,128)(2,1)} %constant.20.clone.cos_ref) | copy-start | bytes 1769476
  6.6 25.5 %copy-start.5 = (bf16[384,256]{1,0:T(8,128)(2,1)S(1)}, bf16[384,256]{1,0:T(8,128)(2,1)}, u32[]{:S(2)}) copy-start(bf16[384,256]{1,0:T(8,128)(2,1)} %constant.16.clone.forward_ref) | copy-start | bytes 589828
  36.2 22.2 %all-to-all-start.1 = ((f32[16,96,128]{2,1,0:T(8,128)}), f32[16,96,128]{2,1,0:T(8,128)S(1)}, u32[]{:S(2)}, u32[]{:S(2)}) async-start(f32[16,96,128]{2,1,0:T(8,128)} %planes.1), calls=%async_computation.1 | async-start | bytes 1572864 | tf_op jit(solution)/shard_map/all_to_all | solution.py:428
  58.5 0.9 %copy-start.6 = (f32[16,96,128]{2,1,0:T(8,128)}, f32[16,96,128]{2,1,0:T(8,128)S(1)}, u32[]{:S(2)}) copy-start(f32[16,96,128]{2,1,0:T(8,128)S(1)} %all-to-all-done.1.nonlinear_ref) | copy-start | bytes 2359300
Sparse Core Ops, SparseCore 0:
  11.1 43.7 all-gather.1
where the time goes:
time: 69 us; the launch traced here: 68.6 us
  blocking collectives  21.1 us (31%)
  Pallas kernels  19.5 us (28%)
  between operations  13.5 us (20%)
  waiting for transfers between devices  9.96 us (14%)
  starting transfers between devices  3.61 us (5%)
  local copies, waits for them, and re-layouts  0.92 us (1%)
    all_to_all x1, blocking collectives, local(): got = lax.all_to_all(packed, 'four', 0, 0, tiled=True)  21.1 us
    all_gather x1, waiting for transfers between devices, local(): pieces = lax.all_gather(trace, 'elem', axis=0, tiled=True)  9.94 us
    pallas_call x1, Pallas kernels, helmholtz(): pl.pallas_call(helm_kernel, grid=(GROUPS // step,), in_specs=[pl.BlockSpe...  5.11 us
    pallas_call x1, Pallas kernels, planes(): pl.pallas_call(plane_kernel, in_specs=[pl.BlockSpec(memory_space=SMEM)] +...  4.1 us
    all_to_all x1, starting transfers between devices, local(): nonlinear = lax.all_to_all(advect_hat, 'four', 0, 0, tiled=True)  3.61 us
    pallas_call x1, Pallas kernels, penalty(): pl.pallas_call(penalty_kernel, in_specs=[scalars] * 3 + [whole] * 3, out_...  3.56 us
    pallas_call x1, Pallas kernels, final_sum(): pl.pallas_call(sum_kernel, in_specs=[whole, whole], out_specs=pl.BlockSpe...  2.38 us
    pallas_call x1, Pallas kernels, pack(): pl.pallas_call(pack_kernel, in_specs=[anywhere], out_specs=anywhere, out_...  2.19 us
  transfers between devices with their start and end apart: 2, of which 1 were waited for; matrix products, arithmetic and copies ran while one was open for 0% of the time, Pallas kernels for 19%

commit v1 on v0

--- a/solution.py
+++ b/solution.py
@@ -13,6 +13,8 @@
 PLANES = 768
 HALF = PLANES // 2
 PAIRS = MODES // 2
+HELD = 9
+RING = 8
 GROUPS = 16
 ROWS = 96
 LANES = 128
@@ -119,27 +121,24 @@
     return jnp.where(lane < LANES // 2, first, second)
 
 
-def pack_kernel(field_ref, out_ref, in_ref, done_ref, in_sems, out_sems):
-    def load(block):
-        return pltpu.make_async_copy(
-            field_ref.at[:, pl.ds(block * LANES, LANES)], in_ref.at[block], in_sems.at[block]
+def pack_kernel(field_ref, out_ref, held_ref, in_sems, out_sems):
+    loads = [
+        pltpu.make_async_copy(
+            field_ref.at[:, pl.ds(block * LANES, LANES)], held_ref.at[block], in_sems.at[block]
         )
-
-    def store(block):
-        return pltpu.make_async_copy(done_ref.at[block], out_ref.at[block], out_sems.at[block])
-
-    for block in range(GROUPS):
-        load(block).start()
-    for block in range(GROUPS):
-        load(block).wait()
-        for component in range(3):
-            for parity in range(2):
-                done_ref[block, pl.ds(component * 32 + parity * 16, 16), :] = in_ref[
-                    block, pl.ds(component * 32 + parity, 16, stride=2), :
-                ]
-        store(block).start()
-    for block in range(GROUPS):
-        store(block).wait()
+        for block in range(GROUPS)
+    ]
+    stores = [
+        pltpu.make_async_copy(held_ref.at[block], out_ref.at[block], out_sems.at[block])
+        for block in range(GROUPS)
+    ]
+    for load in loads:
+        load.start()
+    for load, store in zip(loads, stores):
+        load.wait()
+        store.start()
+    for store in stores:
+        store.wait()
 
 
 def pack(field):
@@ -150,7 +149,6 @@
         out_specs=anywhere,
         out_shape=jax.ShapeDtypeStruct((GROUPS, ROWS, LANES), F32),
         scratch_shapes=[
-            pltpu.VMEM((GROUPS, ROWS, LANES), F32),
             pltpu.VMEM((GROUPS, ROWS, LANES), F32),
             pltpu.SemaphoreType.DMA((GROUPS,)),
             pltpu.SemaphoreType.DMA((GROUPS,)),
@@ -161,11 +159,17 @@
 
 
 def trace_kernel(rotor_ref, packed_ref, out_ref, top_ref):
+    lane = lax.broadcasted_iota(jnp.int32, (ROWS, LANES), 1)
     zeros = jnp.zeros((LANES - ROWS, LANES), F32)
-    for block in range(GROUPS):
-        turned = jnp.concatenate([packed_ref[block], zeros], 0).T
-        top_ref[pl.ds(block * 16, 8), :] = turned[56:64]
-        top_ref[pl.ds(block * 16 + 8, 8), :] = turned[120:128]
+    for half in range(2):
+        rows = jnp.zeros((ROWS, LANES), F32)
+        for block in range(8):
+            field = packed_ref[half * 8 + block]
+            low = pltpu.roll(field, (16 * block - 56) % LANES, 1)
+            high = pltpu.roll(field, (16 * block + 8 - 120) % LANES, 1)
+            rows = jnp.where(lane // 8 == 2 * block, low, rows)
+            rows = jnp.where(lane // 8 == 2 * block + 1, high, rows)
+        top_ref[pl.ds(half * LANES, LANES), :] = jnp.concatenate([rows, zeros], 0).T
     for slot in range(32):
         start = pl.multiple_of(rotor_ref[slot] * 8, 8)
         out_ref[pl.ds(slot * 8, 8), :] = top_ref[pl.ds(start, 8), :]
@@ -183,17 +187,52 @@
     )(rotor_element, packed)
 
 
+def pair_kernel(mine_ref, other_ref, out_ref):
+    out_ref[pl.ds(0, 256), :] = mine_ref[...]
+    out_ref[pl.ds(256, 256), :] = other_ref[...]
+
+
+def pair(mine, other):
+    whole = pl.BlockSpec(memory_space=VMEM)
+    return pl.pallas_call(
+        pair_kernel,
+        in_specs=[whole, whole],
+        out_specs=whole,
+        out_shape=jax.ShapeDtypeStruct((512, LANES), F32),
+        cost_estimate=pl.CostEstimate(flops=0, bytes_accessed=1000000, transcendentals=0),
+        name="pair",
+    )(mine, other)
+
+
+def moves(distance, cores=(0, 1)):
+    return [
+        (2 * z + c, 2 * ((z + (distance if c == 0 else -distance)) % RING) + c)
+        for z in range(RING)
+        for c in cores
+    ]
+
+
+ACROSS = [(i, i ^ 1) for i in range(2 * RING)]
+
+
 def helm_kernel(
-    metric_ref, area_ref, stator_ref, packed_ref, visc_ref, weight_ref, forward_ref, back_ref, out_ref
+    metric_ref, area_ref, stator_ref, packed_ref, visc_ref, weight_ref, forward_ref, back_ref, out_ref,
+    count_ref,
 ):
     step = packed_ref.shape[0]
     first = pl.program_id(0) * step
+
+    @pl.when(pl.program_id(0) == 0)
+    def _():
+        for element in range(32):
+            count_ref[element] = 0
+        for edge in range(32):
+            count_ref[stator_ref[edge]] = count_ref[stator_ref[edge]] + 1
+
     four = lax.axis_index("four")
     row = lax.broadcasted_iota(jnp.int32, (ROWS, LANES), 0)
     inner = row % 32
-    number = jnp.where(
-        (inner == 16) & (four == 0), MODES // 2, four * 16 + inner % 16
-    )
+    number = jnp.where((inner == 1) & (four == 0), MODES // 2, four * 16 + inner // 2)
     wave = number.astype(F32) / KZ_DIV
     wave_sq = wave * wave
     lane = lax.broadcasted_iota(jnp.int32, (1, LANES), 1)
@@ -206,12 +245,7 @@
         rx, ry, sx, sy = [
             lane_scalars(metric_ref[i, pair], metric_ref[i, pair + 1]) for i in range(4)
         ]
-        count_a, count_b = jnp.int32(0), jnp.int32(0)
-        for edge in range(32):
-            here = stator_ref[edge]
-            count_a = count_a + jnp.where(here == pair, 1, 0)
-            count_b = count_b + jnp.where(here == pair + 1, 1, 0)
-        count = lane_scalars(count_a, count_b).astype(F32)
+        count = lane_scalars(count_ref[pair], count_ref[pair + 1]).astype(F32)
         own = jnp.where(bottom, TAU_COEF * count, 0.0)
         area = lane_scalars(area_ref[pair], area_ref[pair + 1])
         weight = area * weight_ref[...]
@@ -245,6 +279,7 @@
         ],
         out_specs=pl.BlockSpec((step, ROWS, LANES), lambda i: (i, 0, 0)),
         out_shape=jax.ShapeDtypeStruct((GROUPS, ROWS, LANES), F32),
+        scratch_shapes=[pltpu.SMEM((32,), jnp.int32)],
         cost_estimate=pl.CostEstimate(flops=2000000000, bytes_accessed=8000000, transcendentals=0),
         name="helm",
     )(metric, area, stator_element, packed, visc, weight, forward, back)
@@ -265,8 +300,9 @@
     is_first = plane == 0
     evens, odds = [], []
     for component in range(3):
-        evens.append(got_ref[:, pl.ds(component * 32, 16), :].reshape(PAIRS, LANES))
-        odds.append(got_ref[:, pl.ds(component * 32 + 16, 16), :].reshape(PAIRS, LANES))
+        start = component * 32
+        evens.append(got_ref[:, pl.ds(start, 16, stride=2), :].reshape(PAIRS, LANES))
+        odds.append(got_ref[:, pl.ds(start + 1, 16, stride=2), :].reshape(PAIRS, LANES))
     evens_z = [wave * odd for odd in odds]
     odds_z = [-wave * even for even in evens]
     last_cos = [odd[0:1] for odd in odds]
@@ -313,8 +349,9 @@
             jnp.sum(third * even_sum[component], 0, keepdims=True) + middles[component]
         )
         odd_here = jnp.where(number == 0, last, odd_out[:, lanes])
-        out_ref[:, pl.ds(component * 32, 16), :] = even_here.reshape(GROUPS, 16, LANES)
-        out_ref[:, pl.ds(component * 32 + 16, 16), :] = odd_here.reshape(GROUPS, 16, LANES)
+        start = component * 32
+        out_ref[:, pl.ds(start, 16, stride=2), :] = even_here.reshape(GROUPS, 16, LANES)
+        out_ref[:, pl.ds(start + 1, 16, stride=2), :] = odd_here.reshape(GROUPS, 16, LANES)
 
 
 def planes(metric, got, cosine, sine, cos_back, sin_back, forward):
@@ -330,25 +367,45 @@
     )(metric, got, cosine, sine, cos_back, sin_back, forward)
 
 
-def penalty_kernel(
-    source_ref, stator_ref, offset_ref, interp_ref, pieces_ref, helm_ref, out_ref,
-    received_ref, base_ref, place_ref,
-):
+def penalty_kernel(source_ref, stator_ref, offset_ref, interp_ref, *refs):
+    piece_refs, refs = refs[:HELD], refs[HELD:]
+    helm_ref, out_ref, received_ref, base_ref, place_ref = refs
+    elem = lax.axis_index("elem")
     for edge in range(32):
         rows = pl.ds(edge * 8, 8)
-        start = pl.multiple_of(source_ref[edge] * 8, 8)
-        received_ref[rows, :] = pieces_ref[pl.ds(start, 8), :]
         base_ref[rows, :] = interp_ref[pl.ds(pl.multiple_of(offset_ref[edge] * 8, 8), 8), :]
-        place_ref[rows, :] = jnp.full((8, LANES), stator_ref[edge], jnp.int32)
-    lane = lax.broadcasted_iota(jnp.int32, (256, LANES), 1)
-    home = place_ref[...] - jnp.where(lane < 64, 0, 1)
-    base = base_ref[...]
-    left = left_split(received_ref[...].T[:ROWS])
+        place_ref[rows, :] = jnp.full((8, 256), stator_ref[edge], jnp.int32)
+    lane = lax.broadcasted_iota(jnp.int32, (256, 256), 1)
+    matrix = jnp.where(place_ref[...] == lane // 8, base_ref[...], 0.0)
+    high, low = split(matrix)
+    right = jnp.concatenate([high, low, high], 0)
+    core = elem % 2
+    for edge in range(32):
+        source = source_ref[edge]
+        owner, slot = source // 32, source % 32
+        owner_core = owner % 2
+        behind = (elem // 2 - owner // 2 + RING) % RING
+        near = jnp.where(behind <= 4, behind, RING - behind)
+        side = jnp.where(
+            behind == 0, core, jnp.where(behind == 4, owner_core, jnp.where(behind < 4, 0, 1))
+        )
+        piece = jnp.where((behind == 0) | (side == core), near, near + 4)
+        first = pl.multiple_of(slot * 8, 8)
+        start = pl.multiple_of((jnp.where(side == owner_core, 0, 32) + slot) * 8, 8)
+        tile = piece_refs[0][pl.ds(start, 8), :]
+        for index in range(1, HELD):
+            at = first if index % 4 == 0 else start
+            tile = jnp.where(piece == index, piece_refs[index][pl.ds(at, 8), :], tile)
+        received_ref[pl.ds(edge * 8, 8), :] = tile
+    placed = dot(left_split(received_ref[...].T[:ROWS]), right)
+    lane = lax.broadcasted_iota(jnp.int32, (ROWS, LANES), 1)
     for block in range(GROUPS):
-        matrix = jnp.where(home == 2 * block, base, 0.0)
-        high, low = split(matrix)
-        right = jnp.concatenate([high, low, high], 0)
-        out_ref[block] = helm_ref[block] - dot(left, right)
+        half = placed[:, (block // 8) * LANES : (block // 8 + 1) * LANES]
+        start = 16 * (block % 8)
+        low = pltpu.roll(half, (-start) % LANES, 1)
+        high = pltpu.roll(half, (64 - 8 - start) % LANES, 1)
+        value = jnp.where(lane < 8, low, jnp.where(lane // 8 == 8, high, 0.0))
+        out_ref[block] = helm_ref[block] - value
 
 
 def penalty(stator_source, stator_element, mortar_offset, interp, pieces, helm):
@@ -356,47 +413,51 @@
     scalars = pl.BlockSpec(memory_space=SMEM)
     return pl.pallas_call(
         penalty_kernel,
-        in_specs=[scalars] * 3 + [whole] * 3,
+        in_specs=[scalars] * 3 + [whole] * (HELD + 2),
         out_specs=whole,
         out_shape=jax.ShapeDtypeStruct((GROUPS, ROWS, LANES), F32),
         scratch_shapes=[
             pltpu.VMEM((256, LANES), F32),
-            pltpu.VMEM((256, LANES), F32),
-            pltpu.VMEM((256, LANES), jnp.int32),
+            pltpu.VMEM((256, 256), F32),
+            pltpu.VMEM((256, 256), jnp.int32),
         ],
-        cost_estimate=pl.CostEstimate(flops=1000000000, bytes_accessed=8000000, transcendentals=0),
+        cost_estimate=pl.CostEstimate(flops=1000, bytes_accessed=1000, transcendentals=0),
         name="penalty",
-    )(stator_source, stator_element, mortar_offset, interp, pieces, helm)
-
-
-def sum_kernel(nonlinear_ref, rest_ref, out_ref, done_ref, out_sems):
-    def store(block):
-        return pltpu.make_async_copy(
+    )(stator_source, stator_element, mortar_offset, interp, *pieces, helm)
+
+
+def sum_kernel(nonlinear_ref, rest_ref, out_ref, in_ref, done_ref, in_sems, out_sems):
+    loads = [
+        pltpu.make_async_copy(nonlinear_ref.at[block], in_ref.at[block], in_sems.at[block])
+        for block in range(GROUPS)
+    ]
+    stores = [
+        pltpu.make_async_copy(
             done_ref.at[block], out_ref.at[:, pl.ds(block * LANES, LANES)], out_sems.at[block]
         )
-
+        for block in range(GROUPS)
+    ]
+    for load in loads:
+        load.start()
     for block in range(GROUPS):
-        value = -nonlinear_ref[block] - rest_ref[block]
-        for component in range(3):
-            for parity in range(2):
-                start = component * 32 + parity * 16
-                done_ref[block, pl.ds(component * 32 + parity, 16, stride=2), :] = value[
-                    start : start + 16
-                ]
-        store(block).start()
-    for block in range(GROUPS):
-        store(block).wait()
+        loads[block].wait()
+        done_ref[block] = -in_ref[block] - rest_ref[block]
+        stores[block].start()
+    for store in stores:
+        store.wait()
 
 
 def final_sum(nonlinear, rest):
-    whole = pl.BlockSpec(memory_space=VMEM)
+    anywhere = pl.BlockSpec(memory_space=pl.ANY)
     return pl.pallas_call(
         sum_kernel,
-        in_specs=[whole, whole],
-        out_specs=pl.BlockSpec(memory_space=pl.ANY),
+        in_specs=[anywhere, pl.BlockSpec(memory_space=VMEM)],
+        out_specs=anywhere,
         out_shape=jax.ShapeDtypeStruct((ROWS, GROUPS * LANES), F32),
         scratch_shapes=[
             pltpu.VMEM((GROUPS, ROWS, LANES), F32),
+            pltpu.VMEM((GROUPS, ROWS, LANES), F32),
+            pltpu.SemaphoreType.DMA((GROUPS,)),
             pltpu.SemaphoreType.DMA((GROUPS,)),
         ],
         cost_estimate=pl.CostEstimate(flops=0, bytes_accessed=2400000, transcendentals=0),
@@ -410,22 +471,27 @@
     forward = as_right(np.concatenate([along_xi.T, along_eta.T], 1))
     back = as_right(np.concatenate([along_xi, along_eta], 0))
     weight = jnp.asarray(np.tile(node_weight, 2)[None, :], F32)
-    spread = np.zeros((NQ, NQ, LANES))
-    spread[:, :, 0:NQ] = TAU_COEF * interp.transpose(0, 2, 1)
-    spread[:, :, 64 : 64 + NQ] = TAU_COEF * interp.transpose(0, 2, 1)
-    spread = jnp.asarray(spread.reshape(NQ * NQ, LANES), F32)
+    spread = np.tile(TAU_COEF * interp.transpose(0, 2, 1), (1, 1, 32))
+    spread = jnp.asarray(spread.reshape(NQ * NQ, 256), F32)
 
     packed = pack(vel_hat.reshape(ROWS, GROUPS * LANES))
     got = lax.all_to_all(packed, "four", 0, 0, tiled=True)
-    trace = traces(rotor_element, packed)
-    pieces = lax.all_gather(trace, "elem", axis=0, tiled=True)
+    mine = traces(rotor_element, packed)
+    both = pair(mine, lax.ppermute(mine, "elem", ACROSS))
+    one = lax.ppermute(both, "elem", moves(1))
+    two = lax.ppermute(both, "elem", moves(2))
     helm = helmholtz(
         metric, area, stator_element, packed, visc.reshape(GROUPS, LANES), weight, forward, back
     )
+    got, helm = lax.optimization_barrier((got, helm))
     advect_hat = planes(
         metric, got, as_left(cosine), as_left(sine), as_left(cos_back), as_left(sin_back), forward
     )
     nonlinear = lax.all_to_all(advect_hat, "four", 0, 0, tiled=True)
+    three = lax.ppermute(two, "elem", moves(1))
+    four = lax.ppermute(two[:256], "elem", moves(2))
+    held = [one, two, three, four]
+    pieces = [both] + held + [lax.ppermute(piece, "elem", ACROSS) for piece in held]
     rest = penalty(stator_source, stator_element, mortar_offset, spread, pieces, helm)
     return final_sum(nonlinear, rest).reshape(vel_hat.shape)
 

time: 69 us -> 61.5 us (0.89)
  starting transfers between devices: 3.61 us -> 26.4 us
  blocking collectives: 21.1 us -> 0 us
  between operations: 13.5 us -> 0.16 us
  Pallas kernels: 19.5 us -> 22.7 us
  local copies, waits for them, and re-layouts: 0.92 us -> 4.05 us
  waiting for transfers between devices: 9.96 us -> 7.49 us
    all_to_all x1 -> x0, blocking collectives: 21.1 us -> none  [local(): got = lax.all_to_all(packed, 'four', 0, 0, tiled=True)]
    ppermute x0 -> x9, starting transfers between devices: none -> 11.8 us  [the longest x1 6.02 us: local(): two = lax.ppermute(both, 'elem', moves(2))]
    all_gather x1 -> x0, waiting for transfers between devices: 9.94 us -> none  [local(): pieces = lax.all_gather(trace, 'elem', axis=0, tiled=True)]
    all_to_all x0 -> x1, starting transfers between devices: none -> 7.6 us  [local(): got = lax.all_to_all(packed, 'four', 0, 0, tiled=True)]
    ppermute x0 -> x9, waiting for transfers between devices: none -> 7.48 us  [the longest x1 3.26 us: local(): four = lax.ppermute(two[:256], 'elem', moves(2))]
    all_to_all x1, starting transfers between devices: 3.61 us -> 7.07 us  [local(): nonlinear = lax.all_to_all(advect_hat, 'four', 0, 0, tiled=True)]
    pallas_call x2 -> x3, Pallas kernels: 5.94 us -> 9.19 us  [the longest x1 4.31 us: penalty(): pl.pallas_call(penalty_kernel, in_specs=[scalars] * 3 + [whole] * (HELD +...]
    unnamed x14 -> x32, local copies, waits for them, and re-layouts: 0.92 us -> 3.11 us
  transfers between devices with their start and end apart: 2 -> 11, of which waited for: 1 -> 4; matrix products, arithmetic and copies ran while one was open for 0% -> 2% of each run, Pallas kernels for 19% -> 29%
where the time goes in v1:
time: 61.5 us; the launch traced here: 60.9 us
  starting transfers between devices  26.4 us (43%)
  Pallas kernels  22.7 us (37%)
  waiting for transfers between devices  7.49 us (12%)
  local copies, waits for them, and re-layouts  4.05 us (7%)
    all_to_all x1, starting transfers between devices, local(): got = lax.all_to_all(packed, 'four', 0, 0, tiled=True)  7.6 us
    all_to_all x1, starting transfers between devices, local(): nonlinear = lax.all_to_all(advect_hat, 'four', 0, 0, tiled=True)  7.07 us
    ppermute x1, starting transfers between devices, local(): two = lax.ppermute(both, 'elem', moves(2))  6.02 us
    pallas_call x1, Pallas kernels, helmholtz(): pl.pallas_call(helm_kernel, grid=(GROUPS // step,), in_specs=[pl.BlockSpe...  5.08 us
    pallas_call x1, Pallas kernels, penalty(): pl.pallas_call(penalty_kernel, in_specs=[scalars] * 3 + [whole] * (HELD +...  4.31 us
    pallas_call x1, Pallas kernels, planes(): pl.pallas_call(plane_kernel, in_specs=[pl.BlockSpec(memory_space=SMEM)] +...  4.01 us
    ppermute x1, waiting for transfers between devices, local(): four = lax.ppermute(two[:256], 'elem', moves(2))  3.26 us
    ppermute x4, starting transfers between devices, local(): lax.ppermute(piece, 'elem', ACROSS)  3.19 us
  transfers between devices with their start and end apart: 11, of which 4 were waited for; matrix products, arithmetic and copies ran while one was open for 2% of the time, Pallas kernels for 29%

profile of v1, /device:TPU:1, one launch (start us, length us, event | category | flops | bytes accessed | tf_op | source)
XLA Modules:
  0.0 60.9 jit_solution(13103382160912982226)
XLA Ops:
  0.0 2.0 %pack.1.packed_ref = f32[16,96,128]{2,1,0:T(8,128)} custom-call(f32[96,2048]{1,0:T(8,128)} %bitcast.3), custom_call_target="tpu_custom_call" | custom-call | bytes 1600000 | tf_op jit(solution)/shard_map/pack/pallas_call | solution.py:146
  2.0 7.6 %all-to-all-start = ((f32[16,96,128]{2,1,0:T(8,128)}), f32[16,96,128]{2,1,0:T(8,128)S(1)}, u32[]{:S(2)}, u32[]{:S(2)}) async-start(f32[16,96,128]{2,1,0:T(8,128)} %pack.1.packed_ref), calls=%async_computation | async-start | bytes 1572864 | tf_op jit(solution)/shard_map/all_to_all | solution.py:478
  9.6 2.4 %traces.1.mine_ref = f32[256,128]{1,0:T(8,128)} custom-call(s32[32]{0:T(128)} %rotor_ref.1, f32[16,96,128]{2,1,0:T(8,128)} %pack.1.packed_ref), custom_call_target="tpu_custom_call" | custom-call | bytes 8000000 | tf_op jit(solution)/shard_map/traces/pallas_call | solution.py:179
  12.0 1.0 %collective-permute-start = (f32[256,128]{1,0:T(8,128)}, f32[256,128]{1,0:T(8,128)S(1)}, u32[]{:S(2)}, u32[]{:S(2)}) collective-permute-start(f32[256,128]{1,0:T(8,128)} %traces.1.mine_ref), channel_id=1, source_target_pairs={{0,16},{16,0},{32,48},{48,32},{64,80},{80,64},{96,112},{112,96},{1... | collective-permute-start | bytes 393224 | tf_op jit(solution)/shard_map/ppermute | solution.py:480
  13.0 5.1 %helm.1.refs_9_ = f32[16,96,128]{2,1,0:T(8,128)} custom-call(f32[4,32]{1,0:T(4,128)} %metric_ref.3, f32[32]{0:T(128)} %area_ref.1, s32[32]{0:T(128)} %stator_ref.3, f32[16,96,128]{2,1,0:T(8,128)} %pack.1.packed_ref, f32[16,128]{1,0:T(8,128)} %bitcast.4, f32[1,128]{1,0:T(1,128)} %constant.18.clone.weight_ref, bf16[384,256]{1,0:T(8,128)(2,1)} %constant.16.clone.forward_ref, ...), custom_call_target="tpu_custom_call" | custom-call | flops 2000000000 | bytes 8000000 | tf_op jit(solution)/shard_map/helm/pallas_call | solution.py:267
  18.1 0.0 collective-permute-done.other_ref
  18.1 0.0 copy-start.15
  18.1 0.6 %copy-done.15 = f32[256,128]{1,0:T(8,128)} copy-done((f32[256,128]{1,0:T(8,128)}, f32[256,128]{1,0:T(8,128)S(1)}, u32[]{:S(2)}) %copy-start.15) | copy-done | bytes 131096
  18.8 1.7 %pair.1.refs_0_ = f32[512,128]{1,0:T(8,128)} custom-call(f32[256,128]{1,0:T(8,128)} %traces.1.mine_ref, f32[256,128]{1,0:T(8,128)} %copy-done.15), custom_call_target="tpu_custom_call" | custom-call | bytes 1000000 | tf_op jit(solution)/shard_map/pair/pallas_call | solution.py:197
  20.5 6.0 %collective-permute-start.2 = (f32[512,128]{1,0:T(8,128)}, f32[512,128]{1,0:T(8,128)}, u32[]{:S(2)}, u32[]{:S(2)}) collective-permute-start(f32[512,128]{1,0:T(8,128)} %pair.1.refs_0_), channel_id=1, source_target_pairs={{0,64},{16,208},{32,96},{48,240},{64,128},{80,16},{96,160},{112,48... | collective-permute-start | bytes 786440 | tf_op jit(solution)/shard_map/ppermute | solution.py:482
  26.5 0.0 all-to-all-done.got_ref
  26.5 0.0 copy-done.1
  26.5 0.0 copy-done.2
  26.5 0.0 copy-done.3
  26.5 0.0 copy-done.4
  26.5 0.0 copy-done
  26.5 0.0 copy-done.5
  26.6 4.0 %planes.1 = f32[16,96,128]{2,1,0:T(8,128)} custom-call(f32[4,32]{1,0:T(4,128)S(1)} %copy-done, f32[16,96,128]{2,1,0:T(8,128)S(1)} %all-to-all-done.got_ref, bf16[384,768]{1,0:T(8,128)(2,1)S(1)} %copy-done.4, bf16[384,768]{1,0:T(8,128)(2,1)S(1)} %copy-done.3, bf16[256,1152]{1,0:T(8,128)(2,1)S(1)} %copy-done.2, bf16[256,1152]{1,0:T(8,128)(2,1)S(1)} %copy-done.1, ...), custom_call_target="tpu_custom_call" | custom-call | flops 3000000000 | bytes 4000000 | tf_op jit(solution)/shard_map/planes/pallas_call | solution.py:359
  30.6 7.1 %all-to-all-start.1 = ((f32[16,96,128]{2,1,0:T(8,128)}), f32[16,96,128]{2,1,0:T(8,128)S(1)}, u32[]{:S(2)}, u32[]{:S(2)}) async-start(f32[16,96,128]{2,1,0:T(8,128)} %planes.1), calls=%async_computation.1 | async-start | bytes 1572864 | tf_op jit(solution)/shard_map/all_to_all | solution.py:490
  37.6 0.0 copy-done.7
  37.7 0.8 %collective-permute-start.1 = (f32[512,128]{1,0:T(8,128)S(1)}, f32[512,128]{1,0:T(8,128)S(1)}, u32[]{:S(2)}, u32[]{:S(2)}) collective-permute-start(f32[512,128]{1,0:T(8,128)S(1)} %copy-done.7), channel_id=1, source_target_pairs={{0,32},{16,240},{32,64},{48,16},{64,96},{80,48},{96,128},{112,80},... | collective-permute-start | bytes 786440 | tf_op jit(solution)/shard_map/ppermute | solution.py:481
  38.5 0.0 collective-permute-done.2.refs_2_
  38.5 0.7 %collective-permute-start.3 = (f32[512,128]{1,0:T(8,128)}, f32[512,128]{1,0:T(8,128)S(1)}, u32[]{:S(2)}, u32[]{:S(2)}) collective-permute-start(f32[512,128]{1,0:T(8,128)} %collective-permute-done.2.refs_2_), channel_id=1, source_target_pairs={{0,32},{16,240},{32,64},{48,16},{64,96},{80,48},{96,128},{112,80},... | collective-permute-start | bytes 786440 | tf_op jit(solution)/shard_map/ppermute | solution.py:491
  39.2 0.9 %slice.4 = f32[256,128]{1,0:T(8,128)S(1)} slice(f32[512,128]{1,0:T(8,128)} %collective-permute-done.2.refs_2_), slice={[0:256], [0:128]} | slice | bytes 262144 | tf_op jit(solution)/shard_map/slice | solution.py:492
  40.1 0.1 collective-permute-start.4
  40.2 2.6 %collective-permute-start.6 = (f32[512,128]{1,0:T(8,128)}, f32[512,128]{1,0:T(8,128)S(1)}, u32[]{:S(2)}, u32[]{:S(2)}) collective-permute-start(f32[512,128]{1,0:T(8,128)} %collective-permute-done.2.refs_2_), channel_id=1, source_target_pairs={{0,16},{16,0},{32,48},{48,32},{64,80},{80,64},{96,112},{112,96},{1... | collective-permute-start | bytes 786440 | tf_op jit(solution)/shard_map/ppermute | solution.py:494
  42.8 0.4 collective-permute-done.1.refs_1_
  43.3 0.0 collective-permute-start.5
  43.3 2.8 %collective-permute-done.3.refs_3_ = f32[512,128]{1,0:T(8,128)S(1)} collective-permute-done((f32[512,128]{1,0:T(8,128)}, f32[512,128]{1,0:T(8,128)S(1)}, u32[]{:S(2)}, u32[]{:S(2)}) %collective-permute-start.3) | collective-permute-done | bytes 262176 | tf_op jit(solution)/shard_map/ppermute | solution.py:491
  46.1 0.0 collective-permute-start.7
  46.1 3.3 %collective-permute-done.4.refs_4_ = f32[256,128]{1,0:T(8,128)S(1)} collective-permute-done((f32[256,128]{1,0:T(8,128)S(1)}, f32[256,128]{1,0:T(8,128)S(1)}, u32[]{:S(2)}, u32[]{:S(2)}) %collective-permute-start.4) | collective-permute-done | bytes 131104 | tf_op jit(solution)/shard_map/ppermute | solution.py:492
  49.3 0.6 collective-permute-start.8
  49.9 1.0 %collective-permute-done.8.refs_8_ = f32[256,128]{1,0:T(8,128)S(1)} collective-permute-done((f32[256,128]{1,0:T(8,128)S(1)}, f32[256,128]{1,0:T(8,128)S(1)}, u32[]{:S(2)}, u32[]{:S(2)}) %collective-permute-start.8) | collective-permute-done | bytes 131104 | tf_op jit(solution)/shard_map/ppermute | solution.py:494
  50.9 0.0 collective-permute-done.6.refs_6_
  50.9 0.0 collective-permute-done.5.refs_5_
  50.9 0.0 copy-start.11
  50.9 0.0 collective-permute-done.7.refs_7_
  50.9 0.0 copy-done.8
  50.9 0.0 copy-done.9
  51.0 0.0 copy-done.13
  51.0 0.6 copy-done.14
  51.6 0.1 copy-done.10
  51.7 0.1 copy-done.11
  51.8 0.7 %copy-done.12 = f32[512,128]{1,0:T(8,128)} copy-done((f32[512,128]{1,0:T(8,128)}, f32[512,128]{1,0:T(8,128)S(1)}, u32[]{:S(2)}) %copy-start.12) | copy-done | bytes 262168
  52.5 4.3 %penalty.1.rest_ref = f32[16,96,128]{2,1,0:T(8,128)} custom-call(s32[32]{0:T(128)} %source_ref.1, s32[32]{0:T(128)} %stator_ref.3, s32[32]{0:T(128)} %offset_ref.1, f32[64,256]{1,0:T(8,128)} %constant.19.clone.interp_ref, f32[512,128]{1,0:T(8,128)} %pair.1.refs_0_, f32[512,128]{1,0:T(8,128)} %copy-done.8, f32[512,128]{1,0:T(8,128)} %collective-permute-done.2.refs_2_, ...), custom_call_target="tpu_custom_call" | custom-call | flops 1000 | bytes 1000 | tf_op jit(solution)/shard_map/penalty/pallas_call | solution.py:414
  56.8 0.0 all-to-all-done.1.nonlinear_ref
  56.8 0.9 %copy-done.6 = f32[16,96,128]{2,1,0:T(8,128)} copy-done((f32[16,96,128]{2,1,0:T(8,128)}, f32[16,96,128]{2,1,0:T(8,128)S(1)}, u32[]{:S(2)}) %copy-start.6) | copy-done | bytes 786456
  57.7 3.2 %final_sum.1 = f32[96,2048]{1,0:T(8,128)} custom-call(f32[16,96,128]{2,1,0:T(8,128)} %copy-done.6, f32[16,96,128]{2,1,0:T(8,128)} %penalty.1.rest_ref), custom_call_target="tpu_custom_call" | custom-call | bytes 2400000 | tf_op jit(solution)/shard_map/final_sum/pallas_call | solution.py:452
  (14 shorter events, 0.0 us)
Async XLA Ops:
  2.0 24.5 %all-to-all-start = ((f32[16,96,128]{2,1,0:T(8,128)}), f32[16,96,128]{2,1,0:T(8,128)S(1)}, u32[]{:S(2)}, u32[]{:S(2)}) async-start(f32[16,96,128]{2,1,0:T(8,128)} %pack.1.packed_ref), calls=%async_computation | async-start | bytes 1572864 | tf_op jit(solution)/shard_map/all_to_all | solution.py:478
  12.0 6.1 %collective-permute-start = (f32[256,128]{1,0:T(8,128)}, f32[256,128]{1,0:T(8,128)S(1)}, u32[]{:S(2)}, u32[]{:S(2)}) collective-permute-start(f32[256,128]{1,0:T(8,128)} %traces.1.mine_ref), channel_id=1, source_target_pairs={{0,16},{16,0},{32,48},{48,32},{64,80},{80,64},{96,112},{112,96},{1... | collective-permute-start | bytes 393224 | tf_op jit(solution)/shard_map/ppermute | solution.py:480
  13.0 13.5 %copy-start.1 = (bf16[256,1152]{1,0:T(8,128)(2,1)S(1)}, bf16[256,1152]{1,0:T(8,128)(2,1)}, u32[]{:S(2)}) copy-start(bf16[256,1152]{1,0:T(8,128)(2,1)} %constant.23.clone.sin_back_ref) | copy-start | bytes 1769476
  13.0 13.5 %copy-start.2 = (bf16[256,1152]{1,0:T(8,128)(2,1)S(1)}, bf16[256,1152]{1,0:T(8,128)(2,1)}, u32[]{:S(2)}) copy-start(bf16[256,1152]{1,0:T(8,128)(2,1)} %constant.22.clone.cos_back_ref) | copy-start | bytes 1769476
  13.0 13.5 %copy-start.3 = (bf16[384,768]{1,0:T(8,128)(2,1)S(1)}, bf16[384,768]{1,0:T(8,128)(2,1)}, u32[]{:S(2)}) copy-start(bf16[384,768]{1,0:T(8,128)(2,1)} %constant.21.clone.sin_ref) | copy-start | bytes 1769476
  13.0 13.5 %copy-start.4 = (bf16[384,768]{1,0:T(8,128)(2,1)S(1)}, bf16[384,768]{1,0:T(8,128)(2,1)}, u32[]{:S(2)}) copy-start(bf16[384,768]{1,0:T(8,128)(2,1)} %constant.20.clone.cos_ref) | copy-start | bytes 1769476
  18.1 8.4 %copy-start = (f32[4,32]{1,0:T(4,128)S(1)}, f32[4,32]{1,0:T(4,128)}, u32[]{:S(2)}) copy-start(f32[4,32]{1,0:T(4,128)} %metric_ref.3) | copy-start | bytes 1540
  18.1 8.4 %copy-start.5 = (bf16[384,256]{1,0:T(8,128)(2,1)S(1)}, bf16[384,256]{1,0:T(8,128)(2,1)}, u32[]{:S(2)}) copy-start(bf16[384,256]{1,0:T(8,128)(2,1)} %constant.16.clone.forward_ref) | copy-start | bytes 589828
  18.1 0.7 %copy-start.15 = (f32[256,128]{1,0:T(8,128)}, f32[256,128]{1,0:T(8,128)S(1)}, u32[]{:S(2)}) copy-start(f32[256,128]{1,0:T(8,128)S(1)} %collective-permute-done.other_ref) | copy-start | bytes 393220
  20.5 18.0 %collective-permute-start.2 = (f32[512,128]{1,0:T(8,128)}, f32[512,128]{1,0:T(8,128)}, u32[]{:S(2)}, u32[]{:S(2)}) collective-permute-start(f32[512,128]{1,0:T(8,128)} %pair.1.refs_0_), channel_id=1, source_target_pairs={{0,64},{16,208},{32,96},{48,240},{64,128},{80,16},{96,160},{112,48... | collective-permute-start | bytes 786440 | tf_op jit(solution)/shard_map/ppermute | solution.py:482
  30.6 7.1 %copy-start.7 = (f32[512,128]{1,0:T(8,128)S(1)}, f32[512,128]{1,0:T(8,128)}, u32[]{:S(2)}) copy-start(f32[512,128]{1,0:T(8,128)} %pair.1.refs_0_) | copy-start | bytes 786436
  30.6 26.2 %all-to-all-start.1 = ((f32[16,96,128]{2,1,0:T(8,128)}), f32[16,96,128]{2,1,0:T(8,128)S(1)}, u32[]{:S(2)}, u32[]{:S(2)}) async-start(f32[16,96,128]{2,1,0:T(8,128)} %planes.1), calls=%async_computation.1 | async-start | bytes 1572864 | tf_op jit(solution)/shard_map/all_to_all | solution.py:490
  37.7 5.6 %collective-permute-start.1 = (f32[512,128]{1,0:T(8,128)S(1)}, f32[512,128]{1,0:T(8,128)S(1)}, u32[]{:S(2)}, u32[]{:S(2)}) collective-permute-start(f32[512,128]{1,0:T(8,128)S(1)} %copy-done.7), channel_id=1, source_target_pairs={{0,32},{16,240},{32,64},{48,16},{64,96},{80,48},{96,128},{112,80},... | collective-permute-start | bytes 786440 | tf_op jit(solution)/shard_map/ppermute | solution.py:481
  38.5 7.6 %collective-permute-start.3 = (f32[512,128]{1,0:T(8,128)}, f32[512,128]{1,0:T(8,128)S(1)}, u32[]{:S(2)}, u32[]{:S(2)}) collective-permute-start(f32[512,128]{1,0:T(8,128)} %collective-permute-done.2.refs_2_), channel_id=1, source_target_pairs={{0,32},{16,240},{32,64},{48,16},{64,96},{80,48},{96,128},{112,80},... | collective-permute-start | bytes 786440 | tf_op jit(solution)/shard_map/ppermute | solution.py:491
  40.1 9.2 %collective-permute-start.4 = (f32[256,128]{1,0:T(8,128)S(1)}, f32[256,128]{1,0:T(8,128)S(1)}, u32[]{:S(2)}, u32[]{:S(2)}) collective-permute-start(f32[256,128]{1,0:T(8,128)S(1)} %slice.4), channel_id=1, source_target_pairs={{0,64},{16,208},{32,96},{48,240},{64,128},{80,16},{96,160},{112,48... | collective-permute-start | bytes 393224 | tf_op jit(solution)/shard_map/ppermute | solution.py:492
  40.2 10.7 %collective-permute-start.6 = (f32[512,128]{1,0:T(8,128)}, f32[512,128]{1,0:T(8,128)S(1)}, u32[]{:S(2)}, u32[]{:S(2)}) collective-permute-start(f32[512,128]{1,0:T(8,128)} %collective-permute-done.2.refs_2_), channel_id=1, source_target_pairs={{0,16},{16,0},{32,48},{48,32},{64,80},{80,64},{96,112},{112,96},{1... | collective-permute-start | bytes 786440 | tf_op jit(solution)/shard_map/ppermute | solution.py:494
  43.2 7.7 %copy-start.8 = (f32[512,128]{1,0:T(8,128)}, f32[512,128]{1,0:T(8,128)S(1)}, u32[]{:S(2)}) copy-start(f32[512,128]{1,0:T(8,128)S(1)} %collective-permute-done.1.refs_1_) | copy-start | bytes 786436
  43.3 7.7 %collective-permute-start.5 = (f32[512,128]{1,0:T(8,128)S(1)}, f32[512,128]{1,0:T(8,128)S(1)}, u32[]{:S(2)}, u32[]{:S(2)}) collective-permute-start(f32[512,128]{1,0:T(8,128)S(1)} %collective-permute-done.1.refs_1_), channel_id=1, source_target_pairs={{0,16},{16,0},{32,48},{48,32},{64,80},{80,64},{96,112},{112,96},{1... | collective-permute-start | bytes 786440 | tf_op jit(solution)/shard_map/ppermute | solution.py:494
  46.1 4.9 %copy-start.9 = (f32[512,128]{1,0:T(8,128)}, f32[512,128]{1,0:T(8,128)S(1)}, u32[]{:S(2)}) copy-start(f32[512,128]{1,0:T(8,128)S(1)} %collective-permute-done.3.refs_3_) | copy-start | bytes 786436
  46.1 4.9 %collective-permute-start.7 = (f32[512,128]{1,0:T(8,128)S(1)}, f32[512,128]{1,0:T(8,128)S(1)}, u32[]{:S(2)}, u32[]{:S(2)}) collective-permute-start(f32[512,128]{1,0:T(8,128)S(1)} %collective-permute-done.3.refs_3_), channel_id=1, source_target_pairs={{0,16},{16,0},{32,48},{48,32},{64,80},{80,64},{96,112},{112,96},{1... | collective-permute-start | bytes 786440 | tf_op jit(solution)/shard_map/ppermute | solution.py:494
  49.3 1.6 %copy-start.13 = (f32[256,128]{1,0:T(8,128)}, f32[256,128]{1,0:T(8,128)S(1)}, u32[]{:S(2)}) copy-start(f32[256,128]{1,0:T(8,128)S(1)} %collective-permute-done.4.refs_4_) | copy-start | bytes 393220
  49.3 1.6 %collective-permute-start.8 = (f32[256,128]{1,0:T(8,128)S(1)}, f32[256,128]{1,0:T(8,128)S(1)}, u32[]{:S(2)}, u32[]{:S(2)}) collective-permute-start(f32[256,128]{1,0:T(8,128)S(1)} %collective-permute-done.4.refs_4_), channel_id=1, source_target_pairs={{0,16},{16,0},{32,48},{48,32},{64,80},{80,64},{96,112},{112,96},{1... | collective-permute-start | bytes 393224 | tf_op jit(solution)/shard_map/ppermute | solution.py:494
  50.9 0.7 %copy-start.14 = (f32[256,128]{1,0:T(8,128)}, f32[256,128]{1,0:T(8,128)S(1)}, u32[]{:S(2)}) copy-start(f32[256,128]{1,0:T(8,128)S(1)} %collective-permute-done.8.refs_8_) | copy-start | bytes 393220
  50.9 0.7 %copy-start.10 = (f32[512,128]{1,0:T(8,128)}, f32[512,128]{1,0:T(8,128)S(1)}, u32[]{:S(2)}) copy-start(f32[512,128]{1,0:T(8,128)S(1)} %collective-permute-done.6.refs_6_) | copy-start | bytes 786436
  50.9 0.9 %copy-start.11 = (f32[512,128]{1,0:T(8,128)}, f32[512,128]{1,0:T(8,128)S(1)}, u32[]{:S(2)}) copy-start(f32[512,128]{1,0:T(8,128)S(1)} %collective-permute-done.5.refs_5_) | copy-start | bytes 786436
  51.8 0.7 %copy-start.12 = (f32[512,128]{1,0:T(8,128)}, f32[512,128]{1,0:T(8,128)S(1)}, u32[]{:S(2)}) copy-start(f32[512,128]{1,0:T(8,128)S(1)} %collective-permute-done.7.refs_7_) | copy-start | bytes 786436
  56.8 0.9 %copy-start.6 = (f32[16,96,128]{2,1,0:T(8,128)}, f32[16,96,128]{2,1,0:T(8,128)S(1)}, u32[]{:S(2)}) copy-start(f32[16,96,128]{2,1,0:T(8,128)S(1)} %all-to-all-done.1.nonlinear_ref) | copy-start | bytes 2359300

commit v2 on v1

--- a/solution.py
+++ b/solution.py
@@ -96,6 +96,10 @@
     return cosine, sine, cosine.T * scale, sine.T * (2.0 / PLANES)
 
 
+def granted(mebibytes):
+    return pltpu.CompilerParams(vmem_limit_bytes=mebibytes * 1024 * 1024)
+
+
 def split(value):
     high = value.astype(BF16)
     low = (value - high.astype(F32)).astype(BF16)
@@ -121,38 +125,27 @@
     return jnp.where(lane < LANES // 2, first, second)
 
 
-def pack_kernel(field_ref, out_ref, held_ref, in_sems, out_sems):
+def pack_kernel(field_ref, out_ref, sems):
     loads = [
         pltpu.make_async_copy(
-            field_ref.at[:, pl.ds(block * LANES, LANES)], held_ref.at[block], in_sems.at[block]
+            field_ref.at[:, pl.ds(block * LANES, LANES)], out_ref.at[block], sems.at[block]
         )
-        for block in range(GROUPS)
-    ]
-    stores = [
-        pltpu.make_async_copy(held_ref.at[block], out_ref.at[block], out_sems.at[block])
         for block in range(GROUPS)
     ]
     for load in loads:
         load.start()
-    for load, store in zip(loads, stores):
+    for load in loads:
         load.wait()
-        store.start()
-    for store in stores:
-        store.wait()
 
 
 def pack(field):
-    anywhere = pl.BlockSpec(memory_space=pl.ANY)
     return pl.pallas_call(
         pack_kernel,
-        in_specs=[anywhere],
-        out_specs=anywhere,
+        in_specs=[pl.BlockSpec(memory_space=pl.ANY)],
+        out_specs=pl.BlockSpec(memory_space=VMEM),
         out_shape=jax.ShapeDtypeStruct((GROUPS, ROWS, LANES), F32),
-        scratch_shapes=[
-            pltpu.VMEM((GROUPS, ROWS, LANES), F32),
-            pltpu.SemaphoreType.DMA((GROUPS,)),
-            pltpu.SemaphoreType.DMA((GROUPS,)),
-        ],
+        scratch_shapes=[pltpu.SemaphoreType.DMA((GROUPS,))],
+        compiler_params=granted(4),
         cost_estimate=pl.CostEstimate(flops=0, bytes_accessed=1600000, transcendentals=0),
         name="pack",
     )(field)
@@ -182,6 +175,7 @@
         out_specs=pl.BlockSpec(memory_space=VMEM),
         out_shape=jax.ShapeDtypeStruct((256, LANES), F32),
         scratch_shapes=[pltpu.VMEM((256, LANES), F32)],
+        compiler_params=granted(4),
         cost_estimate=pl.CostEstimate(flops=0, bytes_accessed=8000000, transcendentals=0),
         name="traces",
     )(rotor_element, packed)
@@ -199,6 +193,7 @@
         in_specs=[whole, whole],
         out_specs=whole,
         out_shape=jax.ShapeDtypeStruct((512, LANES), F32),
+        compiler_params=granted(2),
         cost_estimate=pl.CostEstimate(flops=0, bytes_accessed=1000000, transcendentals=0),
         name="pair",
     )(mine, other)
@@ -280,6 +275,7 @@
         out_specs=pl.BlockSpec((step, ROWS, LANES), lambda i: (i, 0, 0)),
         out_shape=jax.ShapeDtypeStruct((GROUPS, ROWS, LANES), F32),
         scratch_shapes=[pltpu.SMEM((32,), jnp.int32)],
+        compiler_params=granted(8),
         cost_estimate=pl.CostEstimate(flops=2000000000, bytes_accessed=8000000, transcendentals=0),
         name="helm",
     )(metric, area, stator_element, packed, visc, weight, forward, back)
@@ -361,30 +357,46 @@
         in_specs=[pl.BlockSpec(memory_space=SMEM)] + [whole] * 6,
         out_specs=whole,
         out_shape=jax.ShapeDtypeStruct((GROUPS, ROWS, LANES), F32),
-        compiler_params=pltpu.CompilerParams(vmem_limit_bytes=48 * 1024 * 1024),
+        compiler_params=granted(20),
         cost_estimate=pl.CostEstimate(flops=3000000000, bytes_accessed=4000000, transcendentals=0),
         name="planes",
     )(metric, got, cosine, sine, cos_back, sin_back, forward)
 
 
-def penalty_kernel(source_ref, stator_ref, offset_ref, interp_ref, *refs):
-    piece_refs, refs = refs[:HELD], refs[HELD:]
-    helm_ref, out_ref, received_ref, base_ref, place_ref = refs
-    elem = lax.axis_index("elem")
+def place_kernel(stator_ref, offset_ref, interp_ref, out_ref, base_ref, place_ref):
     for edge in range(32):
         rows = pl.ds(edge * 8, 8)
         base_ref[rows, :] = interp_ref[pl.ds(pl.multiple_of(offset_ref[edge] * 8, 8), 8), :]
         place_ref[rows, :] = jnp.full((8, 256), stator_ref[edge], jnp.int32)
     lane = lax.broadcasted_iota(jnp.int32, (256, 256), 1)
-    matrix = jnp.where(place_ref[...] == lane // 8, base_ref[...], 0.0)
-    high, low = split(matrix)
-    right = jnp.concatenate([high, low, high], 0)
+    high, low = split(jnp.where(place_ref[...] == lane // 8, base_ref[...], 0.0))
+    out_ref[...] = jnp.concatenate([high, low, high], 0)
+
+
+def placing(stator_element, mortar_offset, interp):
+    scalars = pl.BlockSpec(memory_space=SMEM)
+    whole = pl.BlockSpec(memory_space=VMEM)
+    return pl.pallas_call(
+        place_kernel,
+        in_specs=[scalars, scalars, whole],
+        out_specs=whole,
+        out_shape=jax.ShapeDtypeStruct((768, 256), BF16),
+        scratch_shapes=[pltpu.VMEM((256, 256), F32), pltpu.VMEM((256, 256), jnp.int32)],
+        compiler_params=granted(4),
+        cost_estimate=pl.CostEstimate(flops=1000, bytes_accessed=1000, transcendentals=0),
+        name="placing",
+    )(stator_element, mortar_offset, interp)
+
+
+def penalty_kernel(source_ref, place_ref, *refs):
+    piece_refs, (out_ref, received_ref) = refs[:HELD], refs[HELD:]
+    elem = lax.axis_index("elem")
     core = elem % 2
     for edge in range(32):
         source = source_ref[edge]
-        owner, slot = source // 32, source % 32
-        owner_core = owner % 2
-        behind = (elem // 2 - owner // 2 + RING) % RING
+        owner, slot = lax.shift_right_logical(source, 5), source & 31
+        owner_core = owner & 1
+        behind = (elem // 2 - lax.shift_right_logical(owner, 1)) & (RING - 1)
         near = jnp.where(behind <= 4, behind, RING - behind)
         side = jnp.where(
             behind == 0, core, jnp.where(behind == 4, owner_core, jnp.where(behind < 4, 0, 1))
@@ -397,72 +409,58 @@
             at = first if index % 4 == 0 else start
             tile = jnp.where(piece == index, piece_refs[index][pl.ds(at, 8), :], tile)
         received_ref[pl.ds(edge * 8, 8), :] = tile
-    placed = dot(left_split(received_ref[...].T[:ROWS]), right)
+    out_ref[...] = dot(left_split(received_ref[...].T[:ROWS]), place_ref[...])
+
+
+def penalty(stator_source, place, pieces):
+    whole = pl.BlockSpec(memory_space=VMEM)
+    return pl.pallas_call(
+        penalty_kernel,
+        in_specs=[pl.BlockSpec(memory_space=SMEM)] + [whole] * (HELD + 1),
+        out_specs=whole,
+        out_shape=jax.ShapeDtypeStruct((ROWS, 256), F32),
+        scratch_shapes=[pltpu.VMEM((256, LANES), F32)],
+        compiler_params=granted(6),
+        cost_estimate=pl.CostEstimate(flops=1000, bytes_accessed=1000, transcendentals=0),
+        name="penalty",
+    )(stator_source, place, *pieces)
+
+
+def sum_kernel(nonlinear_ref, helm_ref, placed_ref, out_ref, done_ref, sems):
+    stores = [
+        pltpu.make_async_copy(
+            done_ref.at[block], out_ref.at[:, pl.ds(block * LANES, LANES)], sems.at[block]
+        )
+        for block in range(GROUPS)
+    ]
     lane = lax.broadcasted_iota(jnp.int32, (ROWS, LANES), 1)
     for block in range(GROUPS):
-        half = placed[:, (block // 8) * LANES : (block // 8 + 1) * LANES]
+        half = placed_ref[:, pl.ds((block // 8) * LANES, LANES)]
         start = 16 * (block % 8)
         low = pltpu.roll(half, (-start) % LANES, 1)
         high = pltpu.roll(half, (64 - 8 - start) % LANES, 1)
         value = jnp.where(lane < 8, low, jnp.where(lane // 8 == 8, high, 0.0))
-        out_ref[block] = helm_ref[block] - value
-
-
-def penalty(stator_source, stator_element, mortar_offset, interp, pieces, helm):
-    whole = pl.BlockSpec(memory_space=VMEM)
-    scalars = pl.BlockSpec(memory_space=SMEM)
-    return pl.pallas_call(
-        penalty_kernel,
-        in_specs=[scalars] * 3 + [whole] * (HELD + 2),
-        out_specs=whole,
-        out_shape=jax.ShapeDtypeStruct((GROUPS, ROWS, LANES), F32),
-        scratch_shapes=[
-            pltpu.VMEM((256, LANES), F32),
-            pltpu.VMEM((256, 256), F32),
-            pltpu.VMEM((256, 256), jnp.int32),
-        ],
-        cost_estimate=pl.CostEstimate(flops=1000, bytes_accessed=1000, transcendentals=0),
-        name="penalty",
-    )(stator_source, stator_element, mortar_offset, interp, *pieces, helm)
-
-
-def sum_kernel(nonlinear_ref, rest_ref, out_ref, in_ref, done_ref, in_sems, out_sems):
-    loads = [
-        pltpu.make_async_copy(nonlinear_ref.at[block], in_ref.at[block], in_sems.at[block])
-        for block in range(GROUPS)
-    ]
-    stores = [
-        pltpu.make_async_copy(
-            done_ref.at[block], out_ref.at[:, pl.ds(block * LANES, LANES)], out_sems.at[block]
-        )
-        for block in range(GROUPS)
-    ]
-    for load in loads:
-        load.start()
-    for block in range(GROUPS):
-        loads[block].wait()
-        done_ref[block] = -in_ref[block] - rest_ref[block]
+        done_ref[block] = value - helm_ref[block] - nonlinear_ref[block]
         stores[block].start()
     for store in stores:
         store.wait()
 
 
-def final_sum(nonlinear, rest):
-    anywhere = pl.BlockSpec(memory_space=pl.ANY)
+def final_sum(nonlinear, helm, placed):
+    whole = pl.BlockSpec(memory_space=VMEM)
     return pl.pallas_call(
         sum_kernel,
-        in_specs=[anywhere, pl.BlockSpec(memory_space=VMEM)],
-        out_specs=anywhere,
+        in_specs=[whole] * 3,
+        out_specs=pl.BlockSpec(memory_space=pl.ANY),
         out_shape=jax.ShapeDtypeStruct((ROWS, GROUPS * LANES), F32),
         scratch_shapes=[
             pltpu.VMEM((GROUPS, ROWS, LANES), F32),
-            pltpu.VMEM((GROUPS, ROWS, LANES), F32),
-            pltpu.SemaphoreType.DMA((GROUPS,)),
             pltpu.SemaphoreType.DMA((GROUPS,)),
         ],
+        compiler_params=granted(6),
         cost_estimate=pl.CostEstimate(flops=0, bytes_accessed=2400000, transcendentals=0),
         name="final_sum",
-    )(nonlinear, rest)
+    )(nonlinear, helm, placed)
 
 
 def local(vel_hat, metric, area, visc, rotor_element, stator_element, mortar_offset, stator_source):
@@ -483,17 +481,20 @@
     helm = helmholtz(
         metric, area, stator_element, packed, visc.reshape(GROUPS, LANES), weight, forward, back
     )
+    place = placing(stator_element, mortar_offset, spread)
     got, helm = lax.optimization_barrier((got, helm))
+    one, two = lax.optimization_barrier((one, two))
     advect_hat = planes(
         metric, got, as_left(cosine), as_left(sine), as_left(cos_back), as_left(sin_back), forward
     )
     nonlinear = lax.all_to_all(advect_hat, "four", 0, 0, tiled=True)
     three = lax.ppermute(two, "elem", moves(1))
     four = lax.ppermute(two[:256], "elem", moves(2))
+    four, place = lax.optimization_barrier((four, place))
     held = [one, two, three, four]
     pieces = [both] + held + [lax.ppermute(piece, "elem", ACROSS) for piece in held]
-    rest = penalty(stator_source, stator_element, mortar_offset, spread, pieces, helm)
-    return final_sum(nonlinear, rest).reshape(vel_hat.shape)
+    placed = penalty(stator_source, place, pieces)
+    return final_sum(nonlinear, helm, placed).reshape(vel_hat.shape)
 
 
 def solution(mesh):

time: 61.5 us -> 54.6 us (0.89)
  Pallas kernels: 22.7 us -> 14.1 us
  starting transfers between devices: 26.4 us -> 32 us
  waiting for transfers between devices: 7.49 us -> 3.27 us
    pallas_call x3 -> x4, Pallas kernels: 9.51 us -> 4.3 us  [the longest x1 1.32 us: penalty(): pl.pallas_call(penalty_kernel, in_specs=[pl.BlockSpec(memory_space=SMEM)]...]
    ppermute x1, starting transfers between devices: 0.8 us -> 5.65 us  [local(): one = lax.ppermute(both, 'elem', moves(1))]
    ppermute x1, starting transfers between devices: 6.02 us -> 1.18 us  [local(): two = lax.ppermute(both, 'elem', moves(2))]
    ppermute x4, starting transfers between devices: 3.19 us -> 6.52 us  [local(): lax.ppermute(piece, 'elem', ACROSS)]
    ppermute x1, waiting for transfers between devices: 3.26 us -> 0.01 us  [local(): four = lax.ppermute(two[:256], 'elem', moves(2))]
    pallas_call x1, Pallas kernels: 1.72 us -> 0.02 us  [pair(): pl.pallas_call(pair_kernel, in_specs=[whole, whole], out_specs=whole, out...]
    unnamed x32, local copies, waits for them, and re-layouts: 3.11 us -> 4.4 us
    ppermute x1, starting transfers between devices: 0.09 us -> 1.24 us  [local(): four = lax.ppermute(two[:256], 'elem', moves(2))]
  transfers between devices with their start and end apart: 11 -> 11, of which waited for: 4 -> 3; matrix products, arithmetic and copies ran while one was open for 2% -> 0% of each run, Pallas kernels for 29% -> 22%
where the time goes in v2:
time: 54.6 us; the launch traced here: 54.1 us
  starting transfers between devices  32 us (59%)
  Pallas kernels  14.1 us (26%)
  local copies, waits for them, and re-layouts  4.41 us (8%)
  waiting for transfers between devices  3.27 us (6%)
    all_to_all x1, starting transfers between devices, local(): got = lax.all_to_all(packed, 'four', 0, 0, tiled=True)  7.6 us
    all_to_all x1, starting transfers between devices, local(): nonlinear = lax.all_to_all(advect_hat, 'four', 0, 0, tiled=True)  6.94 us
    ppermute x4, starting transfers between devices, local(): lax.ppermute(piece, 'elem', ACROSS)  6.52 us
    ppermute x1, starting transfers between devices, local(): one = lax.ppermute(both, 'elem', moves(1))  5.65 us
    unnamed x32, local copies, waits for them, and re-layouts  4.4 us
    pallas_call x1, Pallas kernels, helmholtz(): pl.pallas_call(helm_kernel, grid=(GROUPS // step,), in_specs=[pl.BlockSpe...  4.01 us
    pallas_call x1, Pallas kernels, planes(): pl.pallas_call(plane_kernel, in_specs=[pl.BlockSpec(memory_space=SMEM)] +...  4 us
    ppermute x1, starting transfers between devices, local(): three = lax.ppermute(two, 'elem', moves(1))  1.84 us
  transfers between devices with their start and end apart: 11, of which 3 were waited for; matrix products, arithmetic and copies ran while one was open for 0% of the time, Pallas kernels for 22%

profile of v2, /device:TPU:1, one launch (start us, length us, event | category | flops | bytes accessed | tf_op | source)
XLA Modules:
  0.0 54.1 jit_solution(8629405132635019486)
XLA Ops:
  0.0 1.1 %copy-done = f32[3,32,2048]{2,1,0:T(8,128)S(1)} copy-done((f32[3,32,2048]{2,1,0:T(8,128)S(1)}, f32[3,32,2048]{2,1,0:T(8,128)}, u32[]{:S(2)}) %copy-start) | copy-done | bytes 786456
  1.1 1.2 %pack.1.packed_ref = f32[16,96,128]{2,1,0:T(8,128)} custom-call(f32[96,2048]{1,0:T(8,128)S(1)} %bitcast.3), custom_call_target="tpu_custom_call" | custom-call | bytes 1600000 | tf_op jit(solution)/shard_map/pack/pallas_call | solution.py:142
  2.3 0.0 copy-start.2
  2.3 7.6 %all-to-all-start = ((f32[16,96,128]{2,1,0:T(8,128)}), f32[16,96,128]{2,1,0:T(8,128)S(1)}, u32[]{:S(2)}, u32[]{:S(2)}) async-start(f32[16,96,128]{2,1,0:T(8,128)} %pack.1.packed_ref), calls=%async_computation | async-start | bytes 1572864 | tf_op jit(solution)/shard_map/all_to_all | solution.py:476
  9.9 0.0 copy-start.6
  9.9 0.0 copy-start.7
  10.0 0.0 copy-start.13
  10.0 0.0 copy-start.14
  10.0 1.8 %traces.1.mine_ref = f32[256,128]{1,0:T(8,128)S(1)} custom-call(s32[32]{0:T(128)S(1)} %copy-done.2, f32[16,96,128]{2,1,0:T(8,128)} %pack.1.packed_ref), custom_call_target="tpu_custom_call" | custom-call | bytes 8000000 | tf_op jit(solution)/shard_map/traces/pallas_call | solution.py:172
  11.8 0.0 copy-start.3
  11.8 0.0 copy-start.8
  11.8 0.0 copy-start.15
  11.8 1.0 %collective-permute-start = (f32[256,128]{1,0:T(8,128)S(1)}, f32[256,128]{1,0:T(8,128)S(1)}, u32[]{:S(2)}, u32[]{:S(2)}) collective-permute-start(f32[256,128]{1,0:T(8,128)S(1)} %traces.1.mine_ref), channel_id=1, source_target_pairs={{0,16},{16,0},{32,48},{48,32},{64,80},{80,64},{96,112},{112,96},{1... | collective-permute-start | bytes 393224 | tf_op jit(solution)/shard_map/ppermute | solution.py:478
  12.8 0.0 copy-done.7
  12.9 0.0 copy-start.9
  12.9 4.0 %helm.1.helm_ref = f32[16,96,128]{2,1,0:T(8,128)S(1)} custom-call(f32[4,32]{1,0:T(4,128)S(1)} %copy-done.7, f32[32]{0:T(128)S(1)} %copy-done.8, s32[32]{0:T(128)S(1)} %copy-done.3, f32[16,96,128]{2,1,0:T(8,128)} %pack.1.packed_ref, f32[16,128]{1,0:T(8,128)S(1)} %bitcast.4, f32[1,128]{1,0:T(1,128)S(1)} %copy-done.15, bf16[384,256]{1,0:T(8,128)(2,1)S(1)} %copy-done.13, ...), custom_call_target="tpu_custom_call" | custom-call | flops 2000000000 | bytes 8000000 | tf_op jit(solution)/shard_map/helm/pallas_call | solution.py:262
  16.9 0.0 collective-permute-done.other_ref
  17.0 5.7 %collective-permute-start.1 = (f32[512,128]{1,0:T(8,128)S(1)}, f32[512,128]{1,0:T(8,128)S(1)}, u32[]{:S(2)}, u32[]{:S(2)}) collective-permute-start(f32[512,128]{1,0:T(8,128)S(1)} %pair.1.refs_0_), channel_id=1, source_target_pairs={{0,32},{16,240},{32,64},{48,16},{64,96},{80,48},{96,128},{112,80},... | collective-permute-start | bytes 786440 | tf_op jit(solution)/shard_map/ppermute | solution.py:479
  22.6 1.2 %collective-permute-start.2 = (f32[512,128]{1,0:T(8,128)S(1)}, f32[512,128]{1,0:T(8,128)S(1)}, u32[]{:S(2)}, u32[]{:S(2)}) collective-permute-start(f32[512,128]{1,0:T(8,128)S(1)} %pair.1.refs_0_), channel_id=1, source_target_pairs={{0,64},{16,208},{32,96},{48,240},{64,128},{80,16},{96,160},{112,48... | collective-permute-start | bytes 786440 | tf_op jit(solution)/shard_map/ppermute | solution.py:480
  23.8 0.0 all-to-all-done.got_ref
  23.8 0.0 copy-done.9
  23.8 1.1 %copy-done.10 = bf16[384,768]{1,0:T(8,128)(2,1)S(1)} copy-done((bf16[384,768]{1,0:T(8,128)(2,1)S(1)}, bf16[384,768]{1,0:T(8,128)(2,1)}, u32[]{:S(2)}) %copy-start.10) | copy-done | bytes 589848
  24.9 1.1 %copy-done.11 = bf16[256,1152]{1,0:T(8,128)(2,1)S(1)} copy-done((bf16[256,1152]{1,0:T(8,128)(2,1)S(1)}, bf16[256,1152]{1,0:T(8,128)(2,1)}, u32[]{:S(2)}) %copy-start.11) | copy-done | bytes 589848
  25.9 1.1 %copy-done.12 = bf16[256,1152]{1,0:T(8,128)(2,1)S(1)} copy-done((bf16[256,1152]{1,0:T(8,128)(2,1)S(1)}, bf16[256,1152]{1,0:T(8,128)(2,1)}, u32[]{:S(2)}) %copy-start.12) | copy-done | bytes 589848
  27.0 4.0 %planes.1 = f32[16,96,128]{2,1,0:T(8,128)} custom-call(f32[4,32]{1,0:T(4,128)S(1)} %copy-done.7, f32[16,96,128]{2,1,0:T(8,128)S(1)} %all-to-all-done.got_ref, bf16[384,768]{1,0:T(8,128)(2,1)S(1)} %copy-done.9, bf16[384,768]{1,0:T(8,128)(2,1)S(1)} %copy-done.10, bf16[256,1152]{1,0:T(8,128)(2,1)S(1)} %copy-done.11, bf16[256,1152]{1,0:T(8,128)(2,1)S(1)} %copy-done.12, ...), custom_call_target="tpu_custom_call" | custom-call | flops 3000000000 | bytes 4000000 | tf_op jit(solution)/shard_map/planes/pallas_call | solution.py:355
  31.0 6.9 %all-to-all-start.1 = ((f32[16,96,128]{2,1,0:T(8,128)}), f32[16,96,128]{2,1,0:T(8,128)S(1)}, u32[]{:S(2)}, u32[]{:S(2)}) async-start(f32[16,96,128]{2,1,0:T(8,128)} %planes.1), calls=%async_computation.1 | async-start | bytes 1572864 | tf_op jit(solution)/shard_map/all_to_all | solution.py:490
  37.9 0.0 copy-start.1
  37.9 0.0 copy-start.4
  38.0 0.0 collective-permute-done.1.refs_1_
  38.0 0.0 collective-permute-done.2.refs_2_
  38.0 1.8 %collective-permute-start.4 = (f32[512,128]{1,0:T(8,128)S(1)}, f32[512,128]{1,0:T(8,128)S(1)}, u32[]{:S(2)}, u32[]{:S(2)}) collective-permute-start(f32[512,128]{1,0:T(8,128)S(1)} %collective-permute-done.2.refs_2_), channel_id=1, source_target_pairs={{0,32},{16,240},{32,64},{48,16},{64,96},{80,48},{96,128},{112,80},... | collective-permute-start | bytes 786440 | tf_op jit(solution)/shard_map/ppermute | solution.py:491
  39.8 0.0 copy-start.5
  39.8 1.2 %collective-permute-start.3 = (f32[256,128]{1,0:T(8,128)S(1)}, f32[256,128]{1,0:T(8,128)S(1)}, u32[]{:S(2)}, u32[]{:S(2)}) collective-permute-start(f32[256,128]{1,0:T(8,128)S(1)} %slice.3), channel_id=1, source_target_pairs={{0,64},{16,208},{32,96},{48,240},{64,128},{80,16},{96,160},{112,48... | collective-permute-start | bytes 393224 | tf_op jit(solution)/shard_map/ppermute | solution.py:492
  41.1 0.9 %collective-permute-start.6 = (f32[512,128]{1,0:T(8,128)S(1)}, f32[512,128]{1,0:T(8,128)S(1)}, u32[]{:S(2)}, u32[]{:S(2)}) collective-permute-start(f32[512,128]{1,0:T(8,128)S(1)} %collective-permute-done.2.refs_2_), channel_id=1, source_target_pairs={{0,16},{16,0},{32,48},{48,32},{64,80},{80,64},{96,112},{112,96},{1... | collective-permute-start | bytes 786440 | tf_op jit(solution)/shard_map/ppermute | solution.py:495
  42.0 0.0 collective-permute-start.5
  42.0 1.7 %collective-permute-done.4.refs_3_ = f32[512,128]{1,0:T(8,128)S(1)} collective-permute-done((f32[512,128]{1,0:T(8,128)S(1)}, f32[512,128]{1,0:T(8,128)S(1)}, u32[]{:S(2)}, u32[]{:S(2)}) %collective-permute-start.4) | collective-permute-done | bytes 262176 | tf_op jit(solution)/shard_map/ppermute | solution.py:491
  43.7 2.9 %collective-permute-start.7 = (f32[512,128]{1,0:T(8,128)S(1)}, f32[512,128]{1,0:T(8,128)S(1)}, u32[]{:S(2)}, u32[]{:S(2)}) collective-permute-start(f32[512,128]{1,0:T(8,128)S(1)} %collective-permute-done.4.refs_3_), channel_id=1, source_target_pairs={{0,16},{16,0},{32,48},{48,32},{64,80},{80,64},{96,112},{112,96},{1... | collective-permute-start | bytes 786440 | tf_op jit(solution)/shard_map/ppermute | solution.py:495
  46.5 0.6 %placing.1.place_ref = bf16[768,256]{1,0:T(8,128)(2,1)S(1)} custom-call(s32[32]{0:T(128)S(1)} %copy-done.3, s32[32]{0:T(128)S(1)} %copy-done.4, f32[64,256]{1,0:T(8,128)S(1)} %copy-done.1), custom_call_target="tpu_custom_call" | custom-call | flops 1000 | bytes 1000 | tf_op jit(solution)/shard_map/placing/pallas_call | solution.py:379
  47.2 0.0 collective-permute-done.3.refs_4_
  47.2 2.8 %collective-permute-start.8 = (f32[256,128]{1,0:T(8,128)S(1)}, f32[256,128]{1,0:T(8,128)S(1)}, u32[]{:S(2)}, u32[]{:S(2)}) collective-permute-start(f32[256,128]{1,0:T(8,128)S(1)} %collective-permute-done.3.refs_4_), channel_id=1, source_target_pairs={{0,16},{16,0},{32,48},{48,32},{64,80},{80,64},{96,112},{112,96},{1... | collective-permute-start | bytes 393224 | tf_op jit(solution)/shard_map/ppermute | solution.py:495
  49.9 1.0 %collective-permute-done.8.refs_8_ = f32[256,128]{1,0:T(8,128)S(1)} collective-permute-done((f32[256,128]{1,0:T(8,128)S(1)}, f32[256,128]{1,0:T(8,128)S(1)}, u32[]{:S(2)}, u32[]{:S(2)}) %collective-permute-start.8) | collective-permute-done | bytes 131104 | tf_op jit(solution)/shard_map/ppermute | solution.py:495
  50.9 0.0 collective-permute-done.6.refs_6_
  50.9 0.0 collective-permute-done.5.refs_5_
  50.9 0.0 collective-permute-done.7.refs_7_
  50.9 0.0 copy-done.5
  51.0 1.3 %penalty.1.placed_ref = f32[96,256]{1,0:T(8,128)S(1)} custom-call(s32[32]{0:T(128)S(1)} %copy-done.5, bf16[768,256]{1,0:T(8,128)(2,1)S(1)} %placing.1.place_ref, f32[512,128]{1,0:T(8,128)S(1)} %pair.1.refs_0_, f32[512,128]{1,0:T(8,128)S(1)} %collective-permute-done.1.refs_1_, f32[512,128]{1,0:T(8,128)S(1)} %collective-permute-done.2.refs_2_, ...), custom_call_target="tpu_custom_call" | custom-call | flops 1000 | bytes 1000 | tf_op jit(solution)/shard_map/penalty/pallas_call | solution.py:417
  52.3 0.6 %all-to-all-done.1.nonlinear_ref = f32[16,96,128]{2,1,0:T(8,128)S(1)} async-done(((f32[16,96,128]{2,1,0:T(8,128)}), f32[16,96,128]{2,1,0:T(8,128)S(1)}, u32[]{:S(2)}, u32[]{:S(2)}) %all-to-all-start.1) | async-done | bytes 786464 | tf_op jit(solution)/shard_map/all_to_all | solution.py:490
  52.8 1.2 %final_sum.1 = f32[96,2048]{1,0:T(8,128)} custom-call(f32[16,96,128]{2,1,0:T(8,128)S(1)} %all-to-all-done.1.nonlinear_ref, f32[16,96,128]{2,1,0:T(8,128)S(1)} %helm.1.helm_ref, f32[96,256]{1,0:T(8,128)S(1)} %penalty.1.placed_ref), custom_call_target="tpu_custom_call" | custom-call | bytes 2400000 | tf_op jit(solution)/shard_map/final_sum/pallas_call | solution.py:451
  (15 shorter events, 0.1 us)
Async XLA Ops:
  0.0 1.1 %copy-start = (f32[3,32,2048]{2,1,0:T(8,128)S(1)}, f32[3,32,2048]{2,1,0:T(8,128)}, u32[]{:S(2)}) copy-start(f32[3,32,2048]{2,1,0:T(8,128)} %param.16) | copy-start | bytes 2359300
  2.3 7.6 %copy-start.2 = (s32[32]{0:T(128)S(1)}, s32[32]{0:T(128)}, u32[]{:S(2)}) copy-start(s32[32]{0:T(128)} %rotor_ref.1) | copy-start | bytes 388
  2.3 21.5 %all-to-all-start = ((f32[16,96,128]{2,1,0:T(8,128)}), f32[16,96,128]{2,1,0:T(8,128)S(1)}, u32[]{:S(2)}, u32[]{:S(2)}) async-start(f32[16,96,128]{2,1,0:T(8,128)} %pack.1.packed_ref), calls=%async_computation | async-start | bytes 1572864 | tf_op jit(solution)/shard_map/all_to_all | solution.py:476
  9.9 2.9 %copy-start.6 = (f32[2048]{0:T(1024)S(1)}, f32[2048]{0:T(1024)}, u32[]{:S(2)}) copy-start(f32[2048]{0:T(1024)} %param.19) | copy-start | bytes 24580
  9.9 2.9 %copy-start.7 = (f32[4,32]{1,0:T(4,128)S(1)}, f32[4,32]{1,0:T(4,128)}, u32[]{:S(2)}) copy-start(f32[4,32]{1,0:T(4,128)} %metric_ref.3) | copy-start | bytes 1540
  10.0 2.9 %copy-start.13 = (bf16[384,256]{1,0:T(8,128)(2,1)S(1)}, bf16[384,256]{1,0:T(8,128)(2,1)}, u32[]{:S(2)}) copy-start(bf16[384,256]{1,0:T(8,128)(2,1)} %constant.16.clone.forward_ref) | copy-start | bytes 589828
  10.0 2.9 %copy-start.14 = (bf16[768,128]{1,0:T(8,128)(2,1)S(1)}, bf16[768,128]{1,0:T(8,128)(2,1)}, u32[]{:S(2)}) copy-start(bf16[768,128]{1,0:T(8,128)(2,1)} %constant.17.clone.back_ref) | copy-start | bytes 589828
  11.8 1.1 %copy-start.3 = (s32[32]{0:T(128)S(1)}, s32[32]{0:T(128)}, u32[]{:S(2)}) copy-start(s32[32]{0:T(128)} %stator_ref.3) | copy-start | bytes 388
  11.8 1.1 %copy-start.8 = (f32[32]{0:T(128)S(1)}, f32[32]{0:T(128)}, u32[]{:S(2)}) copy-start(f32[32]{0:T(128)} %area_ref.1) | copy-start | bytes 388
  11.8 1.1 %copy-start.15 = (f32[1,128]{1,0:T(1,128)S(1)}, f32[1,128]{1,0:T(1,128)}, u32[]{:S(2)}) copy-start(f32[1,128]{1,0:T(1,128)} %constant.18.clone.weight_ref) | copy-start | bytes 1540
  11.8 5.1 %collective-permute-start = (f32[256,128]{1,0:T(8,128)S(1)}, f32[256,128]{1,0:T(8,128)S(1)}, u32[]{:S(2)}, u32[]{:S(2)}) collective-permute-start(f32[256,128]{1,0:T(8,128)S(1)} %traces.1.mine_ref), channel_id=1, source_target_pairs={{0,16},{16,0},{32,48},{48,32},{64,80},{80,64},{96,112},{112,96},{1... | collective-permute-start | bytes 393224 | tf_op jit(solution)/shard_map/ppermute | solution.py:478
  12.9 10.9 %copy-start.9 = (bf16[384,768]{1,0:T(8,128)(2,1)S(1)}, bf16[384,768]{1,0:T(8,128)(2,1)}, u32[]{:S(2)}) copy-start(bf16[384,768]{1,0:T(8,128)(2,1)} %constant.20.clone.cos_ref) | copy-start | bytes 1769476
  17.0 21.0 %collective-permute-start.1 = (f32[512,128]{1,0:T(8,128)S(1)}, f32[512,128]{1,0:T(8,128)S(1)}, u32[]{:S(2)}, u32[]{:S(2)}) collective-permute-start(f32[512,128]{1,0:T(8,128)S(1)} %pair.1.refs_0_), channel_id=1, source_target_pairs={{0,32},{16,240},{32,64},{48,16},{64,96},{80,48},{96,128},{112,80},... | collective-permute-start | bytes 786440 | tf_op jit(solution)/shard_map/ppermute | solution.py:479
  22.6 15.4 %collective-permute-start.2 = (f32[512,128]{1,0:T(8,128)S(1)}, f32[512,128]{1,0:T(8,128)S(1)}, u32[]{:S(2)}, u32[]{:S(2)}) collective-permute-start(f32[512,128]{1,0:T(8,128)S(1)} %pair.1.refs_0_), channel_id=1, source_target_pairs={{0,64},{16,208},{32,96},{48,240},{64,128},{80,16},{96,160},{112,48... | collective-permute-start | bytes 786440 | tf_op jit(solution)/shard_map/ppermute | solution.py:480
  23.8 1.1 %copy-start.10 = (bf16[384,768]{1,0:T(8,128)(2,1)S(1)}, bf16[384,768]{1,0:T(8,128)(2,1)}, u32[]{:S(2)}) copy-start(bf16[384,768]{1,0:T(8,128)(2,1)} %constant.21.clone.sin_ref) | copy-start | bytes 1769476
  24.9 1.1 %copy-start.11 = (bf16[256,1152]{1,0:T(8,128)(2,1)S(1)}, bf16[256,1152]{1,0:T(8,128)(2,1)}, u32[]{:S(2)}) copy-start(bf16[256,1152]{1,0:T(8,128)(2,1)} %constant.22.clone.cos_back_ref) | copy-start | bytes 1769476
  25.9 1.1 %copy-start.12 = (bf16[256,1152]{1,0:T(8,128)(2,1)S(1)}, bf16[256,1152]{1,0:T(8,128)(2,1)}, u32[]{:S(2)}) copy-start(bf16[256,1152]{1,0:T(8,128)(2,1)} %constant.23.clone.sin_back_ref) | copy-start | bytes 1769476
  31.0 21.9 %all-to-all-start.1 = ((f32[16,96,128]{2,1,0:T(8,128)}), f32[16,96,128]{2,1,0:T(8,128)S(1)}, u32[]{:S(2)}, u32[]{:S(2)}) async-start(f32[16,96,128]{2,1,0:T(8,128)} %planes.1), calls=%async_computation.1 | async-start | bytes 1572864 | tf_op jit(solution)/shard_map/all_to_all | solution.py:490
  37.9 8.6 %copy-start.1 = (f32[64,256]{1,0:T(8,128)S(1)}, f32[64,256]{1,0:T(8,128)}, u32[]{:S(2)}) copy-start(f32[64,256]{1,0:T(8,128)} %constant.19.clone.interp_ref) | copy-start | bytes 196612
  37.9 8.6 %copy-start.4 = (s32[32]{0:T(128)S(1)}, s32[32]{0:T(128)}, u32[]{:S(2)}) copy-start(s32[32]{0:T(128)} %offset_ref.1) | copy-start | bytes 388
  38.0 5.7 %collective-permute-start.4 = (f32[512,128]{1,0:T(8,128)S(1)}, f32[512,128]{1,0:T(8,128)S(1)}, u32[]{:S(2)}, u32[]{:S(2)}) collective-permute-start(f32[512,128]{1,0:T(8,128)S(1)} %collective-permute-done.2.refs_2_), channel_id=1, source_target_pairs={{0,32},{16,240},{32,64},{48,16},{64,96},{80,48},{96,128},{112,80},... | collective-permute-start | bytes 786440 | tf_op jit(solution)/shard_map/ppermute | solution.py:491
  39.8 11.1 %copy-start.5 = (s32[32]{0:T(128)S(1)}, s32[32]{0:T(128)}, u32[]{:S(2)}) copy-start(s32[32]{0:T(128)} %source_ref.1) | copy-start | bytes 388
  39.8 7.3 %collective-permute-start.3 = (f32[256,128]{1,0:T(8,128)S(1)}, f32[256,128]{1,0:T(8,128)S(1)}, u32[]{:S(2)}, u32[]{:S(2)}) collective-permute-start(f32[256,128]{1,0:T(8,128)S(1)} %slice.3), channel_id=1, source_target_pairs={{0,64},{16,208},{32,96},{48,240},{64,128},{80,16},{96,160},{112,48... | collective-permute-start | bytes 393224 | tf_op jit(solution)/shard_map/ppermute | solution.py:492
  41.1 9.8 %collective-permute-start.6 = (f32[512,128]{1,0:T(8,128)S(1)}, f32[512,128]{1,0:T(8,128)S(1)}, u32[]{:S(2)}, u32[]{:S(2)}) collective-permute-start(f32[512,128]{1,0:T(8,128)S(1)} %collective-permute-done.2.refs_2_), channel_id=1, source_target_pairs={{0,16},{16,0},{32,48},{48,32},{64,80},{80,64},{96,112},{112,96},{1... | collective-permute-start | bytes 786440 | tf_op jit(solution)/shard_map/ppermute | solution.py:495
  42.0 9.0 %collective-permute-start.5 = (f32[512,128]{1,0:T(8,128)S(1)}, f32[512,128]{1,0:T(8,128)S(1)}, u32[]{:S(2)}, u32[]{:S(2)}) collective-permute-start(f32[512,128]{1,0:T(8,128)S(1)} %collective-permute-done.1.refs_1_), channel_id=1, source_target_pairs={{0,16},{16,0},{32,48},{48,32},{64,80},{80,64},{96,112},{112,96},{1... | collective-permute-start | bytes 786440 | tf_op jit(solution)/shard_map/ppermute | solution.py:495
  43.7 7.3 %collective-permute-start.7 = (f32[512,128]{1,0:T(8,128)S(1)}, f32[512,128]{1,0:T(8,128)S(1)}, u32[]{:S(2)}, u32[]{:S(2)}) collective-permute-start(f32[512,128]{1,0:T(8,128)S(1)} %collective-permute-done.4.refs_3_), channel_id=1, source_target_pairs={{0,16},{16,0},{32,48},{48,32},{64,80},{80,64},{96,112},{112,96},{1... | collective-permute-start | bytes 786440 | tf_op jit(solution)/shard_map/ppermute | solution.py:495
  47.2 3.8 %collective-permute-start.8 = (f32[256,128]{1,0:T(8,128)S(1)}, f32[256,128]{1,0:T(8,128)S(1)}, u32[]{:S(2)}, u32[]{:S(2)}) collective-permute-start(f32[256,128]{1,0:T(8,128)S(1)} %collective-permute-done.3.refs_4_), channel_id=1, source_target_pairs={{0,16},{16,0},{32,48},{48,32},{64,80},{80,64},{96,112},{112,96},{1... | collective-permute-start | bytes 393224 | tf_op jit(solution)/shard_map/ppermute | solution.py:495

commit v3 on v2

--- a/solution.py
+++ b/solution.py
@@ -76,24 +76,18 @@
     return high, low
 
 
-def as_left(table):
-    high, low = two_parts(table)
-    return jnp.asarray(np.concatenate([high, low, high], 1))
-
-
 def as_right(table):
     high, low = two_parts(table)
     return jnp.asarray(np.concatenate([high, low, high], 0))
 
 
-def span_tables():
-    plane = np.arange(HALF)[:, None]
-    number = np.arange(PAIRS)[None, :]
-    angle = 2.0 * np.pi * ((plane * number) % PLANES) / PLANES
-    cosine, sine = np.cos(angle), np.sin(angle)
-    scale = np.full((PAIRS, 1), 2.0 / PLANES)
-    scale[0] = 1.0 / PLANES
-    return cosine, sine, cosine.T * scale, sine.T * (2.0 / PLANES)
+def span_factors():
+    other = np.arange(HALF)[None, :]
+    factors = []
+    for own in (16 * np.arange(HALF // 16)[:, None], np.arange(16)[:, None]):
+        angle = 2.0 * np.pi * ((own * other) % PLANES) / PLANES
+        factors += [jnp.asarray(np.cos(angle), F32), jnp.asarray(np.sin(angle), F32)]
+    return factors
 
 
 def granted(mebibytes):
@@ -115,6 +109,10 @@
     return jnp.concatenate([high, high, low], -1)
 
 
+def twice_high(table):
+    return jnp.concatenate([table, table[:, : table.shape[1] // 2]], 1)
+
+
 def right_split(value):
     high, low = split(value)
     return jnp.concatenate([high, high, low], 0)
@@ -125,27 +123,20 @@
     return jnp.where(lane < LANES // 2, first, second)
 
 
-def pack_kernel(field_ref, out_ref, sems):
-    loads = [
-        pltpu.make_async_copy(
-            field_ref.at[:, pl.ds(block * LANES, LANES)], out_ref.at[block], sems.at[block]
-        )
-        for block in range(GROUPS)
-    ]
-    for load in loads:
-        load.start()
-    for load in loads:
-        load.wait()
+def pack_kernel(field_ref, out_ref):
+    for block in range(out_ref.shape[0]):
+        out_ref[block] = field_ref[:, pl.ds(block * LANES, LANES)]
 
 
 def pack(field):
+    step = 8
     return pl.pallas_call(
         pack_kernel,
-        in_specs=[pl.BlockSpec(memory_space=pl.ANY)],
-        out_specs=pl.BlockSpec(memory_space=VMEM),
+        grid=(GROUPS // step,),
+        in_specs=[pl.BlockSpec((ROWS, step * LANES), lambda i: (0, i))],
+        out_specs=pl.BlockSpec((step, ROWS, LANES), lambda i: (i, 0, 0)),
         out_shape=jax.ShapeDtypeStruct((GROUPS, ROWS, LANES), F32),
-        scratch_shapes=[pltpu.SemaphoreType.DMA((GROUPS,))],
-        compiler_params=granted(4),
+        compiler_params=granted(60),
         cost_estimate=pl.CostEstimate(flops=0, bytes_accessed=1600000, transcendentals=0),
         name="pack",
     )(field)
@@ -281,9 +272,38 @@
     )(metric, area, stator_element, packed, visc, weight, forward, back)
 
 
-def plane_kernel(
-    metric_ref, got_ref, cos_ref, sin_ref, cos_back_ref, sin_back_ref, forward_ref, out_ref
-):
+def table_kernel(cos_far_ref, sin_far_ref, cos_near_ref, sin_near_ref, out_ref):
+    row = lax.broadcasted_iota(jnp.int32, (16, HALF), 0)
+    for back, count, width in ((False, HALF, PAIRS), (True, PAIRS, HALF)):
+        near_cos, near_sin = cos_near_ref[:, pl.ds(0, width)], sin_near_ref[:, pl.ds(0, width)]
+        for step in range(count // 16):
+            far_cos = cos_far_ref[pl.ds(step, 1), pl.ds(0, width)]
+            far_sin = sin_far_ref[pl.ds(step, 1), pl.ds(0, width)]
+            cosine = far_cos * near_cos - far_sin * near_sin
+            sine = far_sin * near_cos + far_cos * near_sin
+            if back:
+                half = (row == 0) & (step == 0)
+                cosine = jnp.where(half, 1.0 / PLANES, 2.0 / PLANES) * cosine
+                sine = (2.0 / PLANES) * sine
+            rows = pl.ds((HALF if back else 0) + step * 16, 16)
+            for index, part in enumerate(split(cosine) + split(sine)):
+                out_ref[rows, pl.ds(index * width, width)] = part
+
+
+def tables():
+    whole = pl.BlockSpec(memory_space=VMEM)
+    return pl.pallas_call(
+        table_kernel,
+        in_specs=[whole] * 4,
+        out_specs=whole,
+        out_shape=VMEM((HALF + PAIRS, 4 * HALF), BF16),
+        compiler_params=granted(4),
+        cost_estimate=pl.CostEstimate(flops=1000, bytes_accessed=1000, transcendentals=0),
+        name="tables",
+    )(*span_factors())
+
+
+def plane_kernel(metric_ref, got_ref, table_ref, forward_ref, out_ref, done_ref, sems):
     pair = lax.axis_index("four") * 2
     rx, ry, sx, sy = [
         lane_scalars(metric_ref[i, pair], metric_ref[i, pair + 1]) for i in range(4)
@@ -304,8 +324,8 @@
     last_cos = [odd[0:1] for odd in odds]
     even_all = jnp.concatenate(evens + evens_z, 1)
     odd_all = jnp.concatenate(odds + odds_z, 1)
-    cos_part = dot(cos_ref[...], right_split(even_all))
-    sin_part = dot(sin_ref[...], right_split(odd_all))
+    cos_part = dot(twice_high(table_ref[pl.ds(0, HALF), pl.ds(0, 2 * PAIRS)]), right_split(even_all))
+    sin_part = dot(twice_high(table_ref[pl.ds(0, HALF), pl.ds(2 * PAIRS, 2 * PAIRS)]), right_split(odd_all))
     plus, minus = [], []
     for index in range(6):
         lanes = slice(index * LANES, (index + 1) * LANES)
@@ -317,50 +337,65 @@
         plus.append(cos_here + sin_here)
         minus.append(jnp.where(is_first, middle, cos_here - sin_here))
 
-    def advect(values):
-        along_xi = values[0] * rx + values[1] * ry
-        along_eta = values[0] * sx + values[1] * sy
-        results = []
-        for component in range(3):
-            grads = dot(left_split(values[component]), forward_ref[...])
-            results.append(
-                along_xi * grads[:, :LANES]
-                + along_eta * grads[:, LANES:]
-                + values[2] * values[3 + component]
+    speeds = [
+        (values[0] * rx + values[1] * ry, values[0] * sx + values[1] * sy, values)
+        for values in (plus, minus)
+    ]
+    cos_back, sin_back = [
+        twice_high(table_ref[pl.ds(HALF, PAIRS), pl.ds(start, 2 * HALF)]) for start in (0, 2 * HALF)
+    ]
+    scale = jnp.where(number == 0, 1.0 / PLANES, 2.0 / PLANES).astype(F32)
+    stores = []
+    for index, components in enumerate(((0, 1), (2,))):
+        even_sum, odd_sum, middles = [], [], []
+        for component in components:
+            both = []
+            for along_xi, along_eta, values in speeds:
+                grads = dot(left_split(values[component]), forward_ref[...])
+                both.append(
+                    along_xi * grads[:, :LANES]
+                    + along_eta * grads[:, LANES:]
+                    + values[2] * values[3 + component]
+                )
+            middles.append(both[1][0:1])
+            mirrored = jnp.where(is_first, 0.0, both[1])
+            even_sum.append(both[0] + mirrored)
+            odd_sum.append(both[0] - mirrored)
+        even_out = dot(cos_back, right_split(jnp.concatenate(even_sum, 1)))
+        odd_out = dot(sin_back, right_split(jnp.concatenate(odd_sum, 1)))
+        for i, component in enumerate(components):
+            lanes = slice(i * LANES, (i + 1) * LANES)
+            even_here = even_out[:, lanes] + (scale * sign) * middles[i]
+            last = (2.0 / PLANES) * (
+                jnp.sum(third * even_sum[i], 0, keepdims=True) + middles[i]
             )
-        return results
-
-    ahead, mirrored = advect(plus), advect(minus)
-    middles = [value[0:1] for value in mirrored]
-    mirrored = [jnp.where(is_first, 0.0, value) for value in mirrored]
-    even_sum = [a + b for a, b in zip(ahead, mirrored)]
-    odd_sum = [a - b for a, b in zip(ahead, mirrored)]
-    even_out = dot(cos_back_ref[...], right_split(jnp.concatenate(even_sum, 1)))
-    odd_out = dot(sin_back_ref[...], right_split(jnp.concatenate(odd_sum, 1)))
-    scale = jnp.where(number == 0, 1.0 / PLANES, 2.0 / PLANES).astype(F32)
-    for component in range(3):
-        lanes = slice(component * LANES, (component + 1) * LANES)
-        even_here = even_out[:, lanes] + (scale * sign) * middles[component]
-        last = (2.0 / PLANES) * (
-            jnp.sum(third * even_sum[component], 0, keepdims=True) + middles[component]
-        )
-        odd_here = jnp.where(number == 0, last, odd_out[:, lanes])
-        start = component * 32
-        out_ref[:, pl.ds(start, 16, stride=2), :] = even_here.reshape(GROUPS, 16, LANES)
-        out_ref[:, pl.ds(start + 1, 16, stride=2), :] = odd_here.reshape(GROUPS, 16, LANES)
-
-
-def planes(metric, got, cosine, sine, cos_back, sin_back, forward):
+            odd_here = jnp.where(number == 0, last, odd_out[:, lanes])
+            start = component * 32
+            done_ref[:, pl.ds(start, 16, stride=2), :] = even_here.reshape(GROUPS, 16, LANES)
+            done_ref[:, pl.ds(start + 1, 16, stride=2), :] = odd_here.reshape(GROUPS, 16, LANES)
+        rows = pl.ds(components[0] * 32, len(components) * 32)
+        store = pltpu.make_async_copy(done_ref.at[:, rows], out_ref.at[:, rows], sems.at[index])
+        store.start()
+        stores.append(store)
+    for store in stores:
+        store.wait()
+
+
+def planes(metric, got, tables, forward):
     whole = pl.BlockSpec(memory_space=VMEM)
     return pl.pallas_call(
         plane_kernel,
-        in_specs=[pl.BlockSpec(memory_space=SMEM)] + [whole] * 6,
-        out_specs=whole,
+        in_specs=[pl.BlockSpec(memory_space=SMEM)] + [whole] * 3,
+        out_specs=pl.BlockSpec(memory_space=pl.ANY),
         out_shape=jax.ShapeDtypeStruct((GROUPS, ROWS, LANES), F32),
+        scratch_shapes=[
+            pltpu.VMEM((GROUPS, ROWS, LANES), F32),
+            pltpu.SemaphoreType.DMA((2,)),
+        ],
         compiler_params=granted(20),
         cost_estimate=pl.CostEstimate(flops=3000000000, bytes_accessed=4000000, transcendentals=0),
         name="planes",
-    )(metric, got, cosine, sine, cos_back, sin_back, forward)
+    )(metric, got, tables, forward)
 
 
 def place_kernel(stator_ref, offset_ref, interp_ref, out_ref, base_ref, place_ref):
@@ -465,7 +500,6 @@
 
 def local(vel_hat, metric, area, visc, rotor_element, stator_element, mortar_offset, stator_source):
     along_xi, along_eta, node_weight, interp = element_tables()
-    cosine, sine, cos_back, sin_back = span_tables()
     forward = as_right(np.concatenate([along_xi.T, along_eta.T], 1))
     back = as_right(np.concatenate([along_xi, along_eta], 0))
     weight = jnp.asarray(np.tile(node_weight, 2)[None, :], F32)
@@ -477,20 +511,18 @@
     mine = traces(rotor_element, packed)
     both = pair(mine, lax.ppermute(mine, "elem", ACROSS))
     one = lax.ppermute(both, "elem", moves(1))
-    two = lax.ppermute(both, "elem", moves(2))
+    three = lax.ppermute(both, "elem", moves(3))
     helm = helmholtz(
         metric, area, stator_element, packed, visc.reshape(GROUPS, LANES), weight, forward, back
     )
     place = placing(stator_element, mortar_offset, spread)
-    got, helm = lax.optimization_barrier((got, helm))
-    one, two = lax.optimization_barrier((one, two))
-    advect_hat = planes(
-        metric, got, as_left(cosine), as_left(sine), as_left(cos_back), as_left(sin_back), forward
-    )
+    table = tables()
+    got, helm, table = lax.optimization_barrier((got, helm, table))
+    one, three, place = lax.optimization_barrier((one, three, place))
+    advect_hat = planes(metric, got, table, forward)
     nonlinear = lax.all_to_all(advect_hat, "four", 0, 0, tiled=True)
-    three = lax.ppermute(two, "elem", moves(1))
-    four = lax.ppermute(two[:256], "elem", moves(2))
-    four, place = lax.optimization_barrier((four, place))
+    two = lax.ppermute(one, "elem", moves(1))
+    four = lax.ppermute(three[:256], "elem", moves(1))
     held = [one, two, three, four]
     pieces = [both] + held + [lax.ppermute(piece, "elem", ACROSS) for piece in held]
     placed = penalty(stator_source, place, pieces)

time: 54.6 us -> 50.3 us (0.921)
  local copies, waits for them, and re-layouts: 4.41 us -> 1.03 us
  starting transfers between devices: 32 us -> 30.4 us
  waiting for transfers between devices: 3.27 us -> 3.86 us
    ppermute x1, starting transfers between devices: 5.65 us -> 0.73 us  [local(): one = lax.ppermute(both, 'elem', moves(1))]
    ppermute x3, starting transfers between devices: 4.26 us -> 8.96 us  [the longest x1 6.54 us: local(): three = lax.ppermute(both, 'elem', moves(3))]
    unnamed x32 -> x36, local copies, waits for them, and re-layouts: 4.4 us -> 1.03 us
    ppermute x4, starting transfers between devices: 6.52 us -> 4.99 us  [local(): lax.ppermute(piece, 'elem', ACROSS)]
    pallas_call x1 -> x2, Pallas kernels: 1.17 us -> 2.33 us  [the longest x1 1.94 us: pack(): pl.pallas_call(pack_kernel, grid=(GROUPS // step,), in_specs=[pl.BlockSpe...]
    ppermute x3, waiting for transfers between devices: 1.71 us -> 2.52 us  [the longest x1 2.52 us: local(): two = lax.ppermute(one, 'elem', moves(1))]
    pallas_call x1, Pallas kernels: 4.01 us -> 3.26 us  [helmholtz(): pl.pallas_call(helm_kernel, grid=(GROUPS // step,), in_specs=[pl.BlockSpe...]
    pallas_call x1, Pallas kernels: 1.77 us -> 1.12 us  [traces(): pl.pallas_call(trace_kernel, in_specs=[pl.BlockSpec(memory_space=SMEM), p...]
  transfers between devices with their start and end apart: 11 -> 11, of which waited for: 3 -> 3; matrix products, arithmetic and copies ran while one was open for 0% -> 0% of each run, Pallas kernels for 22% -> 23%
where the time goes in v3:
time: 50.3 us; the launch traced here: 50 us
  starting transfers between devices  30.4 us (60%)
  Pallas kernels  14.4 us (29%)
  waiting for transfers between devices  3.86 us (8%)
  local copies, waits for them, and re-layouts  1.03 us (2%)
    all_to_all x1, starting transfers between devices, local(): got = lax.all_to_all(packed, 'four', 0, 0, tiled=True)  7.77 us
    all_to_all x1, starting transfers between devices, local(): nonlinear = lax.all_to_all(advect_hat, 'four', 0, 0, tiled=True)  6.9 us
    ppermute x1, starting transfers between devices, local(): three = lax.ppermute(both, 'elem', moves(3))  6.54 us
    ppermute x4, starting transfers between devices, local(): lax.ppermute(piece, 'elem', ACROSS)  4.99 us
    pallas_call x1, Pallas kernels, planes(): pl.pallas_call(plane_kernel, in_specs=[pl.BlockSpec(memory_space=SMEM)] +...  4.56 us
    pallas_call x1, Pallas kernels, helmholtz(): pl.pallas_call(helm_kernel, grid=(GROUPS // step,), in_specs=[pl.BlockSpe...  3.26 us
    ppermute x1, waiting for transfers between devices, local(): two = lax.ppermute(one, 'elem', moves(1))  2.52 us
    ppermute x1, starting transfers between devices, local(): two = lax.ppermute(one, 'elem', moves(1))  1.98 us
  transfers between devices with their start and end apart: 11, of which 3 were waited for; matrix products, arithmetic and copies ran while one was open for 0% of the time, Pallas kernels for 23%

profile of v3, /device:TPU:1, one launch (start us, length us, event | category | flops | bytes accessed | tf_op | source)
XLA Modules:
  0.0 50.0 jit_solution(16384154269751140094)
XLA Ops:
  0.0 0.0 copy-start.6
  0.0 0.0 copy-start.7
  0.0 1.9 %pack.1.packed_ref = f32[16,96,128]{2,1,0:T(8,128)} custom-call(f32[96,2048]{1,0:T(8,128)} %bitcast.4), custom_call_target="tpu_custom_call" | custom-call | bytes 1600000 | tf_op jit(solution)/shard_map/pack/pallas_call | solution.py:133
  2.0 0.0 copy-start.14
  2.0 0.0 copy-start.15
  2.0 0.0 copy-start.16
  2.0 0.0 copy-start.17
  2.0 7.8 %all-to-all-start = ((f32[16,96,128]{2,1,0:T(8,128)}), f32[16,96,128]{2,1,0:T(8,128)}, u32[]{:S(2)}, u32[]{:S(2)}) async-start(f32[16,96,128]{2,1,0:T(8,128)} %pack.1.packed_ref), calls=%async_computation | async-start | bytes 1572864 | tf_op jit(solution)/shard_map/all_to_all | solution.py:510
  9.8 0.0 copy-done.8
  9.8 1.1 %traces.1.mine_ref = f32[256,128]{1,0:T(8,128)S(1)} custom-call(s32[32]{0:T(128)S(1)} %copy-done.8, f32[16,96,128]{2,1,0:T(8,128)S(1)} %copy-done), custom_call_target="tpu_custom_call" | custom-call | bytes 8000000 | tf_op jit(solution)/shard_map/traces/pallas_call | solution.py:163
  11.0 1.0 %collective-permute-start = (f32[256,128]{1,0:T(8,128)S(1)}, f32[256,128]{1,0:T(8,128)S(1)}, u32[]{:S(2)}, u32[]{:S(2)}) collective-permute-start(f32[256,128]{1,0:T(8,128)S(1)} %traces.1.mine_ref), channel_id=1, source_target_pairs={{0,16},{16,0},{32,48},{48,32},{64,80},{80,64},{96,112},{112,96},{1... | collective-permute-start | bytes 393224 | tf_op jit(solution)/shard_map/ppermute | solution.py:512
  12.0 0.0 copy-done.5
  12.0 0.0 copy-done.7
  12.0 0.4 tables.1.table_ref
  12.5 3.3 %helm.1.helm_ref = f32[16,96,128]{2,1,0:T(8,128)S(1)} custom-call(f32[4,32]{1,0:T(4,128)S(1)} %copy-done.13, f32[32]{0:T(128)S(1)} %copy-done.14, s32[32]{0:T(128)S(1)} %copy-done.9, f32[16,96,128]{2,1,0:T(8,128)S(1)} %copy-done, f32[16,128]{1,0:T(8,128)S(1)} %bitcast.3, f32[1,128]{1,0:T(1,128)S(1)} %copy-done.17, bf16[384,256]{1,0:T(8,128)(2,1)S(1)} %copy-done.15, ...), custom_call_target="tpu_custom_call" | custom-call | flops 2000000000 | bytes 8000000 | tf_op jit(solution)/shard_map/helm/pallas_call | solution.py:253
  15.8 0.9 %copy-done.1 = f32[16,96,128]{2,1,0:T(8,128)} copy-done((f32[16,96,128]{2,1,0:T(8,128)}, f32[16,96,128]{2,1,0:T(8,128)S(1)}, u32[]{:S(2)}) %copy-start.1) | copy-done | bytes 786456
  16.7 0.0 collective-permute-done.other_ref
  16.7 0.0 copy-start.3
  16.7 0.0 copy-start.10
  16.7 6.5 %collective-permute-start.2 = (f32[512,128]{1,0:T(8,128)S(1)}, f32[512,128]{1,0:T(8,128)S(1)}, u32[]{:S(2)}, u32[]{:S(2)}) collective-permute-start(f32[512,128]{1,0:T(8,128)S(1)} %pair.1.refs_0_), channel_id=1, source_target_pairs={{0,96},{16,176},{32,128},{48,208},{64,160},{80,240},{96,192},{112,... | collective-permute-start | bytes 786440 | tf_op jit(solution)/shard_map/ppermute | solution.py:514
  23.3 0.7 %collective-permute-start.1 = (f32[512,128]{1,0:T(8,128)S(1)}, f32[512,128]{1,0:T(8,128)S(1)}, u32[]{:S(2)}, u32[]{:S(2)}) collective-permute-start(f32[512,128]{1,0:T(8,128)S(1)} %pair.1.refs_0_), channel_id=1, source_target_pairs={{0,32},{16,240},{32,64},{48,16},{64,96},{80,48},{96,128},{112,80},... | collective-permute-start | bytes 786440 | tf_op jit(solution)/shard_map/ppermute | solution.py:513
  24.0 0.0 all-to-all-done.got_ref
  24.0 4.6 %planes.1 = f32[16,96,128]{2,1,0:T(8,128)} custom-call(f32[4,32]{1,0:T(4,128)S(1)} %copy-done.13, f32[16,96,128]{2,1,0:T(8,128)} %all-to-all-done.got_ref, bf16[640,1536]{1,0:T(8,128)(2,1)S(1)} %tables.1.table_ref, bf16[384,256]{1,0:T(8,128)(2,1)S(1)} %copy-done.15), custom_call_target="tpu_custom_call" | custom-call | flops 3000000000 | bytes 4000000 | tf_op jit(solution)/shard_map/planes/pallas_call | solution.py:386
  28.6 0.0 copy-start.11
  28.6 6.9 %all-to-all-start.1 = ((f32[16,96,128]{2,1,0:T(8,128)}), f32[16,96,128]{2,1,0:T(8,128)S(1)}, u32[]{:S(2)}, u32[]{:S(2)}) async-start(f32[16,96,128]{2,1,0:T(8,128)} %planes.1), calls=%async_computation.1 | async-start | bytes 1572864 | tf_op jit(solution)/shard_map/all_to_all | solution.py:523
  35.5 0.0 copy-done.3
  35.5 0.0 copy-done.10
  35.5 0.0 copy-start.2
  35.5 0.6 %placing.1.place_ref = bf16[768,256]{1,0:T(8,128)(2,1)S(1)} custom-call(s32[32]{0:T(128)S(1)} %copy-done.9, s32[32]{0:T(128)S(1)} %copy-done.10, f32[64,256]{1,0:T(8,128)S(1)} %copy-done.3), custom_call_target="tpu_custom_call" | custom-call | flops 1000 | bytes 1000 | tf_op jit(solution)/shard_map/placing/pallas_call | solution.py:414
  36.2 0.0 collective-permute-done.2.refs_3_
  36.2 0.0 collective-permute-done.1.refs_1_
  36.2 2.0 %collective-permute-start.3 = (f32[512,128]{1,0:T(8,128)S(1)}, f32[512,128]{1,0:T(8,128)S(1)}, u32[]{:S(2)}, u32[]{:S(2)}) collective-permute-start(f32[512,128]{1,0:T(8,128)S(1)} %collective-permute-done.1.refs_1_), channel_id=1, source_target_pairs={{0,32},{16,240},{32,64},{48,16},{64,96},{80,48},{96,128},{112,80},... | collective-permute-start | bytes 786440 | tf_op jit(solution)/shard_map/ppermute | solution.py:524
  38.2 0.4 collective-permute-start.4
  38.6 0.6 %collective-permute-start.5 = (f32[512,128]{1,0:T(8,128)S(1)}, f32[512,128]{1,0:T(8,128)S(1)}, u32[]{:S(2)}, u32[]{:S(2)}) collective-permute-start(f32[512,128]{1,0:T(8,128)S(1)} %collective-permute-done.1.refs_1_), channel_id=1, source_target_pairs={{0,16},{16,0},{32,48},{48,32},{64,80},{80,64},{96,112},{112,96},{1... | collective-permute-start | bytes 786440 | tf_op jit(solution)/shard_map/ppermute | solution.py:527
  39.2 0.0 collective-permute-start.7
  39.3 2.5 %collective-permute-done.3.refs_2_ = f32[512,128]{1,0:T(8,128)S(1)} collective-permute-done((f32[512,128]{1,0:T(8,128)S(1)}, f32[512,128]{1,0:T(8,128)S(1)}, u32[]{:S(2)}, u32[]{:S(2)}) %collective-permute-start.3) | collective-permute-done | bytes 262176 | tf_op jit(solution)/shard_map/ppermute | solution.py:524
  41.8 2.9 %collective-permute-start.6 = (f32[512,128]{1,0:T(8,128)S(1)}, f32[512,128]{1,0:T(8,128)S(1)}, u32[]{:S(2)}, u32[]{:S(2)}) collective-permute-start(f32[512,128]{1,0:T(8,128)S(1)} %collective-permute-done.3.refs_2_), channel_id=1, source_target_pairs={{0,16},{16,0},{32,48},{48,32},{64,80},{80,64},{96,112},{112,96},{1... | collective-permute-start | bytes 786440 | tf_op jit(solution)/shard_map/ppermute | solution.py:527
  44.7 0.0 collective-permute-done.4.refs_4_
  44.7 1.4 %collective-permute-start.8 = (f32[256,128]{1,0:T(8,128)S(1)}, f32[256,128]{1,0:T(8,128)S(1)}, u32[]{:S(2)}, u32[]{:S(2)}) collective-permute-start(f32[256,128]{1,0:T(8,128)S(1)} %collective-permute-done.4.refs_4_), channel_id=1, source_target_pairs={{0,16},{16,0},{32,48},{48,32},{64,80},{80,64},{96,112},{112,96},{1... | collective-permute-start | bytes 393224 | tf_op jit(solution)/shard_map/ppermute | solution.py:527
  46.1 1.0 %collective-permute-done.8.refs_8_ = f32[256,128]{1,0:T(8,128)S(1)} collective-permute-done((f32[256,128]{1,0:T(8,128)S(1)}, f32[256,128]{1,0:T(8,128)S(1)}, u32[]{:S(2)}, u32[]{:S(2)}) %collective-permute-start.8) | collective-permute-done | bytes 131104 | tf_op jit(solution)/shard_map/ppermute | solution.py:527
  47.1 0.0 collective-permute-done.5.refs_5_
  47.1 0.0 collective-permute-done.7.refs_7_
  47.1 0.0 collective-permute-done.6.refs_6_
  47.1 0.0 copy-done.11
  47.1 1.3 %penalty.1.placed_ref = f32[96,256]{1,0:T(8,128)S(1)} custom-call(s32[32]{0:T(128)S(1)} %copy-done.11, bf16[768,256]{1,0:T(8,128)(2,1)S(1)} %placing.1.place_ref, f32[512,128]{1,0:T(8,128)S(1)} %pair.1.refs_0_, f32[512,128]{1,0:T(8,128)S(1)} %collective-permute-done.1.refs_1_, f32[512,128]{1,0:T(8,128)S(1)} %collective-permute-done.3.refs_2_, ...), custom_call_target="tpu_custom_call" | custom-call | flops 1000 | bytes 1000 | tf_op jit(solution)/shard_map/penalty/pallas_call | solution.py:452
  48.4 0.3 all-to-all-done.1.nonlinear_ref
  48.8 0.0 copy-done.2
  48.8 1.2 %final_sum.1 = f32[96,2048]{1,0:T(8,128)} custom-call(f32[16,96,128]{2,1,0:T(8,128)S(1)} %all-to-all-done.1.nonlinear_ref, f32[16,96,128]{2,1,0:T(8,128)S(1)} %copy-done.2, f32[96,256]{1,0:T(8,128)S(1)} %penalty.1.placed_ref), custom_call_target="tpu_custom_call" | custom-call | bytes 2400000 | tf_op jit(solution)/shard_map/final_sum/pallas_call | solution.py:486
  (20 shorter events, 0.1 us)
Async XLA Ops:
  0.0 9.8 %copy-start.8 = (s32[32]{0:T(128)S(1)}, s32[32]{0:T(128)}, u32[]{:S(2)}) copy-start(s32[32]{0:T(128)} %rotor_ref.1) | copy-start | bytes 388
  0.0 12.0 %copy-start.4 = (f32[24,384]{1,0:T(8,128)S(1)}, f32[24,384]{1,0:T(8,128)}, u32[]{:S(2)}) copy-start(f32[24,384]{1,0:T(8,128)} %constant.21.clone.sin_far_ref) | copy-start | bytes 110596
  0.0 12.0 %copy-start.5 = (f32[24,384]{1,0:T(8,128)S(1)}, f32[24,384]{1,0:T(8,128)}, u32[]{:S(2)}) copy-start(f32[24,384]{1,0:T(8,128)} %constant.20.clone.cos_far_ref) | copy-start | bytes 110596
  0.0 12.0 %copy-start.6 = (f32[16,384]{1,0:T(8,128)S(1)}, f32[16,384]{1,0:T(8,128)}, u32[]{:S(2)}) copy-start(f32[16,384]{1,0:T(8,128)} %constant.23.clone.sin_near_ref) | copy-start | bytes 73732
  0.0 12.0 %copy-start.7 = (f32[16,384]{1,0:T(8,128)S(1)}, f32[16,384]{1,0:T(8,128)}, u32[]{:S(2)}) copy-start(f32[16,384]{1,0:T(8,128)} %constant.22.clone.cos_near_ref) | copy-start | bytes 73732
  2.0 7.9 %copy-start = (f32[16,96,128]{2,1,0:T(8,128)S(1)}, f32[16,96,128]{2,1,0:T(8,128)}, u32[]{:S(2)}) copy-start(f32[16,96,128]{2,1,0:T(8,128)} %pack.1.packed_ref) | copy-start | bytes 2359300
  2.0 10.4 %copy-start.9 = (s32[32]{0:T(128)S(1)}, s32[32]{0:T(128)}, u32[]{:S(2)}) copy-start(s32[32]{0:T(128)} %stator_ref.3) | copy-start | bytes 388
  2.0 10.4 %copy-start.12 = (f32[2048]{0:T(1024)S(1)}, f32[2048]{0:T(1024)}, u32[]{:S(2)}) copy-start(f32[2048]{0:T(1024)} %param.19) | copy-start | bytes 24580
  2.0 10.4 %copy-start.13 = (f32[4,32]{1,0:T(4,128)S(1)}, f32[4,32]{1,0:T(4,128)}, u32[]{:S(2)}) copy-start(f32[4,32]{1,0:T(4,128)} %metric_ref.3) | copy-start | bytes 1540
  2.0 10.4 %copy-start.14 = (f32[32]{0:T(128)S(1)}, f32[32]{0:T(128)}, u32[]{:S(2)}) copy-start(f32[32]{0:T(128)} %area_ref.1) | copy-start | bytes 388
  2.0 10.4 %copy-start.15 = (bf16[384,256]{1,0:T(8,128)(2,1)S(1)}, bf16[384,256]{1,0:T(8,128)(2,1)}, u32[]{:S(2)}) copy-start(bf16[384,256]{1,0:T(8,128)(2,1)} %constant.16.clone.forward_ref) | copy-start | bytes 589828
  2.0 10.4 %copy-start.16 = (bf16[768,128]{1,0:T(8,128)(2,1)S(1)}, bf16[768,128]{1,0:T(8,128)(2,1)}, u32[]{:S(2)}) copy-start(bf16[768,128]{1,0:T(8,128)(2,1)} %constant.17.clone.back_ref) | copy-start | bytes 589828
  2.0 10.4 %copy-start.17 = (f32[1,128]{1,0:T(1,128)S(1)}, f32[1,128]{1,0:T(1,128)}, u32[]{:S(2)}) copy-start(f32[1,128]{1,0:T(1,128)} %constant.18.clone.weight_ref) | copy-start | bytes 1540
  2.0 22.0 %all-to-all-start = ((f32[16,96,128]{2,1,0:T(8,128)}), f32[16,96,128]{2,1,0:T(8,128)}, u32[]{:S(2)}, u32[]{:S(2)}) async-start(f32[16,96,128]{2,1,0:T(8,128)} %pack.1.packed_ref), calls=%async_computation | async-start | bytes 1572864 | tf_op jit(solution)/shard_map/all_to_all | solution.py:510
  11.0 5.7 %collective-permute-start = (f32[256,128]{1,0:T(8,128)S(1)}, f32[256,128]{1,0:T(8,128)S(1)}, u32[]{:S(2)}, u32[]{:S(2)}) collective-permute-start(f32[256,128]{1,0:T(8,128)S(1)} %traces.1.mine_ref), channel_id=1, source_target_pairs={{0,16},{16,0},{32,48},{48,32},{64,80},{80,64},{96,112},{112,96},{1... | collective-permute-start | bytes 393224 | tf_op jit(solution)/shard_map/ppermute | solution.py:512
  15.8 0.9 %copy-start.1 = (f32[16,96,128]{2,1,0:T(8,128)}, f32[16,96,128]{2,1,0:T(8,128)S(1)}, u32[]{:S(2)}) copy-start(f32[16,96,128]{2,1,0:T(8,128)S(1)} %helm.1.helm_ref) | copy-start | bytes 2359300
  16.7 18.8 %copy-start.3 = (f32[64,256]{1,0:T(8,128)S(1)}, f32[64,256]{1,0:T(8,128)}, u32[]{:S(2)}) copy-start(f32[64,256]{1,0:T(8,128)} %constant.19.clone.interp_ref) | copy-start | bytes 196612
  16.7 18.8 %copy-start.10 = (s32[32]{0:T(128)S(1)}, s32[32]{0:T(128)}, u32[]{:S(2)}) copy-start(s32[32]{0:T(128)} %offset_ref.1) | copy-start | bytes 388
  16.7 19.4 %collective-permute-start.2 = (f32[512,128]{1,0:T(8,128)S(1)}, f32[512,128]{1,0:T(8,128)S(1)}, u32[]{:S(2)}, u32[]{:S(2)}) collective-permute-start(f32[512,128]{1,0:T(8,128)S(1)} %pair.1.refs_0_), channel_id=1, source_target_pairs={{0,96},{16,176},{32,128},{48,208},{64,160},{80,240},{96,192},{112,... | collective-permute-start | bytes 786440 | tf_op jit(solution)/shard_map/ppermute | solution.py:514
  23.3 12.9 %collective-permute-start.1 = (f32[512,128]{1,0:T(8,128)S(1)}, f32[512,128]{1,0:T(8,128)S(1)}, u32[]{:S(2)}, u32[]{:S(2)}) collective-permute-start(f32[512,128]{1,0:T(8,128)S(1)} %pair.1.refs_0_), channel_id=1, source_target_pairs={{0,32},{16,240},{32,64},{48,16},{64,96},{80,48},{96,128},{112,80},... | collective-permute-start | bytes 786440 | tf_op jit(solution)/shard_map/ppermute | solution.py:513
  28.6 18.5 %copy-start.11 = (s32[32]{0:T(128)S(1)}, s32[32]{0:T(128)}, u32[]{:S(2)}) copy-start(s32[32]{0:T(128)} %source_ref.1) | copy-start | bytes 388
  28.6 20.2 %all-to-all-start.1 = ((f32[16,96,128]{2,1,0:T(8,128)}), f32[16,96,128]{2,1,0:T(8,128)S(1)}, u32[]{:S(2)}, u32[]{:S(2)}) async-start(f32[16,96,128]{2,1,0:T(8,128)} %planes.1), calls=%async_computation.1 | async-start | bytes 1572864 | tf_op jit(solution)/shard_map/all_to_all | solution.py:523
  35.5 13.3 %copy-start.2 = (f32[16,96,128]{2,1,0:T(8,128)S(1)}, f32[16,96,128]{2,1,0:T(8,128)}, u32[]{:S(2)}) copy-start(f32[16,96,128]{2,1,0:T(8,128)} %copy-done.1) | copy-start | bytes 2359300
  36.2 5.6 %collective-permute-start.3 = (f32[512,128]{1,0:T(8,128)S(1)}, f32[512,128]{1,0:T(8,128)S(1)}, u32[]{:S(2)}, u32[]{:S(2)}) collective-permute-start(f32[512,128]{1,0:T(8,128)S(1)} %collective-permute-done.1.refs_1_), channel_id=1, source_target_pairs={{0,32},{16,240},{32,64},{48,16},{64,96},{80,48},{96,128},{112,80},... | collective-permute-start | bytes 786440 | tf_op jit(solution)/shard_map/ppermute | solution.py:524
  38.2 6.5 %collective-permute-start.4 = (f32[256,128]{1,0:T(8,128)S(1)}, f32[256,128]{1,0:T(8,128)S(1)}, u32[]{:S(2)}, u32[]{:S(2)}) collective-permute-start(f32[256,128]{1,0:T(8,128)S(1)} %slice.3), channel_id=1, source_target_pairs={{0,32},{16,240},{32,64},{48,16},{64,96},{80,48},{96,128},{112,80},... | collective-permute-start | bytes 393224 | tf_op jit(solution)/shard_map/ppermute | solution.py:525
  38.6 8.5 %collective-permute-start.5 = (f32[512,128]{1,0:T(8,128)S(1)}, f32[512,128]{1,0:T(8,128)S(1)}, u32[]{:S(2)}, u32[]{:S(2)}) collective-permute-start(f32[512,128]{1,0:T(8,128)S(1)} %collective-permute-done.1.refs_1_), channel_id=1, source_target_pairs={{0,16},{16,0},{32,48},{48,32},{64,80},{80,64},{96,112},{112,96},{1... | collective-permute-start | bytes 786440 | tf_op jit(solution)/shard_map/ppermute | solution.py:527
  39.2 7.9 %collective-permute-start.7 = (f32[512,128]{1,0:T(8,128)S(1)}, f32[512,128]{1,0:T(8,128)S(1)}, u32[]{:S(2)}, u32[]{:S(2)}) collective-permute-start(f32[512,128]{1,0:T(8,128)S(1)} %collective-permute-done.2.refs_3_), channel_id=1, source_target_pairs={{0,16},{16,0},{32,48},{48,32},{64,80},{80,64},{96,112},{112,96},{1... | collective-permute-start | bytes 786440 | tf_op jit(solution)/shard_map/ppermute | solution.py:527
  41.8 5.3 %collective-permute-start.6 = (f32[512,128]{1,0:T(8,128)S(1)}, f32[512,128]{1,0:T(8,128)S(1)}, u32[]{:S(2)}, u32[]{:S(2)}) collective-permute-start(f32[512,128]{1,0:T(8,128)S(1)} %collective-permute-done.3.refs_2_), channel_id=1, source_target_pairs={{0,16},{16,0},{32,48},{48,32},{64,80},{80,64},{96,112},{112,96},{1... | collective-permute-start | bytes 786440 | tf_op jit(solution)/shard_map/ppermute | solution.py:527
  44.7 2.4 %collective-permute-start.8 = (f32[256,128]{1,0:T(8,128)S(1)}, f32[256,128]{1,0:T(8,128)S(1)}, u32[]{:S(2)}, u32[]{:S(2)}) collective-permute-start(f32[256,128]{1,0:T(8,128)S(1)} %collective-permute-done.4.refs_4_), channel_id=1, source_target_pairs={{0,16},{16,0},{32,48},{48,32},{64,80},{80,64},{96,112},{112,96},{1... | collective-permute-start | bytes 393224 | tf_op jit(solution)/shard_map/ppermute | solution.py:527

commit v4 on v3

--- a/solution.py
+++ b/solution.py
@@ -272,38 +272,29 @@
     )(metric, area, stator_element, packed, visc, weight, forward, back)
 
 
-def table_kernel(cos_far_ref, sin_far_ref, cos_near_ref, sin_near_ref, out_ref):
-    row = lax.broadcasted_iota(jnp.int32, (16, HALF), 0)
-    for back, count, width in ((False, HALF, PAIRS), (True, PAIRS, HALF)):
-        near_cos, near_sin = cos_near_ref[:, pl.ds(0, width)], sin_near_ref[:, pl.ds(0, width)]
-        for step in range(count // 16):
-            far_cos = cos_far_ref[pl.ds(step, 1), pl.ds(0, width)]
-            far_sin = sin_far_ref[pl.ds(step, 1), pl.ds(0, width)]
-            cosine = far_cos * near_cos - far_sin * near_sin
-            sine = far_sin * near_cos + far_cos * near_sin
-            if back:
-                half = (row == 0) & (step == 0)
-                cosine = jnp.where(half, 1.0 / PLANES, 2.0 / PLANES) * cosine
-                sine = (2.0 / PLANES) * sine
-            rows = pl.ds((HALF if back else 0) + step * 16, 16)
-            for index, part in enumerate(split(cosine) + split(sine)):
-                out_ref[rows, pl.ds(index * width, width)] = part
-
-
-def tables():
-    whole = pl.BlockSpec(memory_space=VMEM)
-    return pl.pallas_call(
-        table_kernel,
-        in_specs=[whole] * 4,
-        out_specs=whole,
-        out_shape=VMEM((HALF + PAIRS, 4 * HALF), BF16),
-        compiler_params=granted(4),
-        cost_estimate=pl.CostEstimate(flops=1000, bytes_accessed=1000, transcendentals=0),
-        name="tables",
-    )(*span_factors())
-
-
-def plane_kernel(metric_ref, got_ref, table_ref, forward_ref, out_ref, done_ref, sems):
+def make_tables(back, factors, table_ref):
+    count, width = (PAIRS, HALF) if back else (HALF, PAIRS)
+    cos_far_ref, sin_far_ref, cos_near_ref, sin_near_ref = factors
+    near_cos, near_sin = cos_near_ref[:, pl.ds(0, width)], sin_near_ref[:, pl.ds(0, width)]
+    row = lax.broadcasted_iota(jnp.int32, (16, width), 0)
+    for step in range(count // 16):
+        far_cos = cos_far_ref[pl.ds(step, 1), pl.ds(0, width)]
+        far_sin = sin_far_ref[pl.ds(step, 1), pl.ds(0, width)]
+        cosine = far_cos * near_cos - far_sin * near_sin
+        sine = far_sin * near_cos + far_cos * near_sin
+        if back:
+            half = (row == 0) & (step == 0)
+            cosine = jnp.where(half, 1.0 / PLANES, 2.0 / PLANES) * cosine
+            sine = (2.0 / PLANES) * sine
+        rows = pl.ds((HALF if back else 0) + step * 16, 16)
+        for index, part in enumerate(split(cosine) + split(sine)):
+            table_ref[rows, pl.ds(index * width, width)] = part
+
+
+def plane_kernel(metric_ref, got_ref, forward_ref, *refs):
+    factors, (out_ref, table_ref, done_ref, sems) = refs[:4], refs[4:]
+    make_tables(False, factors, table_ref)
+    make_tables(True, factors, table_ref)
     pair = lax.axis_index("four") * 2
     rx, ry, sx, sy = [
         lane_scalars(metric_ref[i, pair], metric_ref[i, pair + 1]) for i in range(4)
@@ -381,21 +372,22 @@
         store.wait()
 
 
-def planes(metric, got, tables, forward):
+def planes(metric, got, factors, forward):
     whole = pl.BlockSpec(memory_space=VMEM)
     return pl.pallas_call(
         plane_kernel,
-        in_specs=[pl.BlockSpec(memory_space=SMEM)] + [whole] * 3,
+        in_specs=[pl.BlockSpec(memory_space=SMEM)] + [whole] * 6,
         out_specs=pl.BlockSpec(memory_space=pl.ANY),
         out_shape=jax.ShapeDtypeStruct((GROUPS, ROWS, LANES), F32),
         scratch_shapes=[
+            pltpu.VMEM((HALF + PAIRS, 4 * HALF), BF16),
             pltpu.VMEM((GROUPS, ROWS, LANES), F32),
             pltpu.SemaphoreType.DMA((2,)),
         ],
         compiler_params=granted(20),
         cost_estimate=pl.CostEstimate(flops=3000000000, bytes_accessed=4000000, transcendentals=0),
         name="planes",
-    )(metric, got, tables, forward)
+    )(metric, got, forward, *factors)
 
 
 def place_kernel(stator_ref, offset_ref, interp_ref, out_ref, base_ref, place_ref):
@@ -516,13 +508,13 @@
         metric, area, stator_element, packed, visc.reshape(GROUPS, LANES), weight, forward, back
     )
     place = placing(stator_element, mortar_offset, spread)
-    table = tables()
-    got, helm, table = lax.optimization_barrier((got, helm, table))
-    one, three, place = lax.optimization_barrier((one, three, place))
-    advect_hat = planes(metric, got, table, forward)
+    got, helm = lax.optimization_barrier((got, helm))
+    one, three = lax.optimization_barrier((one, three))
+    advect_hat = planes(metric, got, span_factors(), forward)
     nonlinear = lax.all_to_all(advect_hat, "four", 0, 0, tiled=True)
     two = lax.ppermute(one, "elem", moves(1))
     four = lax.ppermute(three[:256], "elem", moves(1))
+    four, place = lax.optimization_barrier((four, place))
     held = [one, two, three, four]
     pieces = [both] + held + [lax.ppermute(piece, "elem", ACROSS) for piece in held]
     placed = penalty(stator_source, place, pieces)

time: 50.3 us -> 48.5 us (0.964)
  local copies, waits for them, and re-layouts: 1.03 us -> 0.11 us
  Pallas kernels: 14.4 us -> 13.6 us
  waiting for transfers between devices: 3.86 us -> 3.22 us
  starting transfers between devices: 30.4 us -> 31 us
    ppermute x1, starting transfers between devices: 6.54 us -> 1.62 us  [local(): three = lax.ppermute(both, 'elem', moves(3))]
    ppermute x1, starting transfers between devices: 0.73 us -> 5.65 us  [local(): one = lax.ppermute(both, 'elem', moves(1))]
    unnamed x36 -> x32, local copies, waits for them, and re-layouts: 1.03 us -> 0.1 us
    ppermute x1, starting transfers between devices: 1.98 us -> 2.76 us  [local(): two = lax.ppermute(one, 'elem', moves(1))]
    ppermute x1, waiting for transfers between devices: 2.52 us -> 1.98 us  [local(): two = lax.ppermute(one, 'elem', moves(1))]
  transfers between devices with their start and end apart: 11 -> 11, of which waited for: 3 -> 3; matrix products, arithmetic and copies ran while one was open for 0% -> 0% of each run, Pallas kernels for 23% -> 22%
where the time goes in v4:
time: 48.5 us; the launch traced here: 48.2 us
  starting transfers between devices  31 us (64%)
  Pallas kernels  13.6 us (28%)
  waiting for transfers between devices  3.22 us (7%)
    all_to_all x1, starting transfers between devices, local(): got = lax.all_to_all(packed, 'four', 0, 0, tiled=True)  7.72 us
    all_to_all x1, starting transfers between devices, local(): nonlinear = lax.all_to_all(advect_hat, 'four', 0, 0, tiled=True)  6.72 us
    ppermute x1, starting transfers between devices, local(): one = lax.ppermute(both, 'elem', moves(1))  5.65 us
    ppermute x4, starting transfers between devices, local(): lax.ppermute(piece, 'elem', ACROSS)  4.68 us
    pallas_call x1, Pallas kernels, planes(): pl.pallas_call(plane_kernel, in_specs=[pl.BlockSpec(memory_space=SMEM)] +...  4.14 us
    pallas_call x1, Pallas kernels, helmholtz(): pl.pallas_call(helm_kernel, grid=(GROUPS // step,), in_specs=[pl.BlockSpe...  3.26 us
    ppermute x1, starting transfers between devices, local(): two = lax.ppermute(one, 'elem', moves(1))  2.76 us
    ppermute x1, waiting for transfers between devices, local(): two = lax.ppermute(one, 'elem', moves(1))  1.98 us
  transfers between devices with their start and end apart: 11, of which 3 were waited for; matrix products, arithmetic and copies ran while one was open for 0% of the time, Pallas kernels for 22%

profile of v4, /device:TPU:1, one launch (start us, length us, event | category | flops | bytes accessed | tf_op | source)
XLA Modules:
  0.0 48.2 jit_solution(9494584936655178430)
XLA Ops:
  0.0 1.9 %pack.1.packed_ref = f32[16,96,128]{2,1,0:T(8,128)} custom-call(f32[96,2048]{1,0:T(8,128)} %bitcast.4), custom_call_target="tpu_custom_call" | custom-call | bytes 1600000 | tf_op jit(solution)/shard_map/pack/pallas_call | solution.py:133
  1.9 7.7 %all-to-all-start = ((f32[16,96,128]{2,1,0:T(8,128)}), f32[16,96,128]{2,1,0:T(8,128)S(1)}, u32[]{:S(2)}, u32[]{:S(2)}) async-start(f32[16,96,128]{2,1,0:T(8,128)} %pack.1.packed_ref), calls=%async_computation | async-start | bytes 1572864 | tf_op jit(solution)/shard_map/all_to_all | solution.py:502
  9.6 0.0 copy-done
  9.6 0.0 copy-done.2
  9.6 0.0 copy-start.6
  9.7 0.0 copy-start.7
  9.7 0.0 copy-start.9
  9.7 0.0 copy-start.10
  9.7 1.1 %traces.1.mine_ref = f32[256,128]{1,0:T(8,128)S(1)} custom-call(s32[32]{0:T(128)S(1)} %copy-done.2, f32[16,96,128]{2,1,0:T(8,128)S(1)} %copy-done), custom_call_target="tpu_custom_call" | custom-call | bytes 8000000 | tf_op jit(solution)/shard_map/traces/pallas_call | solution.py:163
  10.8 0.0 copy-start.3
  10.8 0.0 copy-start.8
  10.8 0.0 copy-start.15
  10.9 1.0 %collective-permute-start = (f32[256,128]{1,0:T(8,128)S(1)}, f32[256,128]{1,0:T(8,128)S(1)}, u32[]{:S(2)}, u32[]{:S(2)}) collective-permute-start(f32[256,128]{1,0:T(8,128)S(1)} %traces.1.mine_ref), channel_id=1, source_target_pairs={{0,16},{16,0},{32,48},{48,32},{64,80},{80,64},{96,112},{112,96},{1... | collective-permute-start | bytes 393224 | tf_op jit(solution)/shard_map/ppermute | solution.py:504
  11.9 0.0 copy-done.7
  11.9 3.3 %helm.1.helm_ref = f32[16,96,128]{2,1,0:T(8,128)S(1)} custom-call(f32[4,32]{1,0:T(4,128)S(1)} %copy-done.7, f32[32]{0:T(128)S(1)} %copy-done.8, s32[32]{0:T(128)S(1)} %copy-done.3, f32[16,96,128]{2,1,0:T(8,128)S(1)} %copy-done, f32[16,128]{1,0:T(8,128)S(1)} %bitcast.3, f32[1,128]{1,0:T(1,128)S(1)} %copy-done.15, bf16[384,256]{1,0:T(8,128)(2,1)S(1)} %copy-done.9, ...), custom_call_target="tpu_custom_call" | custom-call | flops 2000000000 | bytes 8000000 | tf_op jit(solution)/shard_map/helm/pallas_call | solution.py:253
  15.2 0.0 copy-start.11
  15.2 0.0 copy-start.12
  15.2 0.0 copy-start.13
  15.3 0.0 copy-start.14
  15.3 0.0 collective-permute-done.other_ref
  15.3 5.7 %collective-permute-start.1 = (f32[512,128]{1,0:T(8,128)S(1)}, f32[512,128]{1,0:T(8,128)S(1)}, u32[]{:S(2)}, u32[]{:S(2)}) collective-permute-start(f32[512,128]{1,0:T(8,128)S(1)} %pair.1.refs_0_), channel_id=1, source_target_pairs={{0,32},{16,240},{32,64},{48,16},{64,96},{80,48},{96,128},{112,80},... | collective-permute-start | bytes 786440 | tf_op jit(solution)/shard_map/ppermute | solution.py:505
  21.0 1.6 %collective-permute-start.2 = (f32[512,128]{1,0:T(8,128)S(1)}, f32[512,128]{1,0:T(8,128)S(1)}, u32[]{:S(2)}, u32[]{:S(2)}) collective-permute-start(f32[512,128]{1,0:T(8,128)S(1)} %pair.1.refs_0_), channel_id=1, source_target_pairs={{0,96},{16,176},{32,128},{48,208},{64,160},{80,240},{96,192},{112,... | collective-permute-start | bytes 786440 | tf_op jit(solution)/shard_map/ppermute | solution.py:506
  22.6 0.2 all-to-all-done.got_ref
  22.8 0.0 copy-done.12
  22.8 4.1 %planes.1 = f32[16,96,128]{2,1,0:T(8,128)} custom-call(f32[4,32]{1,0:T(4,128)S(1)} %copy-done.7, f32[16,96,128]{2,1,0:T(8,128)S(1)} %all-to-all-done.got_ref, bf16[384,256]{1,0:T(8,128)(2,1)S(1)} %copy-done.9, f32[24,384]{1,0:T(8,128)S(1)} %copy-done.11, f32[24,384]{1,0:T(8,128)S(1)} %copy-done.12, f32[16,384]{1,0:T(8,128)S(1)} %copy-done.13, ...), custom_call_target="tpu_custom_call" | custom-call | flops 3000000000 | bytes 4000000 | tf_op jit(solution)/shard_map/planes/pallas_call | solution.py:377
  27.0 6.7 %all-to-all-start.1 = ((f32[16,96,128]{2,1,0:T(8,128)}), f32[16,96,128]{2,1,0:T(8,128)S(1)}, u32[]{:S(2)}, u32[]{:S(2)}) async-start(f32[16,96,128]{2,1,0:T(8,128)} %planes.1), calls=%async_computation.1 | async-start | bytes 1572864 | tf_op jit(solution)/shard_map/all_to_all | solution.py:514
  33.7 0.0 copy-start.1
  33.7 0.0 copy-start.4
  33.7 0.0 collective-permute-done.1.refs_1_
  33.7 0.0 collective-permute-done.2.refs_3_
  33.7 2.8 %collective-permute-start.4 = (f32[512,128]{1,0:T(8,128)S(1)}, f32[512,128]{1,0:T(8,128)S(1)}, u32[]{:S(2)}, u32[]{:S(2)}) collective-permute-start(f32[512,128]{1,0:T(8,128)S(1)} %collective-permute-done.1.refs_1_), channel_id=1, source_target_pairs={{0,32},{16,240},{32,64},{48,16},{64,96},{80,48},{96,128},{112,80},... | collective-permute-start | bytes 786440 | tf_op jit(solution)/shard_map/ppermute | solution.py:515
  36.5 0.0 copy-start.5
  36.5 0.8 %collective-permute-start.3 = (f32[256,128]{1,0:T(8,128)S(1)}, f32[256,128]{1,0:T(8,128)S(1)}, u32[]{:S(2)}, u32[]{:S(2)}) collective-permute-start(f32[256,128]{1,0:T(8,128)S(1)} %slice.3), channel_id=1, source_target_pairs={{0,32},{16,240},{32,64},{48,16},{64,96},{80,48},{96,128},{112,80},... | collective-permute-start | bytes 393224 | tf_op jit(solution)/shard_map/ppermute | solution.py:516
  37.3 0.3 collective-permute-start.5
  37.6 0.2 collective-permute-start.7
  37.8 2.0 %collective-permute-done.4.refs_2_ = f32[512,128]{1,0:T(8,128)S(1)} collective-permute-done((f32[512,128]{1,0:T(8,128)S(1)}, f32[512,128]{1,0:T(8,128)S(1)}, u32[]{:S(2)}, u32[]{:S(2)}) %collective-permute-start.4) | collective-permute-done | bytes 262176 | tf_op jit(solution)/shard_map/ppermute | solution.py:515
  39.8 3.4 %collective-permute-start.6 = (f32[512,128]{1,0:T(8,128)S(1)}, f32[512,128]{1,0:T(8,128)S(1)}, u32[]{:S(2)}, u32[]{:S(2)}) collective-permute-start(f32[512,128]{1,0:T(8,128)S(1)} %collective-permute-done.4.refs_2_), channel_id=1, source_target_pairs={{0,16},{16,0},{32,48},{48,32},{64,80},{80,64},{96,112},{112,96},{1... | collective-permute-start | bytes 786440 | tf_op jit(solution)/shard_map/ppermute | solution.py:519
  43.2 0.0 copy-done.4
  43.2 0.6 %placing.1.place_ref = bf16[768,256]{1,0:T(8,128)(2,1)S(1)} custom-call(s32[32]{0:T(128)S(1)} %copy-done.3, s32[32]{0:T(128)S(1)} %copy-done.4, f32[64,256]{1,0:T(8,128)S(1)} %copy-done.1), custom_call_target="tpu_custom_call" | custom-call | flops 1000 | bytes 1000 | tf_op jit(solution)/shard_map/placing/pallas_call | solution.py:406
  43.8 0.0 collective-permute-done.3.refs_4_
  43.8 0.8 %collective-permute-start.8 = (f32[256,128]{1,0:T(8,128)S(1)}, f32[256,128]{1,0:T(8,128)S(1)}, u32[]{:S(2)}, u32[]{:S(2)}) collective-permute-start(f32[256,128]{1,0:T(8,128)S(1)} %collective-permute-done.3.refs_4_), channel_id=1, source_target_pairs={{0,16},{16,0},{32,48},{48,32},{64,80},{80,64},{96,112},{112,96},{1... | collective-permute-start | bytes 393224 | tf_op jit(solution)/shard_map/ppermute | solution.py:519
  44.6 1.0 %collective-permute-done.8.refs_8_ = f32[256,128]{1,0:T(8,128)S(1)} collective-permute-done((f32[256,128]{1,0:T(8,128)S(1)}, f32[256,128]{1,0:T(8,128)S(1)}, u32[]{:S(2)}, u32[]{:S(2)}) %collective-permute-start.8) | collective-permute-done | bytes 131104 | tf_op jit(solution)/shard_map/ppermute | solution.py:519
  45.6 0.0 collective-permute-done.5.refs_5_
  45.6 0.0 collective-permute-done.7.refs_7_
  45.6 0.0 collective-permute-done.6.refs_6_
  45.6 1.3 %penalty.1.placed_ref = f32[96,256]{1,0:T(8,128)S(1)} custom-call(s32[32]{0:T(128)S(1)} %copy-done.5, bf16[768,256]{1,0:T(8,128)(2,1)S(1)} %placing.1.place_ref, f32[512,128]{1,0:T(8,128)S(1)} %pair.1.refs_0_, f32[512,128]{1,0:T(8,128)S(1)} %collective-permute-done.1.refs_1_, f32[512,128]{1,0:T(8,128)S(1)} %collective-permute-done.4.refs_2_, ...), custom_call_target="tpu_custom_call" | custom-call | flops 1000 | bytes 1000 | tf_op jit(solution)/shard_map/penalty/pallas_call | solution.py:444
  47.0 0.0 all-to-all-done.1.nonlinear_ref
  47.0 1.2 %final_sum.1 = f32[96,2048]{1,0:T(8,128)} custom-call(f32[16,96,128]{2,1,0:T(8,128)S(1)} %all-to-all-done.1.nonlinear_ref, f32[16,96,128]{2,1,0:T(8,128)S(1)} %helm.1.helm_ref, f32[96,256]{1,0:T(8,128)S(1)} %penalty.1.placed_ref), custom_call_target="tpu_custom_call" | custom-call | bytes 2400000 | tf_op jit(solution)/shard_map/final_sum/pallas_call | solution.py:478
  (15 shorter events, 0.1 us)
Async XLA Ops:
  1.9 7.7 %copy-start = (f32[16,96,128]{2,1,0:T(8,128)S(1)}, f32[16,96,128]{2,1,0:T(8,128)}, u32[]{:S(2)}) copy-start(f32[16,96,128]{2,1,0:T(8,128)} %pack.1.packed_ref) | copy-start | bytes 2359300
  1.9 7.7 %copy-start.2 = (s32[32]{0:T(128)S(1)}, s32[32]{0:T(128)}, u32[]{:S(2)}) copy-start(s32[32]{0:T(128)} %rotor_ref.1) | copy-start | bytes 388
  1.9 20.9 %all-to-all-start = ((f32[16,96,128]{2,1,0:T(8,128)}), f32[16,96,128]{2,1,0:T(8,128)S(1)}, u32[]{:S(2)}, u32[]{:S(2)}) async-start(f32[16,96,128]{2,1,0:T(8,128)} %pack.1.packed_ref), calls=%async_computation | async-start | bytes 1572864 | tf_op jit(solution)/shard_map/all_to_all | solution.py:502
  9.6 2.3 %copy-start.6 = (f32[2048]{0:T(1024)S(1)}, f32[2048]{0:T(1024)}, u32[]{:S(2)}) copy-start(f32[2048]{0:T(1024)} %param.19) | copy-start | bytes 24580
  9.7 2.2 %copy-start.7 = (f32[4,32]{1,0:T(4,128)S(1)}, f32[4,32]{1,0:T(4,128)}, u32[]{:S(2)}) copy-start(f32[4,32]{1,0:T(4,128)} %metric_ref.3) | copy-start | bytes 1540
  9.7 2.2 %copy-start.9 = (bf16[384,256]{1,0:T(8,128)(2,1)S(1)}, bf16[384,256]{1,0:T(8,128)(2,1)}, u32[]{:S(2)}) copy-start(bf16[384,256]{1,0:T(8,128)(2,1)} %constant.16.clone.forward_ref) | copy-start | bytes 589828
  9.7 2.2 %copy-start.10 = (bf16[768,128]{1,0:T(8,128)(2,1)S(1)}, bf16[768,128]{1,0:T(8,128)(2,1)}, u32[]{:S(2)}) copy-start(bf16[768,128]{1,0:T(8,128)(2,1)} %constant.17.clone.back_ref) | copy-start | bytes 589828
  10.8 1.1 %copy-start.3 = (s32[32]{0:T(128)S(1)}, s32[32]{0:T(128)}, u32[]{:S(2)}) copy-start(s32[32]{0:T(128)} %stator_ref.3) | copy-start | bytes 388
  10.8 1.1 %copy-start.8 = (f32[32]{0:T(128)S(1)}, f32[32]{0:T(128)}, u32[]{:S(2)}) copy-start(f32[32]{0:T(128)} %area_ref.1) | copy-start | bytes 388
  10.8 1.1 %copy-start.15 = (f32[1,128]{1,0:T(1,128)S(1)}, f32[1,128]{1,0:T(1,128)}, u32[]{:S(2)}) copy-start(f32[1,128]{1,0:T(1,128)} %constant.18.clone.weight_ref) | copy-start | bytes 1540
  10.9 4.4 %collective-permute-start = (f32[256,128]{1,0:T(8,128)S(1)}, f32[256,128]{1,0:T(8,128)S(1)}, u32[]{:S(2)}, u32[]{:S(2)}) collective-permute-start(f32[256,128]{1,0:T(8,128)S(1)} %traces.1.mine_ref), channel_id=1, source_target_pairs={{0,16},{16,0},{32,48},{48,32},{64,80},{80,64},{96,112},{112,96},{1... | collective-permute-start | bytes 393224 | tf_op jit(solution)/shard_map/ppermute | solution.py:504
  15.2 7.6 %copy-start.11 = (f32[24,384]{1,0:T(8,128)S(1)}, f32[24,384]{1,0:T(8,128)}, u32[]{:S(2)}) copy-start(f32[24,384]{1,0:T(8,128)} %constant.20.clone.refs_0_) | copy-start | bytes 110596
  15.2 7.6 %copy-start.12 = (f32[24,384]{1,0:T(8,128)S(1)}, f32[24,384]{1,0:T(8,128)}, u32[]{:S(2)}) copy-start(f32[24,384]{1,0:T(8,128)} %constant.21.clone.refs_1_) | copy-start | bytes 110596
  15.2 7.6 %copy-start.13 = (f32[16,384]{1,0:T(8,128)S(1)}, f32[16,384]{1,0:T(8,128)}, u32[]{:S(2)}) copy-start(f32[16,384]{1,0:T(8,128)} %constant.22.clone.refs_2_) | copy-start | bytes 73732
  15.3 7.6 %copy-start.14 = (f32[16,384]{1,0:T(8,128)S(1)}, f32[16,384]{1,0:T(8,128)}, u32[]{:S(2)}) copy-start(f32[16,384]{1,0:T(8,128)} %constant.23.clone.refs_3_) | copy-start | bytes 73732
  15.3 18.4 %collective-permute-start.1 = (f32[512,128]{1,0:T(8,128)S(1)}, f32[512,128]{1,0:T(8,128)S(1)}, u32[]{:S(2)}, u32[]{:S(2)}) collective-permute-start(f32[512,128]{1,0:T(8,128)S(1)} %pair.1.refs_0_), channel_id=1, source_target_pairs={{0,32},{16,240},{32,64},{48,16},{64,96},{80,48},{96,128},{112,80},... | collective-permute-start | bytes 786440 | tf_op jit(solution)/shard_map/ppermute | solution.py:505
  21.0 12.8 %collective-permute-start.2 = (f32[512,128]{1,0:T(8,128)S(1)}, f32[512,128]{1,0:T(8,128)S(1)}, u32[]{:S(2)}, u32[]{:S(2)}) collective-permute-start(f32[512,128]{1,0:T(8,128)S(1)} %pair.1.refs_0_), channel_id=1, source_target_pairs={{0,96},{16,176},{32,128},{48,208},{64,160},{80,240},{96,192},{112,... | collective-permute-start | bytes 786440 | tf_op jit(solution)/shard_map/ppermute | solution.py:506
  27.0 20.0 %all-to-all-start.1 = ((f32[16,96,128]{2,1,0:T(8,128)}), f32[16,96,128]{2,1,0:T(8,128)S(1)}, u32[]{:S(2)}, u32[]{:S(2)}) async-start(f32[16,96,128]{2,1,0:T(8,128)} %planes.1), calls=%async_computation.1 | async-start | bytes 1572864 | tf_op jit(solution)/shard_map/all_to_all | solution.py:514
  33.7 9.5 %copy-start.1 = (f32[64,256]{1,0:T(8,128)S(1)}, f32[64,256]{1,0:T(8,128)}, u32[]{:S(2)}) copy-start(f32[64,256]{1,0:T(8,128)} %constant.19.clone.interp_ref) | copy-start | bytes 196612
  33.7 9.5 %copy-start.4 = (s32[32]{0:T(128)S(1)}, s32[32]{0:T(128)}, u32[]{:S(2)}) copy-start(s32[32]{0:T(128)} %offset_ref.1) | copy-start | bytes 388
  33.7 6.1 %collective-permute-start.4 = (f32[512,128]{1,0:T(8,128)S(1)}, f32[512,128]{1,0:T(8,128)S(1)}, u32[]{:S(2)}, u32[]{:S(2)}) collective-permute-start(f32[512,128]{1,0:T(8,128)S(1)} %collective-permute-done.1.refs_1_), channel_id=1, source_target_pairs={{0,32},{16,240},{32,64},{48,16},{64,96},{80,48},{96,128},{112,80},... | collective-permute-start | bytes 786440 | tf_op jit(solution)/shard_map/ppermute | solution.py:515
  36.5 9.1 %copy-start.5 = (s32[32]{0:T(128)S(1)}, s32[32]{0:T(128)}, u32[]{:S(2)}) copy-start(s32[32]{0:T(128)} %source_ref.1) | copy-start | bytes 388
  36.5 7.3 %collective-permute-start.3 = (f32[256,128]{1,0:T(8,128)S(1)}, f32[256,128]{1,0:T(8,128)S(1)}, u32[]{:S(2)}, u32[]{:S(2)}) collective-permute-start(f32[256,128]{1,0:T(8,128)S(1)} %slice.3), channel_id=1, source_target_pairs={{0,32},{16,240},{32,64},{48,16},{64,96},{80,48},{96,128},{112,80},... | collective-permute-start | bytes 393224 | tf_op jit(solution)/shard_map/ppermute | solution.py:516
  37.3 8.3 %collective-permute-start.5 = (f32[512,128]{1,0:T(8,128)S(1)}, f32[512,128]{1,0:T(8,128)S(1)}, u32[]{:S(2)}, u32[]{:S(2)}) collective-permute-start(f32[512,128]{1,0:T(8,128)S(1)} %collective-permute-done.1.refs_1_), channel_id=1, source_target_pairs={{0,16},{16,0},{32,48},{48,32},{64,80},{80,64},{96,112},{112,96},{1... | collective-permute-start | bytes 786440 | tf_op jit(solution)/shard_map/ppermute | solution.py:519
  37.6 8.0 %collective-permute-start.7 = (f32[512,128]{1,0:T(8,128)S(1)}, f32[512,128]{1,0:T(8,128)S(1)}, u32[]{:S(2)}, u32[]{:S(2)}) collective-permute-start(f32[512,128]{1,0:T(8,128)S(1)} %collective-permute-done.2.refs_3_), channel_id=1, source_target_pairs={{0,16},{16,0},{32,48},{48,32},{64,80},{80,64},{96,112},{112,96},{1... | collective-permute-start | bytes 786440 | tf_op jit(solution)/shard_map/ppermute | solution.py:519
  39.8 5.8 %collective-permute-start.6 = (f32[512,128]{1,0:T(8,128)S(1)}, f32[512,128]{1,0:T(8,128)S(1)}, u32[]{:S(2)}, u32[]{:S(2)}) collective-permute-start(f32[512,128]{1,0:T(8,128)S(1)} %collective-permute-done.4.refs_2_), channel_id=1, source_target_pairs={{0,16},{16,0},{32,48},{48,32},{64,80},{80,64},{96,112},{112,96},{1... | collective-permute-start | bytes 786440 | tf_op jit(solution)/shard_map/ppermute | solution.py:519
  43.8 1.8 %collective-permute-start.8 = (f32[256,128]{1,0:T(8,128)S(1)}, f32[256,128]{1,0:T(8,128)S(1)}, u32[]{:S(2)}, u32[]{:S(2)}) collective-permute-start(f32[256,128]{1,0:T(8,128)S(1)} %collective-permute-done.3.refs_4_), channel_id=1, source_target_pairs={{0,16},{16,0},{32,48},{48,32},{64,80},{80,64},{96,112},{112,96},{1... | collective-permute-start | bytes 393224 | tf_op jit(solution)/shard_map/ppermute | solution.py:519

commit v5 on v4

--- a/solution.py
+++ b/solution.py
@@ -294,7 +294,6 @@
 def plane_kernel(metric_ref, got_ref, forward_ref, *refs):
     factors, (out_ref, table_ref, done_ref, sems) = refs[:4], refs[4:]
     make_tables(False, factors, table_ref)
-    make_tables(True, factors, table_ref)
     pair = lax.axis_index("four") * 2
     rx, ry, sx, sy = [
         lane_scalars(metric_ref[i, pair], metric_ref[i, pair + 1]) for i in range(4)
@@ -317,6 +316,7 @@
     odd_all = jnp.concatenate(odds + odds_z, 1)
     cos_part = dot(twice_high(table_ref[pl.ds(0, HALF), pl.ds(0, 2 * PAIRS)]), right_split(even_all))
     sin_part = dot(twice_high(table_ref[pl.ds(0, HALF), pl.ds(2 * PAIRS, 2 * PAIRS)]), right_split(odd_all))
+    make_tables(True, factors, table_ref)
     plus, minus = [], []
     for index in range(6):
         lanes = slice(index * LANES, (index + 1) * LANES)

time: 48.5 us -> 48.5 us (level)
  no operation moved by 1% of the time
where the time goes in v5:
time: 48.5 us; the launch traced here: 48.2 us
  starting transfers between devices  31 us (64%)
  Pallas kernels  13.6 us (28%)
  waiting for transfers between devices  3.22 us (7%)
    all_to_all x1, starting transfers between devices, local(): got = lax.all_to_all(packed, 'four', 0, 0, tiled=True)  7.72 us
    all_to_all x1, starting transfers between devices, local(): nonlinear = lax.all_to_all(advect_hat, 'four', 0, 0, tiled=True)  6.73 us
    ppermute x1, starting transfers between devices, local(): one = lax.ppermute(both, 'elem', moves(1))  5.66 us
    ppermute x4, starting transfers between devices, local(): lax.ppermute(piece, 'elem', ACROSS)  4.68 us
    pallas_call x1, Pallas kernels, planes(): pl.pallas_call(plane_kernel, in_specs=[pl.BlockSpec(memory_space=SMEM)] +...  4.14 us
    pallas_call x1, Pallas kernels, helmholtz(): pl.pallas_call(helm_kernel, grid=(GROUPS // step,), in_specs=[pl.BlockSpe...  3.26 us
    ppermute x1, starting transfers between devices, local(): two = lax.ppermute(one, 'elem', moves(1))  2.74 us
    ppermute x1, waiting for transfers between devices, local(): two = lax.ppermute(one, 'elem', moves(1))  1.98 us
  transfers between devices with their start and end apart: 11, of which 3 were waited for; matrix products, arithmetic and copies ran while one was open for 0% of the time, Pallas kernels for 22%

profile of v5, /device:TPU:1, one launch (start us, length us, event | category | flops | bytes accessed | tf_op | source)
XLA Modules:
  0.0 48.2 jit_solution(11028515786916252372)
XLA Ops:
  0.0 1.9 %pack.1.packed_ref = f32[16,96,128]{2,1,0:T(8,128)} custom-call(f32[96,2048]{1,0:T(8,128)} %bitcast.4), custom_call_target="tpu_custom_call" | custom-call | bytes 1600000 | tf_op jit(solution)/shard_map/pack/pallas_call | solution.py:133
  1.9 7.7 %all-to-all-start = ((f32[16,96,128]{2,1,0:T(8,128)}), f32[16,96,128]{2,1,0:T(8,128)S(1)}, u32[]{:S(2)}, u32[]{:S(2)}) async-start(f32[16,96,128]{2,1,0:T(8,128)} %pack.1.packed_ref), calls=%async_computation | async-start | bytes 1572864 | tf_op jit(solution)/shard_map/all_to_all | solution.py:502
  9.6 0.0 copy-done
  9.6 0.0 copy-done.2
  9.6 0.0 copy-start.6
  9.7 0.0 copy-start.7
  9.7 0.0 copy-start.9
  9.7 0.0 copy-start.10
  9.7 1.1 %traces.1.mine_ref = f32[256,128]{1,0:T(8,128)S(1)} custom-call(s32[32]{0:T(128)S(1)} %copy-done.2, f32[16,96,128]{2,1,0:T(8,128)S(1)} %copy-done), custom_call_target="tpu_custom_call" | custom-call | bytes 8000000 | tf_op jit(solution)/shard_map/traces/pallas_call | solution.py:163
  10.8 0.0 copy-start.3
  10.8 0.0 copy-start.8
  10.8 0.0 copy-start.15
  10.9 1.0 %collective-permute-start = (f32[256,128]{1,0:T(8,128)S(1)}, f32[256,128]{1,0:T(8,128)S(1)}, u32[]{:S(2)}, u32[]{:S(2)}) collective-permute-start(f32[256,128]{1,0:T(8,128)S(1)} %traces.1.mine_ref), channel_id=1, source_target_pairs={{0,16},{16,0},{32,48},{48,32},{64,80},{80,64},{96,112},{112,96},{1... | collective-permute-start | bytes 393224 | tf_op jit(solution)/shard_map/ppermute | solution.py:504
  11.9 0.0 copy-done.7
  11.9 3.3 %helm.1.helm_ref = f32[16,96,128]{2,1,0:T(8,128)S(1)} custom-call(f32[4,32]{1,0:T(4,128)S(1)} %copy-done.7, f32[32]{0:T(128)S(1)} %copy-done.8, s32[32]{0:T(128)S(1)} %copy-done.3, f32[16,96,128]{2,1,0:T(8,128)S(1)} %copy-done, f32[16,128]{1,0:T(8,128)S(1)} %bitcast.3, f32[1,128]{1,0:T(1,128)S(1)} %copy-done.15, bf16[384,256]{1,0:T(8,128)(2,1)S(1)} %copy-done.9, ...), custom_call_target="tpu_custom_call" | custom-call | flops 2000000000 | bytes 8000000 | tf_op jit(solution)/shard_map/helm/pallas_call | solution.py:253
  15.2 0.0 copy-start.11
  15.2 0.0 copy-start.12
  15.2 0.0 copy-start.13
  15.2 0.0 copy-start.14
  15.3 0.0 collective-permute-done.other_ref
  15.3 5.7 %collective-permute-start.1 = (f32[512,128]{1,0:T(8,128)S(1)}, f32[512,128]{1,0:T(8,128)S(1)}, u32[]{:S(2)}, u32[]{:S(2)}) collective-permute-start(f32[512,128]{1,0:T(8,128)S(1)} %pair.1.refs_0_), channel_id=1, source_target_pairs={{0,32},{16,240},{32,64},{48,16},{64,96},{80,48},{96,128},{112,80},... | collective-permute-start | bytes 786440 | tf_op jit(solution)/shard_map/ppermute | solution.py:505
  21.0 1.6 %collective-permute-start.2 = (f32[512,128]{1,0:T(8,128)S(1)}, f32[512,128]{1,0:T(8,128)S(1)}, u32[]{:S(2)}, u32[]{:S(2)}) collective-permute-start(f32[512,128]{1,0:T(8,128)S(1)} %pair.1.refs_0_), channel_id=1, source_target_pairs={{0,96},{16,176},{32,128},{48,208},{64,160},{80,240},{96,192},{112,... | collective-permute-start | bytes 786440 | tf_op jit(solution)/shard_map/ppermute | solution.py:506
  22.6 0.2 all-to-all-done.got_ref
  22.8 0.0 copy-done.14
  22.8 4.1 %planes.1 = f32[16,96,128]{2,1,0:T(8,128)} custom-call(f32[4,32]{1,0:T(4,128)S(1)} %copy-done.7, f32[16,96,128]{2,1,0:T(8,128)S(1)} %all-to-all-done.got_ref, bf16[384,256]{1,0:T(8,128)(2,1)S(1)} %copy-done.9, f32[24,384]{1,0:T(8,128)S(1)} %copy-done.11, f32[24,384]{1,0:T(8,128)S(1)} %copy-done.12, f32[16,384]{1,0:T(8,128)S(1)} %copy-done.13, ...), custom_call_target="tpu_custom_call" | custom-call | flops 3000000000 | bytes 4000000 | tf_op jit(solution)/shard_map/planes/pallas_call | solution.py:377
  27.0 6.7 %all-to-all-start.1 = ((f32[16,96,128]{2,1,0:T(8,128)}), f32[16,96,128]{2,1,0:T(8,128)S(1)}, u32[]{:S(2)}, u32[]{:S(2)}) async-start(f32[16,96,128]{2,1,0:T(8,128)} %planes.1), calls=%async_computation.1 | async-start | bytes 1572864 | tf_op jit(solution)/shard_map/all_to_all | solution.py:514
  33.7 0.0 copy-start.1
  33.7 0.0 copy-start.4
  33.7 0.0 collective-permute-done.1.refs_1_
  33.7 0.0 collective-permute-done.2.refs_3_
  33.8 2.7 %collective-permute-start.4 = (f32[512,128]{1,0:T(8,128)S(1)}, f32[512,128]{1,0:T(8,128)S(1)}, u32[]{:S(2)}, u32[]{:S(2)}) collective-permute-start(f32[512,128]{1,0:T(8,128)S(1)} %collective-permute-done.1.refs_1_), channel_id=1, source_target_pairs={{0,32},{16,240},{32,64},{48,16},{64,96},{80,48},{96,128},{112,80},... | collective-permute-start | bytes 786440 | tf_op jit(solution)/shard_map/ppermute | solution.py:515
  36.5 0.0 copy-start.5
  36.5 0.8 %collective-permute-start.3 = (f32[256,128]{1,0:T(8,128)S(1)}, f32[256,128]{1,0:T(8,128)S(1)}, u32[]{:S(2)}, u32[]{:S(2)}) collective-permute-start(f32[256,128]{1,0:T(8,128)S(1)} %slice.3), channel_id=1, source_target_pairs={{0,32},{16,240},{32,64},{48,16},{64,96},{80,48},{96,128},{112,80},... | collective-permute-start | bytes 393224 | tf_op jit(solution)/shard_map/ppermute | solution.py:516
  37.3 0.3 collective-permute-start.5
  37.6 0.2 collective-permute-start.7
  37.8 2.0 %collective-permute-done.4.refs_2_ = f32[512,128]{1,0:T(8,128)S(1)} collective-permute-done((f32[512,128]{1,0:T(8,128)S(1)}, f32[512,128]{1,0:T(8,128)S(1)}, u32[]{:S(2)}, u32[]{:S(2)}) %collective-permute-start.4) | collective-permute-done | bytes 262176 | tf_op jit(solution)/shard_map/ppermute | solution.py:515
  39.8 3.4 %collective-permute-start.6 = (f32[512,128]{1,0:T(8,128)S(1)}, f32[512,128]{1,0:T(8,128)S(1)}, u32[]{:S(2)}, u32[]{:S(2)}) collective-permute-start(f32[512,128]{1,0:T(8,128)S(1)} %collective-permute-done.4.refs_2_), channel_id=1, source_target_pairs={{0,16},{16,0},{32,48},{48,32},{64,80},{80,64},{96,112},{112,96},{1... | collective-permute-start | bytes 786440 | tf_op jit(solution)/shard_map/ppermute | solution.py:519
  43.2 0.6 %placing.1.place_ref = bf16[768,256]{1,0:T(8,128)(2,1)S(1)} custom-call(s32[32]{0:T(128)S(1)} %copy-done.3, s32[32]{0:T(128)S(1)} %copy-done.4, f32[64,256]{1,0:T(8,128)S(1)} %copy-done.1), custom_call_target="tpu_custom_call" | custom-call | flops 1000 | bytes 1000 | tf_op jit(solution)/shard_map/placing/pallas_call | solution.py:406
  43.8 0.0 collective-permute-done.3.refs_4_
  43.8 0.8 %collective-permute-start.8 = (f32[256,128]{1,0:T(8,128)S(1)}, f32[256,128]{1,0:T(8,128)S(1)}, u32[]{:S(2)}, u32[]{:S(2)}) collective-permute-start(f32[256,128]{1,0:T(8,128)S(1)} %collective-permute-done.3.refs_4_), channel_id=1, source_target_pairs={{0,16},{16,0},{32,48},{48,32},{64,80},{80,64},{96,112},{112,96},{1... | collective-permute-start | bytes 393224 | tf_op jit(solution)/shard_map/ppermute | solution.py:519
  44.6 1.0 %collective-permute-done.8.refs_8_ = f32[256,128]{1,0:T(8,128)S(1)} collective-permute-done((f32[256,128]{1,0:T(8,128)S(1)}, f32[256,128]{1,0:T(8,128)S(1)}, u32[]{:S(2)}, u32[]{:S(2)}) %collective-permute-start.8) | collective-permute-done | bytes 131104 | tf_op jit(solution)/shard_map/ppermute | solution.py:519
  45.6 0.0 collective-permute-done.5.refs_5_
  45.6 0.0 collective-permute-done.7.refs_7_
  45.6 0.0 collective-permute-done.6.refs_6_
  45.6 0.0 copy-done.5
  45.6 1.3 %penalty.1.placed_ref = f32[96,256]{1,0:T(8,128)S(1)} custom-call(s32[32]{0:T(128)S(1)} %copy-done.5, bf16[768,256]{1,0:T(8,128)(2,1)S(1)} %placing.1.place_ref, f32[512,128]{1,0:T(8,128)S(1)} %pair.1.refs_0_, f32[512,128]{1,0:T(8,128)S(1)} %collective-permute-done.1.refs_1_, f32[512,128]{1,0:T(8,128)S(1)} %collective-permute-done.4.refs_2_, ...), custom_call_target="tpu_custom_call" | custom-call | flops 1000 | bytes 1000 | tf_op jit(solution)/shard_map/penalty/pallas_call | solution.py:444
  47.0 0.0 all-to-all-done.1.nonlinear_ref
  47.0 1.2 %final_sum.1 = f32[96,2048]{1,0:T(8,128)} custom-call(f32[16,96,128]{2,1,0:T(8,128)S(1)} %all-to-all-done.1.nonlinear_ref, f32[16,96,128]{2,1,0:T(8,128)S(1)} %helm.1.helm_ref, f32[96,256]{1,0:T(8,128)S(1)} %penalty.1.placed_ref), custom_call_target="tpu_custom_call" | custom-call | bytes 2400000 | tf_op jit(solution)/shard_map/final_sum/pallas_call | solution.py:478
  (15 shorter events, 0.1 us)
Async XLA Ops:
  1.9 7.7 %copy-start = (f32[16,96,128]{2,1,0:T(8,128)S(1)}, f32[16,96,128]{2,1,0:T(8,128)}, u32[]{:S(2)}) copy-start(f32[16,96,128]{2,1,0:T(8,128)} %pack.1.packed_ref) | copy-start | bytes 2359300
  1.9 7.7 %copy-start.2 = (s32[32]{0:T(128)S(1)}, s32[32]{0:T(128)}, u32[]{:S(2)}) copy-start(s32[32]{0:T(128)} %rotor_ref.1) | copy-start | bytes 388
  1.9 20.9 %all-to-all-start = ((f32[16,96,128]{2,1,0:T(8,128)}), f32[16,96,128]{2,1,0:T(8,128)S(1)}, u32[]{:S(2)}, u32[]{:S(2)}) async-start(f32[16,96,128]{2,1,0:T(8,128)} %pack.1.packed_ref), calls=%async_computation | async-start | bytes 1572864 | tf_op jit(solution)/shard_map/all_to_all | solution.py:502
  9.6 2.3 %copy-start.6 = (f32[2048]{0:T(1024)S(1)}, f32[2048]{0:T(1024)}, u32[]{:S(2)}) copy-start(f32[2048]{0:T(1024)} %param.19) | copy-start | bytes 24580
  9.7 2.2 %copy-start.7 = (f32[4,32]{1,0:T(4,128)S(1)}, f32[4,32]{1,0:T(4,128)}, u32[]{:S(2)}) copy-start(f32[4,32]{1,0:T(4,128)} %metric_ref.3) | copy-start | bytes 1540
  9.7 2.2 %copy-start.9 = (bf16[384,256]{1,0:T(8,128)(2,1)S(1)}, bf16[384,256]{1,0:T(8,128)(2,1)}, u32[]{:S(2)}) copy-start(bf16[384,256]{1,0:T(8,128)(2,1)} %constant.16.clone.forward_ref) | copy-start | bytes 589828
  9.7 2.2 %copy-start.10 = (bf16[768,128]{1,0:T(8,128)(2,1)S(1)}, bf16[768,128]{1,0:T(8,128)(2,1)}, u32[]{:S(2)}) copy-start(bf16[768,128]{1,0:T(8,128)(2,1)} %constant.17.clone.back_ref) | copy-start | bytes 589828
  10.8 1.1 %copy-start.3 = (s32[32]{0:T(128)S(1)}, s32[32]{0:T(128)}, u32[]{:S(2)}) copy-start(s32[32]{0:T(128)} %stator_ref.3) | copy-start | bytes 388
  10.8 1.1 %copy-start.8 = (f32[32]{0:T(128)S(1)}, f32[32]{0:T(128)}, u32[]{:S(2)}) copy-start(f32[32]{0:T(128)} %area_ref.1) | copy-start | bytes 388
  10.8 1.1 %copy-start.15 = (f32[1,128]{1,0:T(1,128)S(1)}, f32[1,128]{1,0:T(1,128)}, u32[]{:S(2)}) copy-start(f32[1,128]{1,0:T(1,128)} %constant.18.clone.weight_ref) | copy-start | bytes 1540
  10.9 4.4 %collective-permute-start = (f32[256,128]{1,0:T(8,128)S(1)}, f32[256,128]{1,0:T(8,128)S(1)}, u32[]{:S(2)}, u32[]{:S(2)}) collective-permute-start(f32[256,128]{1,0:T(8,128)S(1)} %traces.1.mine_ref), channel_id=1, source_target_pairs={{0,16},{16,0},{32,48},{48,32},{64,80},{80,64},{96,112},{112,96},{1... | collective-permute-start | bytes 393224 | tf_op jit(solution)/shard_map/ppermute | solution.py:504
  15.2 7.6 %copy-start.11 = (f32[24,384]{1,0:T(8,128)S(1)}, f32[24,384]{1,0:T(8,128)}, u32[]{:S(2)}) copy-start(f32[24,384]{1,0:T(8,128)} %constant.20.clone.refs_0_) | copy-start | bytes 110596
  15.2 7.6 %copy-start.12 = (f32[24,384]{1,0:T(8,128)S(1)}, f32[24,384]{1,0:T(8,128)}, u32[]{:S(2)}) copy-start(f32[24,384]{1,0:T(8,128)} %constant.21.clone.refs_1_) | copy-start | bytes 110596
  15.2 7.6 %copy-start.13 = (f32[16,384]{1,0:T(8,128)S(1)}, f32[16,384]{1,0:T(8,128)}, u32[]{:S(2)}) copy-start(f32[16,384]{1,0:T(8,128)} %constant.22.clone.refs_2_) | copy-start | bytes 73732
  15.2 7.6 %copy-start.14 = (f32[16,384]{1,0:T(8,128)S(1)}, f32[16,384]{1,0:T(8,128)}, u32[]{:S(2)}) copy-start(f32[16,384]{1,0:T(8,128)} %constant.23.clone.refs_3_) | copy-start | bytes 73732
  15.3 18.4 %collective-permute-start.1 = (f32[512,128]{1,0:T(8,128)S(1)}, f32[512,128]{1,0:T(8,128)S(1)}, u32[]{:S(2)}, u32[]{:S(2)}) collective-permute-start(f32[512,128]{1,0:T(8,128)S(1)} %pair.1.refs_0_), channel_id=1, source_target_pairs={{0,32},{16,240},{32,64},{48,16},{64,96},{80,48},{96,128},{112,80},... | collective-permute-start | bytes 786440 | tf_op jit(solution)/shard_map/ppermute | solution.py:505
  21.0 12.8 %collective-permute-start.2 = (f32[512,128]{1,0:T(8,128)S(1)}, f32[512,128]{1,0:T(8,128)S(1)}, u32[]{:S(2)}, u32[]{:S(2)}) collective-permute-start(f32[512,128]{1,0:T(8,128)S(1)} %pair.1.refs_0_), channel_id=1, source_target_pairs={{0,96},{16,176},{32,128},{48,208},{64,160},{80,240},{96,192},{112,... | collective-permute-start | bytes 786440 | tf_op jit(solution)/shard_map/ppermute | solution.py:506
  27.0 20.0 %all-to-all-start.1 = ((f32[16,96,128]{2,1,0:T(8,128)}), f32[16,96,128]{2,1,0:T(8,128)S(1)}, u32[]{:S(2)}, u32[]{:S(2)}) async-start(f32[16,96,128]{2,1,0:T(8,128)} %planes.1), calls=%async_computation.1 | async-start | bytes 1572864 | tf_op jit(solution)/shard_map/all_to_all | solution.py:514
  33.7 9.5 %copy-start.1 = (f32[64,256]{1,0:T(8,128)S(1)}, f32[64,256]{1,0:T(8,128)}, u32[]{:S(2)}) copy-start(f32[64,256]{1,0:T(8,128)} %constant.19.clone.interp_ref) | copy-start | bytes 196612
  33.7 9.5 %copy-start.4 = (s32[32]{0:T(128)S(1)}, s32[32]{0:T(128)}, u32[]{:S(2)}) copy-start(s32[32]{0:T(128)} %offset_ref.1) | copy-start | bytes 388
  33.8 6.1 %collective-permute-start.4 = (f32[512,128]{1,0:T(8,128)S(1)}, f32[512,128]{1,0:T(8,128)S(1)}, u32[]{:S(2)}, u32[]{:S(2)}) collective-permute-start(f32[512,128]{1,0:T(8,128)S(1)} %collective-permute-done.1.refs_1_), channel_id=1, source_target_pairs={{0,32},{16,240},{32,64},{48,16},{64,96},{80,48},{96,128},{112,80},... | collective-permute-start | bytes 786440 | tf_op jit(solution)/shard_map/ppermute | solution.py:515
  36.5 9.1 %copy-start.5 = (s32[32]{0:T(128)S(1)}, s32[32]{0:T(128)}, u32[]{:S(2)}) copy-start(s32[32]{0:T(128)} %source_ref.1) | copy-start | bytes 388
  36.5 7.3 %collective-permute-start.3 = (f32[256,128]{1,0:T(8,128)S(1)}, f32[256,128]{1,0:T(8,128)S(1)}, u32[]{:S(2)}, u32[]{:S(2)}) collective-permute-start(f32[256,128]{1,0:T(8,128)S(1)} %slice.3), channel_id=1, source_target_pairs={{0,32},{16,240},{32,64},{48,16},{64,96},{80,48},{96,128},{112,80},... | collective-permute-start | bytes 393224 | tf_op jit(solution)/shard_map/ppermute | solution.py:516
  37.3 8.3 %collective-permute-start.5 = (f32[512,128]{1,0:T(8,128)S(1)}, f32[512,128]{1,0:T(8,128)S(1)}, u32[]{:S(2)}, u32[]{:S(2)}) collective-permute-start(f32[512,128]{1,0:T(8,128)S(1)} %collective-permute-done.1.refs_1_), channel_id=1, source_target_pairs={{0,16},{16,0},{32,48},{48,32},{64,80},{80,64},{96,112},{112,96},{1... | collective-permute-start | bytes 786440 | tf_op jit(solution)/shard_map/ppermute | solution.py:519
  37.6 8.0 %collective-permute-start.7 = (f32[512,128]{1,0:T(8,128)S(1)}, f32[512,128]{1,0:T(8,128)S(1)}, u32[]{:S(2)}, u32[]{:S(2)}) collective-permute-start(f32[512,128]{1,0:T(8,128)S(1)} %collective-permute-done.2.refs_3_), channel_id=1, source_target_pairs={{0,16},{16,0},{32,48},{48,32},{64,80},{80,64},{96,112},{112,96},{1... | collective-permute-start | bytes 786440 | tf_op jit(solution)/shard_map/ppermute | solution.py:519
  39.8 5.8 %collective-permute-start.6 = (f32[512,128]{1,0:T(8,128)S(1)}, f32[512,128]{1,0:T(8,128)S(1)}, u32[]{:S(2)}, u32[]{:S(2)}) collective-permute-start(f32[512,128]{1,0:T(8,128)S(1)} %collective-permute-done.4.refs_2_), channel_id=1, source_target_pairs={{0,16},{16,0},{32,48},{48,32},{64,80},{80,64},{96,112},{112,96},{1... | collective-permute-start | bytes 786440 | tf_op jit(solution)/shard_map/ppermute | solution.py:519
  43.8 1.8 %collective-permute-start.8 = (f32[256,128]{1,0:T(8,128)S(1)}, f32[256,128]{1,0:T(8,128)S(1)}, u32[]{:S(2)}, u32[]{:S(2)}) collective-permute-start(f32[256,128]{1,0:T(8,128)S(1)} %collective-permute-done.3.refs_4_), channel_id=1, source_target_pairs={{0,16},{16,0},{32,48},{48,32},{64,80},{80,64},{96,112},{112,96},{1... | collective-permute-start | bytes 393224 | tf_op jit(solution)/shard_map/ppermute | solution.py:519
